TPU v7x, 32 devices: a whole 2x2x4 slice. The times are simulated.
32 devices in a mesh: dp: 2 (over x), fsdp: 16 (over z, y, core).
Axes of the slice: x: 2, y: 2, z: 4, core: 2. Of those that a mesh axis runs over, the one named last changes fastest.
Arguments:
- tokens: bfloat16 [16384, 1024], P(('dp', 'fsdp')), may hold values from -6 to 6
- cotangent: bfloat16 [16384, 1024], P(('dp', 'fsdp')), may hold values from -6 to 6
- group_ids: int32 [8], replicated, may hold values from 0 to 7
- loss_weights: int32 [8], replicated, may hold values from 1 to 4
- gain_one: bfloat16 [1024], P(('dp', 'fsdp')), may hold values from 0.5 to 1.5
- w_query: bfloat16 [1024, 1024], P(('dp', 'fsdp')), may hold values from -0.1875 to 0.1875
- w_key: bfloat16 [1024, 512], P(('dp', 'fsdp')), may hold values from -0.1875 to 0.1875
- w_value: bfloat16 [1024, 512], P(('dp', 'fsdp')), may hold values from -0.1875 to 0.1875
- w_gate: bfloat16 [1024, 16], P(('dp', 'fsdp')), may hold values from -0.1875 to 0.1875
- gate_bias: float32 [16], replicated, may hold values from -12 to 0, as said below
- w_out: bfloat16 [1024, 1024], P(('dp', 'fsdp')), may hold values from -0.1875 to 0.1875
- gain_two: bfloat16 [1024], P(('dp', 'fsdp')), may hold values from 0.5 to 1.5
- w_gate_ff: bfloat16 [1024, 2816], P(('dp', 'fsdp')), may hold values from -0.1875 to 0.1875
- w_up: bfloat16 [1024, 2816], P(('dp', 'fsdp')), may hold values from -0.1875 to 0.1875
- w_down: bfloat16 [2816, 1024], P(None, ('dp', 'fsdp')), may hold values from -0.109375 to 0.109375
Outputs:
- output: bfloat16 [16384, 1024], P(('dp', 'fsdp'))
- grad_input: bfloat16 [16384, 1024], P(('dp', 'fsdp'))
- grad_gain_one: float32 [1024], P(('dp', 'fsdp'))
- grad_w_query: float32 [1024, 1024], P(('dp', 'fsdp'))
- grad_w_key: float32 [1024, 512], P(('dp', 'fsdp'))
- grad_w_value: float32 [1024, 512], P(('dp', 'fsdp'))
- grad_w_gate: float32 [1024, 16], P(('dp', 'fsdp'))
- grad_gate_bias: float32 [16], replicated
- grad_w_out: float32 [1024, 1024], P(('dp', 'fsdp'))
- grad_gain_two: float32 [1024], P(('dp', 'fsdp'))
- grad_w_gate_ff: float32 [1024, 2816], P(('dp', 'fsdp'))
- grad_w_up: float32 [1024, 2816], P(('dp', 'fsdp'))
- grad_w_down: float32 [2816, 1024], P(None, ('dp', 'fsdp'))
Inputs may be any that keep to these rules, and one draw needn't show every extreme that they name: `gate_bias`: per-head offset of the decay gate's input.
All inputs are finite; a program needn't handle non-finite values.
Results may differ from a plain program's by a relative error of at most 0.035.
Values may be sent and summed in bfloat16 or wider, within the bound.
No kernel may reach another device: no remote copies, remote signals or barrier semaphores. Data moves between devices by JAX's collectives and lax.ppermute only.
A program may use at most 384 MiB of HBM per device.

v0:
```python
import jax
import jax.numpy as jnp
from jax import lax
from jax.sharding import PartitionSpec as P

HEADS = 16
HEAD = 64
KVH = 2
LATENT = 256
SPAN = 4


epsilon = 1e-05
head_floor = 0.25
ROPE_BASE = 10000.0
GATE_TEMP = 16.0
HIGHEST = lax.Precision.HIGHEST


def carried_in(shard, axis, combine, identity, reverse):
    devices, index = (lax.axis_size(axis), lax.axis_index(axis))
    everything = jax.tree.map(
        lambda part, kind: lax.all_gather(part.astype(kind), axis),
        shard,
        jax.tree.map(lambda a: jnp.bfloat16 if a.dtype == jnp.float32 else a.dtype, shard),
    )
    start = jax.tree.map(
        lambda part, zero: jnp.broadcast_to(jnp.asarray(zero, part.dtype), part.shape),
        shard,
        identity,
    )

    def step(k, before):
        at = devices - 1 - k if reverse else k
        reached = at > index if reverse else at < index
        new = combine(
            before, jax.tree.map(lambda part, own: part[at].astype(own.dtype), everything, shard)
        )
        return jax.tree.map(lambda a, b: jnp.where(reached, a, b), new, before)

    return lax.fori_loop(0, devices, step, start)


def inverse_rms(values, added=epsilon):
    return lax.rsqrt(jnp.mean(values * values, axis=-1, keepdims=True) + added)


def norm_back(grad_unit, unit_rows, scale_rows):
    return scale_rows * (
        grad_unit - unit_rows * jnp.mean(grad_unit * unit_rows, axis=-1, keepdims=True)
    )


def rotate(values, positions):
    half_width = values.shape[-1] // 2
    frequency = ROPE_BASE ** (-jnp.arange(half_width, dtype=jnp.float32) / half_width)
    angles = positions.astype(jnp.float32)[:, None] * frequency[None, :]
    cosine = jnp.cos(angles)[:, None, :]
    sine_part = jnp.sin(angles)[:, None, :]
    leading = values[..., :half_width]
    trailing = values[..., half_width:]
    return jnp.concatenate(
        [leading * cosine - trailing * sine_part, trailing * cosine + leading * sine_part], axis=-1
    )


def rotate_back(values, positions):
    half_width = values.shape[-1] // 2
    frequency = ROPE_BASE ** (-jnp.arange(half_width, dtype=jnp.float32) / half_width)
    angles = positions.astype(jnp.float32)[:, None] * frequency[None, :]
    cosine = jnp.cos(angles)[:, None, :]
    sine_part = jnp.sin(angles)[:, None, :]
    leading = values[..., :half_width]
    trailing = values[..., half_width:]
    return jnp.concatenate(
        [leading * cosine + trailing * sine_part, trailing * cosine - leading * sine_part], axis=-1
    )


def broaden(latent):
    rows_count = latent.shape[0]
    width = latent.shape[2]
    per_group = latent.shape[1] // KVH
    repeats = HEADS // latent.shape[1]
    shaped = latent.reshape(rows_count, KVH, 1, per_group, width)
    return jnp.broadcast_to(shaped, (rows_count, KVH, repeats, per_group, width)).reshape(
        rows_count, HEADS, width
    )


def narrow(gradient):
    rows_count = gradient.shape[0]
    width = gradient.shape[2]
    per_group = LATENT // HEAD
    repeats = HEADS // (KVH * per_group)
    return jnp.sum(gradient.reshape(rows_count, KVH, repeats, per_group, width), axis=2).reshape(
        rows_count, KVH * per_group, width
    )


def decay_table(cumulative):
    step_count = cumulative.shape[0]
    row_order = jnp.arange(step_count)
    causal = (row_order[:, None] >= row_order[None, :])[None, :, :]
    differences = cumulative.T[:, :, None] - cumulative.T[:, None, :]
    return jnp.where(causal, jnp.exp(jnp.where(causal, differences, 0.0)), 0.0)


def compose(earlier, later):
    return (earlier[0] * later[0], later[0][:, None, None] * earlier[1] + later[1])


def matmul(left, right):
    return jnp.dot(left, right, preferred_element_type=jnp.float32)


def contract_rows(left, right):
    return jnp.einsum("ta,tb->ab", left, right, preferred_element_type=jnp.float32)


def against(left, right):
    return jnp.einsum("tb,ab->ta", left, right, preferred_element_type=jnp.float32)


def sequence_weights(group_ids, loss_weights):
    group_count = loss_weights.shape[0]
    member = (group_ids[:, None] == jnp.arange(group_count, dtype=jnp.int32)[None, :]).astype(
        jnp.float32
    )
    counts = jnp.sum(member, axis=0)
    raw_weight = jnp.sum(member * loss_weights.astype(jnp.float32)[None, :], axis=1) / jnp.sum(
        member * counts[None, :], axis=1
    )
    return raw_weight * (group_ids.shape[0] / jnp.sum(raw_weight))


def front(tokens, params, gate_bias, positions):
    rows_count = tokens.shape[0]
    slot_count = KVH * (LATENT // HEAD)
    inputs = tokens.astype(jnp.float32)
    scale_one = inverse_rms(inputs)
    unit_one = inputs * scale_one
    normed_one = (unit_one * params[0].astype(jnp.float32)).astype(jnp.bfloat16)
    query_pre = matmul(normed_one, params[1])
    key_pre = matmul(normed_one, params[2])
    value_pre = matmul(normed_one, params[3])
    gate_pre = matmul(normed_one, params[4])
    queries = (
        rotate(query_pre.reshape(rows_count, HEADS, HEAD), positions) * float(HEAD) ** (-0.5)
    ).astype(jnp.bfloat16)
    key_heads = broaden(
        rotate(key_pre.reshape(rows_count, slot_count, HEAD), positions).astype(jnp.bfloat16)
    )
    value_heads = broaden(value_pre.astype(jnp.bfloat16).reshape(rows_count, slot_count, HEAD))
    log_decay = -jax.nn.softplus(gate_pre + gate_bias[None, :]) / GATE_TEMP
    cumulative = jnp.cumsum(log_decay, axis=0)
    decay_rows = decay_table(cumulative)
    scores = jnp.einsum("thd,shd->hts", queries, key_heads, preferred_element_type=jnp.float32)
    weighted = (scores * decay_rows).astype(jnp.bfloat16)
    local_part = jnp.einsum(
        "hts,she->the", weighted, value_heads, preferred_element_type=jnp.float32
    )
    last_cum = cumulative[-1]
    tail_decay = jnp.exp(last_cum[None, :] - cumulative)
    key_scaled = key_heads.astype(jnp.float32) * tail_decay[:, :, None]
    update = jnp.einsum(
        "shd,she->hde", key_scaled, value_heads.astype(jnp.float32), precision=HIGHEST
    )
    return dict(
        inputs=inputs,
        scale_one=scale_one,
        unit_one=unit_one,
        normed_one=normed_one,
        gate_pre=gate_pre,
        queries=queries,
        key_heads=key_heads,
        value_heads=value_heads,
        cumulative=cumulative,
        decay_rows=decay_rows,
        scores=scores,
        weighted=weighted,
        local_part=local_part,
        last_cum=last_cum,
        tail_decay=tail_decay,
        key_scaled=key_scaled,
        update=update,
    )


def finish(params, kept_values, state_in):
    rows_count = kept_values["inputs"].shape[0]
    queries_float = kept_values["queries"].astype(jnp.float32)
    growth = jnp.exp(kept_values["cumulative"])
    carried_part = growth[:, :, None] * jnp.einsum(
        "thd,hde->the", queries_float, state_in, precision=HIGHEST
    )
    mixed_out = kept_values["local_part"] + carried_part
    head_scale = inverse_rms(mixed_out, head_floor)
    head_normed = mixed_out * head_scale
    normed_flat = head_normed.astype(jnp.bfloat16).reshape(rows_count, HEADS * HEAD)
    attention = matmul(normed_flat, params[5])
    middle = kept_values["inputs"] + attention
    scale_two = inverse_rms(middle)
    unit_two = middle * scale_two
    normed_two = (unit_two * params[6].astype(jnp.float32)).astype(jnp.bfloat16)
    gate_ff = matmul(normed_two, params[7])
    up_ff = matmul(normed_two, params[8])
    hidden = (jax.nn.silu(gate_ff) * up_ff).astype(jnp.bfloat16)
    output = middle + matmul(hidden, params[9])
    return dict(
        queries_float=queries_float,
        growth=growth,
        carried_part=carried_part,
        head_scale=head_scale,
        head_normed=head_normed,
        normed_flat=normed_flat,
        scale_two=scale_two,
        unit_two=unit_two,
        normed_two=normed_two,
        gate_ff=gate_ff,
        up_ff=up_ff,
        hidden=hidden,
        output=output,
    )


def shards(
    tokens,
    cotangent,
    group_ids,
    loss_weights,
    gain_one,
    w_query,
    w_key,
    w_value,
    w_gate,
    gate_bias,
    w_out,
    gain_two,
    w_gate_ff,
    w_up,
    w_down,
):
    rows_count = tokens.shape[0]
    slot_count = KVH * (LATENT // HEAD)
    device_index = lax.axis_index(("dp", "fsdp"))
    block_index = device_index % SPAN
    positions = block_index * rows_count + jnp.arange(rows_count)
    params = (
        lax.all_gather(gain_one, ("dp", "fsdp"), axis=0, tiled=True),
        lax.all_gather(w_query, ("dp", "fsdp"), axis=0, tiled=True),
        lax.all_gather(w_key, ("dp", "fsdp"), axis=0, tiled=True),
        lax.all_gather(w_value, ("dp", "fsdp"), axis=0, tiled=True),
        lax.all_gather(w_gate, ("dp", "fsdp"), axis=0, tiled=True),
        lax.all_gather(w_out, ("dp", "fsdp"), axis=0, tiled=True),
        lax.all_gather(gain_two, ("dp", "fsdp"), axis=0, tiled=True),
        lax.all_gather(w_gate_ff, ("dp", "fsdp"), axis=0, tiled=True),
        lax.all_gather(w_up, ("dp", "fsdp"), axis=0, tiled=True),
        lax.all_gather(w_down, ("dp", "fsdp"), axis=1, tiled=True),
    )
    kept_values = front(tokens, params, gate_bias, positions)
    identity = (jnp.ones((HEADS,), jnp.float32), jnp.zeros((HEADS, HEAD, HEAD), jnp.float32))
    keep_next = (block_index != SPAN - 1).astype(jnp.float32)
    total_decay = jnp.exp(kept_values["last_cum"])
    state_in = carried_in(
        (keep_next * total_decay, keep_next * kept_values["update"]),
        ("dp", "fsdp"),
        compose,
        identity,
        False,
    )[1]
    finished = finish(params, kept_values, state_in)
    output = finished["output"].astype(jnp.bfloat16)
    seq_weights = sequence_weights(group_ids, loss_weights)
    own_weight = jnp.sum(
        jnp.where(jnp.arange(group_ids.shape[0]) == device_index // SPAN, seq_weights, 0.0)
    )
    grad_out = cotangent.astype(jnp.float32) * own_weight
    grad_branch = grad_out.astype(jnp.bfloat16)
    d_down = contract_rows(finished["hidden"], grad_branch)
    grad_hidden = against(grad_branch, params[9])
    gate_ff = finished["gate_ff"]
    sigmoid_gate = jax.nn.sigmoid(gate_ff)
    grad_gate = (
        grad_hidden * finished["up_ff"] * (sigmoid_gate * (1.0 + gate_ff * (1.0 - sigmoid_gate)))
    ).astype(jnp.bfloat16)
    grad_up = (grad_hidden * jax.nn.silu(gate_ff)).astype(jnp.bfloat16)
    d_gate_ff = contract_rows(finished["normed_two"], grad_gate)
    d_up = contract_rows(finished["normed_two"], grad_up)
    grad_normed_two = against(grad_gate, params[7]) + against(grad_up, params[8])
    d_gain_two = jnp.sum(grad_normed_two * finished["unit_two"], axis=0)
    grad_middle = grad_out + norm_back(
        grad_normed_two * params[6].astype(jnp.float32), finished["unit_two"], finished["scale_two"]
    )
    grad_attention = grad_middle.astype(jnp.bfloat16)
    d_out = contract_rows(finished["normed_flat"], grad_attention)
    grad_normed = against(grad_attention, params[5]).reshape(rows_count, HEADS, HEAD)
    grad_mixed = norm_back(grad_normed, finished["head_normed"], finished["head_scale"]).astype(
        jnp.bfloat16
    )
    grad_mixed_f = grad_mixed.astype(jnp.float32)
    growth = finished["growth"]
    queries_float = finished["queries_float"]
    through = jnp.einsum(
        "thd,the->hde", queries_float * growth[:, :, None], grad_mixed_f, precision=HIGHEST
    )
    keep_start = (block_index != 0).astype(jnp.float32)
    later_state = carried_in(
        (keep_start * total_decay, keep_start * through), ("dp", "fsdp"), compose, identity, True
    )[1]
    queries = kept_values["queries"]
    key_heads = kept_values["key_heads"]
    value_heads = kept_values["value_heads"]
    decay_rows = kept_values["decay_rows"]
    tail_decay = kept_values["tail_decay"]
    grad_weighted = jnp.einsum(
        "the,she->hts", grad_mixed, value_heads, preferred_element_type=jnp.float32
    )
    d_values = jnp.einsum(
        "hts,the->she", kept_values["weighted"], grad_mixed, preferred_element_type=jnp.float32
    )
    grad_scores = (grad_weighted * decay_rows).astype(jnp.bfloat16)
    d_queries = jnp.einsum(
        "hts,shd->thd", grad_scores, key_heads, preferred_element_type=jnp.float32
    )
    d_keys = jnp.einsum("hts,thd->shd", grad_scores, queries, preferred_element_type=jnp.float32)
    spread = grad_weighted * kept_values["scores"] * decay_rows
    grad_cum = jnp.sum(spread, axis=2).T - jnp.sum(spread, axis=1).T
    d_queries = d_queries + growth[:, :, None] * jnp.einsum(
        "the,hde->thd", grad_mixed_f, state_in, precision=HIGHEST
    )
    grad_cum = grad_cum + jnp.sum(grad_mixed_f * finished["carried_part"], axis=2)
    grad_total = jnp.sum(later_state * state_in, axis=(1, 2))
    key_side = jnp.einsum(
        "she,hde->shd", value_heads.astype(jnp.float32), later_state, precision=HIGHEST
    )
    d_keys = d_keys + key_side * tail_decay[:, :, None]
    d_values = d_values + jnp.einsum(
        "shd,hde->she", kept_values["key_scaled"], later_state, precision=HIGHEST
    )
    grad_tail = jnp.sum(key_side * key_heads.astype(jnp.float32), axis=2) * tail_decay
    grad_cum = grad_cum - grad_tail
    last_row = (jnp.arange(rows_count) == rows_count - 1).astype(jnp.float32)[:, None]
    grad_cum = (
        grad_cum + last_row * (jnp.sum(grad_tail, axis=0) + grad_total * total_decay)[None, :]
    )
    grad_log = jnp.flip(jnp.cumsum(jnp.flip(grad_cum, 0), axis=0), 0)
    grad_gate_pre_f = (
        -grad_log * jax.nn.sigmoid(kept_values["gate_pre"] + gate_bias[None, :]) / GATE_TEMP
    )
    d_bias = jnp.sum(grad_gate_pre_f, axis=0)
    grad_gate_pre = grad_gate_pre_f.astype(jnp.bfloat16)
    grad_query_pre = (
        (rotate_back(d_queries, positions) * float(HEAD) ** (-0.5))
        .astype(jnp.bfloat16)
        .reshape(rows_count, HEADS * HEAD)
    )
    grad_key_pre = (
        rotate_back(narrow(d_keys), positions)
        .astype(jnp.bfloat16)
        .reshape(rows_count, slot_count * HEAD)
    )
    grad_value_pre = narrow(d_values).astype(jnp.bfloat16).reshape(rows_count, slot_count * HEAD)
    normed_one = kept_values["normed_one"]
    d_query_w = contract_rows(normed_one, grad_query_pre)
    d_key_w = contract_rows(normed_one, grad_key_pre)
    d_value_w = contract_rows(normed_one, grad_value_pre)
    d_gate_w = contract_rows(normed_one, grad_gate_pre)
    grad_normed_one = (
        against(grad_query_pre, params[1])
        + against(grad_key_pre, params[2])
        + against(grad_value_pre, params[3])
        + against(grad_gate_pre, params[4])
    )
    d_gain_one = jnp.sum(grad_normed_one * kept_values["unit_one"], axis=0)
    grad_input = grad_middle + norm_back(
        grad_normed_one * params[0].astype(jnp.float32),
        kept_values["unit_one"],
        kept_values["scale_one"],
    )
    bias_rows = jnp.broadcast_to(d_bias[None, :], (lax.axis_size(("dp", "fsdp")), HEADS))
    summed = (
        lax.psum_scatter(d_gain_one, ("dp", "fsdp"), scatter_dimension=0, tiled=True),
        lax.psum_scatter(d_query_w, ("dp", "fsdp"), scatter_dimension=0, tiled=True),
        lax.psum_scatter(d_key_w, ("dp", "fsdp"), scatter_dimension=0, tiled=True),
        lax.psum_scatter(d_value_w, ("dp", "fsdp"), scatter_dimension=0, tiled=True),
        lax.psum_scatter(d_gate_w, ("dp", "fsdp"), scatter_dimension=0, tiled=True),
        lax.psum_scatter(bias_rows, ("dp", "fsdp"), scatter_dimension=0, tiled=True),
        lax.psum_scatter(d_out, ("dp", "fsdp"), scatter_dimension=0, tiled=True),
        lax.psum_scatter(d_gain_two, ("dp", "fsdp"), scatter_dimension=0, tiled=True),
        lax.psum_scatter(d_gate_ff, ("dp", "fsdp"), scatter_dimension=0, tiled=True),
        lax.psum_scatter(d_up, ("dp", "fsdp"), scatter_dimension=0, tiled=True),
        lax.psum_scatter(d_down, ("dp", "fsdp"), scatter_dimension=1, tiled=True),
    )
    return (
        output,
        grad_input.astype(jnp.bfloat16),
        summed[0],
        summed[1],
        summed[2],
        summed[3],
        summed[4],
        summed[5][0],
        summed[6],
        summed[7],
        summed[8],
        summed[9],
        summed[10],
    )


def solution(mesh):
    in_specs = (
        P(("dp", "fsdp"), None),
        P(("dp", "fsdp"), None),
        P(),
        P(),
        P(("dp", "fsdp")),
        P(("dp", "fsdp"), None),
        P(("dp", "fsdp"), None),
        P(("dp", "fsdp"), None),
        P(("dp", "fsdp"), None),
        P(),
        P(("dp", "fsdp"), None),
        P(("dp", "fsdp")),
        P(("dp", "fsdp"), None),
        P(("dp", "fsdp"), None),
        P(None, ("dp", "fsdp")),
    )
    out_specs = (
        P(("dp", "fsdp"), None),
        P(("dp", "fsdp"), None),
        P(("dp", "fsdp")),
        P(("dp", "fsdp"), None),
        P(("dp", "fsdp"), None),
        P(("dp", "fsdp"), None),
        P(("dp", "fsdp"), None),
        P(),
        P(("dp", "fsdp"), None),
        P(("dp", "fsdp")),
        P(("dp", "fsdp"), None),
        P(("dp", "fsdp"), None),
        P(None, ("dp", "fsdp")),
    )
    return jax.shard_map(shards, mesh=mesh, in_specs=in_specs, out_specs=out_specs, check_vma=False)
```

profile of v0, /device:TPU:0, one launch (start us, length us, event | category | flops | bytes accessed | tf_op | source)
XLA Modules:
  0.0 1867.0 jit_solution(7931201813034418137)
XLA Ops:
  11.2 42.1 %all-reduce.6 = (bf16[1024]{0:T(1024)(128)(2,1)S(1)}, bf16[1024]{0:T(1024)(128)(2,1)S(1)}) all-reduce(bf16[1024]{0:T(1024)(128)(2,1)S(1)} %dynamic-update-slice, bf16[1024]{0:T(1024)(128)(2,1)S(1)} %dynamic-update-slice.1), channel_id=1, replica_groups=mesh['dp'=2,'fsdp'=16] {'dp','fsdp'}, use_global_device_ids=true, to_apply=%add | all-reduce | flops 2048 | bytes 8192
  53.3 40.8 %all-gather.2 = bf16[32,32,16]{1,2,0:T(8,128)(2,1)S(1)} all-gather(bf16[1,32,16]{1,2,0:T(8,128)(2,1)} %bitcast.220), channel_id=1, replica_groups=mesh['dp'=2,'fsdp'=16] {'dp','fsdp'}, dimensions={0}, use_global_device_ids=true | all-gather | bytes 33792 | tf_op jit(solution)/shard_map/all_gather | solution.py:254
  99.7 2.1 fusion.75
  102.0 21.3 %all-gather.15.cloned.1.call-done = bf16[1024,512]{1,0:T(8,128)(2,1)} async-done(((bf16[32,512]{1,0:T(8,128)(2,1)}), bf16[1024,512]{1,0:T(8,128)(2,1)}) %all-gather.15.cloned.1.call-update) | async-done | bytes 1048592 | tf_op jit(solution)/shard_map/all_gather | solution.py:253
  123.3 2.1 convolution_convert_fusion
  131.8 39.2 %all-gather.3 = bf16[32,1,16]{2,1,0:T(2,128)(2,1)S(1)} all-gather(bf16[1,1,16]{2,1,0:T(2,128)(2,1)S(1)} %bitcast.224), channel_id=1, replica_groups=mesh['dp'=2,'fsdp'=16] {'dp','fsdp'}, dimensions={0}, use_global_device_ids=true | all-gather | bytes 1056 | tf_op jit(solution)/shard_map/all_gather | solution.py:23
  173.2 8.3 all-gather.17.cloned.1.call-done
  181.5 3.0 fusion.77
  186.1 8.2 fusion.82
  194.3 66.9 %all-gather.29.cloned.1.call-done = bf16[512,64,64]{2,1,0:T(8,128)(2,1)} async-done(((bf16[16,64,64]{2,1,0:T(8,128)(2,1)}), bf16[512,64,64]{2,1,0:T(8,128)(2,1)}) %all-gather.29.cloned.1.call-update) | async-done | bytes 4194320 | tf_op jit(solution)/shard_map/all_gather | solution.py:23
  261.2 36.7 %while.30 = (s32[]{:T(128)}, f32[16,64,64]{2,1,0:T(8,128)S(1)}, s32[]{:T(128)}, bf16[32,16]{1,0:T(8,128)(2,1)S(1)}, bf16[32,16,64,64]{3,2,1,0:T(8,128)(2,1)}, /*index=5*/s32[]{:T(128)}, s32[]{:T(128)}) while((s32[]{:T(128)}, f32[16,64,64]{2,1,0:T(8,128)S(1)}, s32[]{:T(128)}, bf16[32,16]{1,0:T(8,128)(2,1)S(1)}, ...), condition=%wide.region_4.5_spmd.clone, body=%wide.region_3.4_spmd.clone.sunk | while | flops 327700 | bytes 655625 | solution.py:41
  299.4 9.6 multiply_reduce_fusion.5
  311.7 7.3 all-gather.21.cloned.1.call-done
  319.0 3.3 multiply_reduce_fusion.4
  323.7 64.2 %all-gather.23.cloned.1.call-done = bf16[1024,2816]{1,0:T(8,128)(2,1)} async-done(((bf16[32,2816]{1,0:T(8,128)(2,1)}), bf16[1024,2816]{1,0:T(8,128)(2,1)}) %all-gather.23.cloned.1.call-update) | async-done | bytes 5767184 | tf_op jit(solution)/shard_map/all_gather | solution.py:257
  387.9 8.6 fusion.84
  396.5 60.6 %all-gather.25.cloned.1.call-done = bf16[1024,2816]{1,0:T(8,128)(2,1)} async-done(((bf16[32,2816]{1,0:T(8,128)(2,1)}), bf16[1024,2816]{1,0:T(8,128)(2,1)}) %all-gather.25.cloned.1.call-update) | async-done | bytes 5767184 | tf_op jit(solution)/shard_map/all_gather | solution.py:258
  457.1 8.5 fusion.85
  465.6 60.6 %all-gather.27.cloned.1.call-done = bf16[2816,1024]{0,1:T(8,128)(2,1)} async-done(((bf16[2816,32]{0,1:T(8,128)(2,1)}), bf16[2816,1024]{0,1:T(8,128)(2,1)}) %all-gather.27.cloned.1.call-update) | async-done | bytes 5767184 | tf_op jit(solution)/shard_map/all_gather | solution.py:259
  526.2 11.7 multiply_convert_fusion.2
  537.9 7.6 fusion.86
  545.5 3.5 multiply_reduce_fusion
  549.0 3.4 multiply_add_fusion
  558.1 39.4 %all-gather.4 = bf16[32,1,16]{2,1,0:T(2,128)(2,1)S(1)} all-gather(bf16[1,1,16]{2,1,0:T(2,128)(2,1)S(1)} %bitcast.223), channel_id=1, replica_groups=mesh['dp'=2,'fsdp'=16] {'dp','fsdp'}, dimensions={0}, use_global_device_ids=true | all-gather | bytes 1056 | tf_op jit(solution)/shard_map/all_gather | solution.py:23
  597.5 15.5 fusion.9
  613.0 9.0 fusion.66
  624.8 9.6 all-gather.31.cloned.1.call-done
  634.4 65.7 %while.31 = (s32[]{:T(128)}, f32[16,64,64]{2,1,0:T(8,128)}, s32[]{:T(128)}, bf16[32,16]{1,0:T(8,128)(2,1)S(1)}, bf16[32,16,64,64]{3,2,1,0:T(8,128)(2,1)}, /*index=5*/s32[]{:T(128)}, s32[]{:T(128)}, s32[]{:T(128)}, s32[]{:T(128)}) while((s32[]{:T(128)}, f32[16,64,64]{2,1,0:T(8,128)}, s32[]{:T(128)}, ...), condition=%wide.region_15.16_spmd.clone, body=%wide.region_14.15_spmd.clone.sunk | while | flops 327704 | bytes 655687 | solution.py:41
  636.3 2.1 fusion.150
  640.5 2.1 fusion.150
  642.5 2.1 fusion.150
  644.6 2.1 fusion.150
  646.6 2.1 fusion.150
  648.7 2.1 fusion.150
  650.8 2.1 fusion.150
  652.8 2.1 fusion.150
  654.9 2.1 fusion.150
  656.9 2.1 fusion.150
  659.0 2.1 fusion.150
  700.2 4.0 fusion.11
  709.4 4.8 fusion.72
  714.3 4.4 fusion.44
  718.7 11.8 fusion.22
  730.5 2.9 reduce_sum.212
  735.6 2.2 fusion.70
  737.9 9.1 fusion.65
  747.1 3.4 fusion.28
  750.5 2.7 reduce_sum.213
  753.2 3.3 fusion.68
  756.6 9.7 fusion.90
  766.4 9.6 fusion.91
  776.2 10.2 fusion.40
  786.4 3.4 fusion.87
  789.8 6.9 add_convert_fusion
  798.9 2.4 fusion.18
  801.2 39.5 %all-reduce.5 = (f32[1024]{0:T(1024)S(1)}, f32[32,16]{1,0:T(8,128)S(1)}, f32[1024]{0:T(1024)S(1)}) all-reduce(f32[1024]{0:T(1024)S(1)} %get-tuple-element.321, f32[32,16]{1,0:T(8,128)S(1)} %broadcast_in_dim.44, f32[1024]{0:T(1024)S(1)} %get-tuple-element.319), channel_id=4, replica_groups=mesh['dp'=2,'fsdp'=16] {'dp','fsdp'}, use_global_device_ids=true, to_apply=%region_28.29.clone | all-reduce | flops 2560 | bytes 20480
  842.4 3.1 fusion.17
  846.9 136.6 %reduce-scatter.11.cloned.1.call-done = f32[32,1024]{1,0:T(8,128)} async-done(((f32[1024,1024]{1,0:T(8,128)}), f32[32,1024]{1,0:T(8,128)}) %reduce-scatter.11.cloned.1.call-update) | async-done | bytes 131088 | tf_op jit(solution)/shard_map/reduce_scatter | solution.py:384
  983.5 140.1 %reduce-scatter.17.cloned.1.call-done = f32[32,1024]{1,0:T(8,128)} async-done(((f32[1024,1024]{1,0:T(8,128)}), f32[32,1024]{1,0:T(8,128)}) %reduce-scatter.17.cloned.1.call-update) | async-done | bytes 131088 | tf_op jit(solution)/shard_map/reduce_scatter | solution.py:389
  1123.6 136.0 %reduce-scatter.13.cloned.1.call-done = f32[32,512]{1,0:T(8,128)} async-done(((f32[1024,512]{1,0:T(8,128)}), f32[32,512]{1,0:T(8,128)}) %reduce-scatter.13.cloned.1.call-update) | async-done | bytes 65552 | tf_op jit(solution)/shard_map/reduce_scatter | solution.py:385
  1259.6 135.7 %reduce-scatter.15.cloned.1.call-done = f32[32,512]{1,0:T(8,128)} async-done(((f32[1024,512]{1,0:T(8,128)}), f32[32,512]{1,0:T(8,128)}) %reduce-scatter.15.cloned.1.call-update) | async-done | bytes 65552 | tf_op jit(solution)/shard_map/reduce_scatter | solution.py:386
  1395.4 153.4 %reduce-scatter.19.cloned.1.call-done = f32[32,2816]{1,0:T(8,128)} async-done(((f32[1024,2816]{1,0:T(8,128)}), f32[32,2816]{1,0:T(8,128)}) %reduce-scatter.19.cloned.1.call-update) | async-done | bytes 360464 | tf_op jit(solution)/shard_map/reduce_scatter | solution.py:391
  1548.7 155.9 %reduce-scatter.21.cloned.1.call-done = f32[32,2816]{1,0:T(8,128)} async-done(((f32[1024,2816]{1,0:T(8,128)}), f32[32,2816]{1,0:T(8,128)}) %reduce-scatter.21.cloned.1.call-update) | async-done | bytes 360464 | tf_op jit(solution)/shard_map/reduce_scatter | solution.py:392
  1704.6 155.6 %reduce-scatter.23.cloned.1.call-done = f32[2816,32]{0,1:T(8,128)} async-done(((f32[2816,1024]{0,1:T(8,128)}), f32[2816,32]{0,1:T(8,128)}) %reduce-scatter.23.cloned.1.call-update) | async-done | bytes 360464 | tf_op jit(solution)/shard_map/reduce_scatter | solution.py:393
  (313 shorter events, 124.5 us)
Async XLA Ops:
  7.2 92.5 %all-gather.19.cloned.1.call-start = ((), (), s32[]{:S(2)}) async-start(), calls=%async_computation.10 | async-start | bytes 1081344 | tf_op jit(solution)/shard_map/all_gather | solution.py:252
  7.9 115.4 %all-gather.15.cloned.1.call-start = ((), (), s32[]{:S(2)}) async-start(), calls=%async_computation.8 | async-start | bytes 1081344 | tf_op jit(solution)/shard_map/all_gather | solution.py:253
  8.7 172.8 %all-gather.17.cloned.1.call-start = ((), (), s32[]{:S(2)}) async-start(), calls=%async_computation.9 | async-start | bytes 2162688 | tf_op jit(solution)/shard_map/all_gather | solution.py:251
  9.4 251.8 %all-gather.29.cloned.1.call-start = ((), (), s32[]{:S(2)}) async-start(), calls=%async_computation.22 | async-start | bytes 8650752 | tf_op jit(solution)/shard_map/all_gather | solution.py:23
  9.4 90.2 %copy-start = (bf16[512,1024]{1,0:T(8,128)(2,1)S(1)}, bf16[512,1024]{1,0:T(8,128)(2,1)}, u32[]{:S(2)}) copy-start(bf16[512,1024]{1,0:T(8,128)(2,1)} %param.19) | copy-start | bytes 3145732
  94.3 7.4 copy-start.32
  102.0 23.4 %copy-start.22 = (bf16[512,2,4,64]{0,3,2,1:T(8,128)(2,1)}, bf16[512,2,4,64]{0,3,2,1:T(8,128)(2,1)S(1)}, u32[]{:S(2)}) copy-start(bf16[512,2,4,64]{0,3,2,1:T(8,128)(2,1)S(1)} %pad_maximum_fusion) | copy-start | bytes 1572868
  125.5 1.0 copy-start.12
  125.6 1.2 copy-start.25
  125.6 45.4 %copy-start.36 = (s32[8]{0:T(128)S(1)}, s32[8]{0:T(128)}, u32[]{:S(2)}) copy-start(s32[8]{0:T(128)} %param.22) | copy-start | bytes 100
  125.6 45.4 %copy-start.34 = (s32[8]{0:T(128)S(1)}, s32[8]{0:T(128)}, u32[]{:S(2)}) copy-start(s32[8]{0:T(128)} %param.21) | copy-start | bytes 100
  128.8 190.3 %all-gather.21.cloned.1.call-start = ((), (), s32[]{:S(2)}) async-start(), calls=%async_computation.11 | async-start | bytes 2162688 | tf_op jit(solution)/shard_map/all_gather | solution.py:255
  129.4 258.6 %all-gather.23.cloned.1.call-start = ((), (), s32[]{:S(2)}) async-start(), calls=%async_computation.12 | async-start | bytes 5947392 | tf_op jit(solution)/shard_map/all_gather | solution.py:257
  129.9 327.1 %all-gather.25.cloned.1.call-start = ((), (), s32[]{:S(2)}) async-start(), calls=%async_computation.13 | async-start | bytes 5947392 | tf_op jit(solution)/shard_map/all_gather | solution.py:258
  130.7 395.5 %all-gather.27.cloned.1.call-start = ((), (), s32[]{:S(2)}) async-start(), calls=%async_computation.14 | async-start | bytes 5947392 | tf_op jit(solution)/shard_map/all_gather | solution.py:259
  131.4 503.0 %all-gather.31.cloned.1.call-start = ((), (), s32[]{:S(2)}) async-start(), calls=%async_computation.23 | async-start | bytes 8650752 | tf_op jit(solution)/shard_map/all_gather | solution.py:23
  131.6 167.5 %copy-start.30 = (pred[512,512]{1,0:T(8,128)(4,1)}, pred[512,512]{1,0:T(8,128)(4,1)S(1)}, u32[]{:S(2)}) copy-start(pred[512,512]{1,0:T(8,128)(4,1)S(1)} %iota_compare_fusion) | copy-start | bytes 786436
  184.9 1.2 copy-start.13
  186.1 111.9 %copy-start.10 = (bf16[512,16,64]{0,2,1:T(8,128)(2,1)}, bf16[512,16,64]{0,2,1:T(8,128)(2,1)S(1)}, u32[]{:S(2)}) copy-start(bf16[512,16,64]{0,2,1:T(8,128)(2,1)S(1)} %fusion.20) | copy-start | bytes 3145732
  298.0 11.1 copy-start.1
  298.0 1.4 copy-start.26
  299.1 10.0 copy-start.16
  309.1 1.3 copy-start.8
  322.3 223.2 %copy-start.6 = (f32[512,1024]{1,0:T(8,128)}, f32[512,1024]{1,0:T(8,128)S(1)}, u32[]{:S(2)}) copy-start(f32[512,1024]{1,0:T(8,128)S(1)} %get-tuple-element.378) | copy-start | bytes 6291460
  537.9 7.6 copy-start.38
  537.9 7.6 copy-start.37
  537.9 7.6 copy-start.35
  545.5 3.5 copy-start.29
  549.0 3.4 copy-start.9
  549.0 3.4 copy-start.18
  552.5 1.6 copy-start.17
  554.1 2.0 copy-start.11
  555.1 1.0 copy-start.23
  558.0 287.5 %reduce-scatter.25.cloned.1.call-start = ((), (), s32[]{:S(2)}) async-start(), calls=%async_computation.24 | async-start | bytes 540672
  597.4 15.5 copy-start.14
  597.5 15.5 copy-start.31
  613.0 9.0 copy-start.2
  613.0 9.0 copy-start.24
  700.2 4.0 copy-start.3
  700.2 4.0 copy-start.4
  709.4 274.1 %reduce-scatter.11.cloned.1.call-start = ((), (), s32[]{:S(2)}) async-start(), calls=%async_computation.15 | async-start | bytes 4325376 | tf_op jit(solution)/shard_map/reduce_scatter | solution.py:384
  714.2 409.4 %reduce-scatter.17.cloned.1.call-start = ((), (), s32[]{:S(2)}) async-start(), calls=%async_computation.18 | async-start | bytes 4325376 | tf_op jit(solution)/shard_map/reduce_scatter | solution.py:389
  718.7 541.0 %reduce-scatter.13.cloned.1.call-start = ((), (), s32[]{:S(2)}) async-start(), calls=%async_computation.16 | async-start | bytes 2162688 | tf_op jit(solution)/shard_map/reduce_scatter | solution.py:385
  734.8 0.8 copy-start.19
  737.8 657.5 %reduce-scatter.15.cloned.1.call-start = ((), (), s32[]{:S(2)}) async-start(), calls=%async_computation.17 | async-start | bytes 2162688 | tf_op jit(solution)/shard_map/reduce_scatter | solution.py:386
  737.9 9.2 copy-start.5
  737.9 9.2 copy-start.15
  756.5 792.2 %reduce-scatter.19.cloned.1.call-start = ((), (), s32[]{:S(2)}) async-start(), calls=%async_computation.19 | async-start | bytes 11894784 | tf_op jit(solution)/shard_map/reduce_scatter | solution.py:391
  766.3 938.3 %reduce-scatter.21.cloned.1.call-start = ((), (), s32[]{:S(2)}) async-start(), calls=%async_computation.20 | async-start | bytes 11894784 | tf_op jit(solution)/shard_map/reduce_scatter | solution.py:392
  775.9 1084.3 %reduce-scatter.23.cloned.1.call-start = ((), (), s32[]{:S(2)}) async-start(), calls=%async_computation.21 | async-start | bytes 11894784 | tf_op jit(solution)/shard_map/reduce_scatter | solution.py:393
  786.4 3.4 copy-start.7
  786.4 3.4 copy-start.39
  789.8 6.9 copy-start.20
  789.8 6.9 copy-start.27
  796.7 1.0 copy-start.21
  796.7 1.4 copy-start.28
  798.1 0.8 copy-start.33
Sparse Core Ops, SparseCore 0:
  10.9 56.5 all-gather.18
  70.4 52.8 all-gather.14
  126.1 55.2 all-gather.16
  184.8 76.4 all-gather.28
  264.0 55.0 all-gather.20
  321.8 66.1 all-gather.22
  390.8 66.2 all-gather.24
  460.0 66.2 all-gather.26
  558.1 76.2 all-gather.30
  709.5 132.6 reduce-scatter.24
  845.1 138.2 reduce-scatter.10
  986.3 137.2 reduce-scatter.16
  1126.5 133.0 reduce-scatter.12
  1262.3 132.9 reduce-scatter.14
  1398.2 150.4 reduce-scatter.18
  1551.6 153.0 reduce-scatter.20
  1707.5 152.7 reduce-scatter.22
where the time goes:
time: 1880 us; the launch traced here: 1870 us
  waiting for transfers between devices  1320 us (70%)
  blocking collectives  201 us (11%)
  matrix products  190 us (10%)
  other arithmetic  129 us (7%)
    reduce_scatter x1, waiting for transfers between devices, shards(): lax.psum_scatter(d_up, ('dp', 'fsdp'), scatter_dimension=0, tiled=True)  156 us
    reduce_scatter x1, waiting for transfers between devices, shards(): lax.psum_scatter(d_down, ('dp', 'fsdp'), scatter_dimension=1, tiled=True)  156 us
    reduce_scatter x1, waiting for transfers between devices, shards(): lax.psum_scatter(d_gate_ff, ('dp', 'fsdp'), scatter_dimension=0, tiled=True)  153 us
    reduce_scatter x1, waiting for transfers between devices, shards(): lax.psum_scatter(d_out, ('dp', 'fsdp'), scatter_dimension=0, tiled=True)  140 us
    reduce_scatter x1, waiting for transfers between devices, shards(): lax.psum_scatter(d_query_w, ('dp', 'fsdp'), scatter_dimension=0, tiled=True)  137 us
    reduce_scatter x1, waiting for transfers between devices, shards(): lax.psum_scatter(d_key_w, ('dp', 'fsdp'), scatter_dimension=0, tiled=True)  136 us
    reduce_scatter x1, waiting for transfers between devices, shards(): lax.psum_scatter(d_value_w, ('dp', 'fsdp'), scatter_dimension=0, tiled=True)  136 us
    select_n x64, other arithmetic, step(): return jax.tree.map(lambda a, b: jnp.where(reached, a, b), new, before)  100 us
  transfers between devices with their start and end apart: 17, of which 15 were waited for; matrix products, arithmetic and copies ran while one was open for 12% of the time, Pallas kernels for 0%

commit v1 on v0

v1 whole, which is shorter than its diff:
```python
import jax
import jax.numpy as jnp
from jax import lax
from jax.sharding import Mesh, PartitionSpec as P

HEADS = 16
HEAD = 64
KVH = 2
LATENT = 256
SPAN = 4

epsilon = 1e-05
head_floor = 0.25
ROPE_BASE = 10000.0
GATE_TEMP = 16.0
HIGHEST = lax.Precision.HIGHEST

CHIPS = ("dp", "hi", "mid")
ALL = ("dp", "hi", "mid", "core")
F32 = jnp.float32
BF16 = jnp.bfloat16


def swap(v, axis):
    return lax.ppermute(v, axis, [(0, 1), (1, 0)])


def place(bit, mine, theirs):
    return jnp.where(
        bit == 0, jnp.concatenate([mine, theirs], 0), jnp.concatenate([theirs, mine], 0)
    )


def square_gather(part):
    half = part.shape[0] // 2
    over_dp, over_mid = swap(part, "dp"), swap(part, "mid")
    first = swap(over_dp[:half], "mid")
    second = swap(over_mid[half:], "dp")
    diagonal = jnp.concatenate([first, second], 0)
    dp, mid = lax.axis_index("dp"), lax.axis_index("mid")
    near = place(mid, part[None], over_mid[None])
    far = place(mid, over_dp[None], diagonal[None])
    return place(dp, near[None], far[None])


def hi_gather(part, by_permutes):
    if not by_permutes:
        return lax.all_gather(part, "hi")
    hi = lax.axis_index("hi")
    other = lax.ppermute(part, "hi", [(i, i ^ 2) for i in range(4)])
    pair = place(hi // 2, part[None], other[None])
    opposite = lax.ppermute(pair, "hi", [(i, i ^ 1) for i in range(4)])
    both = jnp.where(
        hi % 2 == 0, jnp.stack([pair, opposite], 1), jnp.stack([opposite, pair], 1)
    )
    return both.reshape((4,) + part.shape)


def gather(part, how):
    rows, width = part.shape
    if how == "whole" or lax.axis_size("dp") != 2 or lax.axis_size("hi") != 4:
        return lax.all_gather(part, CHIPS, axis=0, tiled=True)
    stacked = hi_gather(part, how == "permutes")
    square = square_gather(stacked)
    return square.transpose(0, 2, 1, 3, 4).reshape(-1, width)


def square_scatter(parts):
    dp, mid = lax.axis_index("dp"), lax.axis_index("mid")
    half = parts.shape[2] // 2

    def at(a, b):
        piece = lax.dynamic_index_in_dim(parts, a, 0, keepdims=False)
        return lax.dynamic_index_in_dim(piece, b, 0, keepdims=False)

    own, over_dp = at(dp, mid), at(1 - dp, mid)
    over_mid, diagonal = at(dp, 1 - mid), at(1 - dp, 1 - mid)
    to_mid = swap(diagonal[:half], "dp")
    to_dp = swap(diagonal[half:], "mid")
    send_mid = jnp.concatenate([over_mid[:half] + to_mid, over_mid[half:]], 0)
    send_dp = jnp.concatenate([over_dp[:half], over_dp[half:] + to_dp], 0)
    return own.astype(F32) + swap(send_dp, "dp").astype(F32) + swap(send_mid, "mid").astype(F32)


def scatter(whole, how):
    rows, width = whole.shape
    chips = lax.axis_size(CHIPS)
    if how == "whole" or lax.axis_size("dp") != 2 or lax.axis_size("hi") != 4:
        return lax.psum_scatter(whole.astype(BF16), CHIPS, scatter_dimension=0, tiled=True)
    parts = whole.astype(BF16).reshape(2, 4, 2, rows // chips, width).transpose(0, 2, 1, 3, 4)
    stacked = square_scatter(parts)
    if how == "permutes":
        hi = lax.axis_index("hi")
        stacked = stacked.reshape(2, 2, rows // chips, width)
        mine = lax.dynamic_index_in_dim(stacked, hi % 2, 1, keepdims=False)
        theirs = lax.dynamic_index_in_dim(stacked, 1 - hi % 2, 1, keepdims=False)
        pair = mine + lax.ppermute(
            theirs.astype(BF16), "hi", [(i, i ^ 1) for i in range(4)]
        ).astype(F32)
        mine = lax.dynamic_index_in_dim(pair, hi // 2, 0, keepdims=False)
        theirs = lax.dynamic_index_in_dim(pair, 1 - hi // 2, 0, keepdims=False)
        return mine + lax.ppermute(
            theirs.astype(BF16), "hi", [(i, i ^ 2) for i in range(4)]
        ).astype(F32)
    return lax.psum_scatter(stacked.astype(BF16), "hi", scatter_dimension=0, tiled=False)


def to_owner(rows, core):
    count = rows.shape[0] // 2
    rows = rows.astype(BF16).reshape(2, count, rows.shape[1])
    mine = lax.dynamic_index_in_dim(rows, core, 0, keepdims=False)
    theirs = lax.dynamic_index_in_dim(rows, 1 - core, 0, keepdims=False)
    return mine, swap(theirs, "core")


def beside(core, mine, theirs):
    return jnp.where(
        core == 0, jnp.concatenate([mine, theirs], 1), jnp.concatenate([theirs, mine], 1)
    ).astype(F32)


def inverse_rms(values, added=epsilon):
    return lax.rsqrt(jnp.mean(values * values, axis=-1, keepdims=True) + added)


def norm_back(grad_unit, unit_rows, scale_rows):
    return scale_rows * (
        grad_unit - unit_rows * jnp.mean(grad_unit * unit_rows, axis=-1, keepdims=True)
    )


def rope_tables(positions):
    half_width = HEAD // 2
    frequency = ROPE_BASE ** (-jnp.arange(half_width, dtype=F32) / half_width)
    angles = positions.astype(F32)[..., None] * frequency
    return jnp.cos(angles)[..., None, :], jnp.sin(angles)[..., None, :]


def rotate(values, cosine, sine_part):
    half_width = values.shape[-1] // 2
    leading = values[..., :half_width]
    trailing = values[..., half_width:]
    return jnp.concatenate(
        [leading * cosine - trailing * sine_part, trailing * cosine + leading * sine_part], axis=-1
    )


def matmul(left, right):
    return jnp.dot(left, right, preferred_element_type=F32)


def contract_rows(left, right):
    return jnp.einsum("ta,tb->ab", left, right, preferred_element_type=F32)


def against(left, right):
    return jnp.einsum("tb,ab->ta", left, right, preferred_element_type=F32)


def sequence_weights(group_ids, loss_weights):
    group_count = loss_weights.shape[0]
    member = (group_ids[:, None] == jnp.arange(group_count, dtype=jnp.int32)[None, :]).astype(F32)
    counts = jnp.sum(member, axis=0)
    raw_weight = jnp.sum(member * loss_weights.astype(F32)[None, :], axis=1) / jnp.sum(
        member * counts[None, :], axis=1
    )
    return raw_weight * (group_ids.shape[0] / jnp.sum(raw_weight))


def broaden(latent):
    return jnp.concatenate([latent, latent], axis=-2)


def narrow(gradient):
    slots = gradient.shape[-2] // 2
    return gradient[..., :slots, :] + gradient[..., slots:, :]


def decay_table(cumulative):
    count = cumulative.shape[1]
    order = jnp.arange(count)
    causal = order[:, None] >= order[None, :]
    rows = cumulative.transpose(0, 2, 1)
    differences = rows[:, :, :, None] - rows[:, :, None, :]
    return jnp.where(causal, jnp.exp(jnp.where(causal, differences, 0.0)), 0.0)


AG = dict(front="permutes", out="permutes", ff="hi", down="hi")
RS = dict(front="permutes", out="hi", gate="hi", up="hi", down="hi")


def shards(
    tokens,
    cotangent,
    group_ids,
    loss_weights,
    gain_one,
    w_query,
    w_key,
    w_value,
    w_gate,
    gate_bias,
    w_out,
    gain_two,
    w_gate_ff,
    w_up,
    w_down,
):
    count, width = tokens.shape
    local = HEADS // 2
    slots = KVH * (LATENT // HEAD) // 2
    core, mid = lax.axis_index("core"), lax.axis_index("mid")
    sequence = (lax.axis_index(("dp", "hi", "mid", "core"))) // SPAN

    def halves(w):
        half = w.shape[1] // 2
        return w[:, :half], w[:, half:]

    wq, wk, wv = halves(w_query), halves(w_key), halves(w_value)
    wo, wg, wu, wd = halves(w_out), halves(w_gate_ff), halves(w_up), halves(w_down.T)
    wa = halves(w_gate)
    pad = 128 - local - 2

    def packed(i):
        front = [wq[i], wk[i], wv[i], wa[i], gain_one[:, None], gain_two[:, None]]
        front.append(jnp.zeros((gain_one.shape[0], pad), BF16))
        return jnp.concatenate(front + [wo[i], wg[i], wu[i], wd[i]], axis=1)

    first, second = packed(0), packed(1)
    kept = jnp.where(core == 0, first, second)
    sent = jnp.where(core == 0, second, first)
    chip = place(core, kept, swap(sent, "core"))
    n_front = (w_query.shape[1] + w_key.shape[1] + w_value.shape[1]) // 2 + 128
    n_out = w_out.shape[1] // 2
    n_ff = w_up.shape[1] // 2
    other_tokens = swap(tokens, "core")
    other_cotangent = swap(cotangent, "core")
    ends = [n_front, n_front + n_out, n_front + n_out + 2 * n_ff]
    w_front = gather(chip[:, : ends[0]], AG["front"])
    w_out_half = gather(chip[:, ends[0] : ends[1]], AG["out"])
    w_ff = gather(chip[:, ends[1] : ends[2]], AG["ff"])
    w_down_t = gather(chip[:, ends[2] :], AG["down"])
    w_gate_ff, w_up = w_ff[:, :n_ff], w_ff[:, n_ff:]
    w_out_other = swap(w_out_half, "core")
    w_out = jnp.where(
        core == 0,
        jnp.concatenate([w_out_half, w_out_other], 1),
        jnp.concatenate([w_out_other, w_out_half], 1),
    )

    gains = w_front[:, n_front - 128 + local : n_front - 128 + local + 2].T.astype(F32)
    gain_one, gain_two = gains[0], gains[1]
    inputs = jnp.stack([tokens, other_tokens]).astype(F32)
    scale_one = inverse_rms(inputs)
    unit_one = inputs * scale_one
    normed_one = (unit_one * gain_one).astype(BF16).reshape(2 * count, width)
    pre = matmul(normed_one, w_front).reshape(2, count, n_front)
    n_q, n_k = local * HEAD, slots * HEAD
    block = 2 * mid + (core ^ jnp.arange(2))
    positions = block[:, None] * count + jnp.arange(count)[None, :]
    cosine, sine_part = rope_tables(positions)
    queries = (
        rotate(pre[..., :n_q].reshape(2, count, local, HEAD), cosine, sine_part)
        * float(HEAD) ** (-0.5)
    ).astype(BF16)
    keys = rotate(
        pre[..., n_q : n_q + n_k].reshape(2, count, slots, HEAD), cosine, sine_part
    ).astype(BF16)
    values = pre[..., n_q + n_k : n_q + 2 * n_k].reshape(2, count, slots, HEAD).astype(BF16)
    own_bias = lax.dynamic_slice_in_dim(gate_bias, core * local, local)
    gate_in = pre[..., n_q + 2 * n_k : n_q + 2 * n_k + local] + own_bias
    key_heads, value_heads = broaden(keys), broaden(values)
    log_decay = -jax.nn.softplus(gate_in) / GATE_TEMP
    cumulative = jnp.cumsum(log_decay, axis=1)
    decay_rows = decay_table(cumulative)
    scores = jnp.einsum("bthd,bshd->bhts", queries, key_heads, preferred_element_type=F32)
    weighted = (scores * decay_rows).astype(BF16)
    local_part = jnp.einsum("bhts,bshe->bthe", weighted, value_heads, preferred_element_type=F32)
    last_cum = cumulative[:, -1]
    total_decay = jnp.exp(last_cum)
    tail_decay = jnp.exp(last_cum[:, None, :] - cumulative)
    key_scaled = key_heads.astype(F32) * tail_decay[..., None]
    update = jnp.einsum("bshd,bshe->bhde", key_scaled, value_heads.astype(F32), precision=HIGHEST)

    def in_order(v):
        return jnp.where(core == 0, v, v[::-1])

    decay_seq = in_order(total_decay)[:, :, None, None]
    update_seq = in_order(update)
    leaving = decay_seq[1] * update_seq[0] + update_seq[1]
    state_0 = lax.ppermute(leaving.astype(BF16), "mid", [(0, 1)]).astype(F32)
    state_1 = decay_seq[0] * state_0 + update_seq[0]
    state_in = in_order(jnp.stack([state_0, state_1]))
    queries_float = queries.astype(F32)
    growth = jnp.exp(cumulative)
    carried_part = growth[..., None] * jnp.einsum(
        "bthd,bhde->bthe", queries_float, state_in, precision=HIGHEST
    )
    mixed_out = local_part + carried_part
    head_scale = inverse_rms(mixed_out, head_floor)
    head_normed = mixed_out * head_scale
    normed_pair = head_normed.astype(BF16).reshape(2, count, local * HEAD)
    normed_theirs = swap(normed_pair[1], "core")
    normed_flat = jnp.where(
        core == 0,
        jnp.concatenate([normed_pair[0], normed_theirs], 1),
        jnp.concatenate([normed_theirs, normed_pair[0]], 1),
    )
    attention = matmul(normed_flat, w_out)
    middle = inputs[0] + attention
    scale_two = inverse_rms(middle)
    unit_two = middle * scale_two
    normed_two_own = (unit_two * gain_two).astype(BF16)
    normed_two = jnp.concatenate([normed_two_own, swap(normed_two_own, "core")], 0)
    gate_ff = matmul(normed_two, w_gate_ff)
    up_ff = matmul(normed_two, w_up)
    sigmoid_gate = jax.nn.sigmoid(gate_ff)
    silu_gate = gate_ff * sigmoid_gate
    hidden = (silu_gate * up_ff).astype(BF16)
    seq_weights = sequence_weights(group_ids, loss_weights)
    own_weight = jnp.sum(jnp.where(jnp.arange(group_ids.shape[0]) == sequence, seq_weights, 0.0))
    grad_out = cotangent.astype(F32) * own_weight
    grad_branch = jnp.concatenate(
        [grad_out.astype(BF16), (other_cotangent.astype(F32) * own_weight).astype(BF16)], 0
    )
    d_down = scatter(contract_rows(grad_branch, hidden), RS["down"])
    grad_hidden = matmul(grad_branch, w_down_t)
    grad_gate = (
        grad_hidden * up_ff * (sigmoid_gate * (1.0 + gate_ff * (1.0 - sigmoid_gate)))
    ).astype(BF16)
    grad_up = (grad_hidden * silu_gate).astype(BF16)
    d_gate_ff = scatter(contract_rows(normed_two, grad_gate), RS["gate"])
    d_up = scatter(contract_rows(normed_two, grad_up), RS["up"])
    part = against(grad_gate, w_gate_ff) + against(grad_up, w_up)
    grad_normed_two = part[:count] + swap(part[count:].astype(BF16), "core").astype(F32)
    d_gain_two = jnp.sum(grad_normed_two * unit_two, axis=0)
    grad_middle = grad_out + norm_back(grad_normed_two * gain_two, unit_two, scale_two)
    grad_attention = grad_middle.astype(BF16)
    out_part = against(hidden, w_down_t)
    output = middle + (out_part[:count] + swap(out_part[count:].astype(BF16), "core").astype(F32))

    d_out_part = contract_rows(normed_flat, grad_attention)
    d_out_halves = d_out_part[:, :n_out], d_out_part[:, n_out:]
    d_out_kept = jnp.where(core == 0, d_out_halves[0], d_out_halves[1])
    d_out_sent = jnp.where(core == 0, d_out_halves[1], d_out_halves[0]).astype(BF16)
    d_out = scatter(d_out_kept + swap(d_out_sent, "core").astype(F32), RS["out"])
    grad_normed = against(grad_attention, w_out)
    grad_halves = grad_normed[:, : local * HEAD], grad_normed[:, local * HEAD :]
    grad_kept = jnp.where(core == 0, grad_halves[0], grad_halves[1])
    grad_sent = jnp.where(core == 0, grad_halves[1], grad_halves[0]).astype(BF16)
    grad_normed = jnp.stack([grad_kept, swap(grad_sent, "core").astype(F32)])
    grad_normed = grad_normed.reshape(2, count, local, HEAD)
    grad_mixed = norm_back(grad_normed, head_normed, head_scale).astype(BF16)
    grad_mixed_f = grad_mixed.astype(F32)
    through = jnp.einsum(
        "bthd,bthe->bhde", queries_float * growth[..., None], grad_mixed_f, precision=HIGHEST
    )
    through_seq = in_order(through)
    entering = through_seq[0] + decay_seq[0] * through_seq[1]
    later_1 = lax.ppermute(entering.astype(BF16), "mid", [(1, 0)]).astype(F32)
    later_0 = through_seq[1] + decay_seq[1] * later_1
    later_state = in_order(jnp.stack([later_0, later_1]))
    grad_weighted = jnp.einsum(
        "bthe,bshe->bhts", grad_mixed, value_heads, preferred_element_type=F32
    )
    d_values = jnp.einsum("bhts,bthe->bshe", weighted, grad_mixed, preferred_element_type=F32)
    grad_scores = (grad_weighted * decay_rows).astype(BF16)
    d_queries = jnp.einsum("bhts,bshd->bthd", grad_scores, key_heads, preferred_element_type=F32)
    d_keys = jnp.einsum("bhts,bthd->bshd", grad_scores, queries, preferred_element_type=F32)
    spread = grad_weighted * scores * decay_rows
    grad_cum = (jnp.sum(spread, axis=3) - jnp.sum(spread, axis=2)).transpose(0, 2, 1)
    d_queries = d_queries + growth[..., None] * jnp.einsum(
        "bthe,bhde->bthd", grad_mixed_f, state_in, precision=HIGHEST
    )
    grad_cum = grad_cum + jnp.sum(grad_mixed_f * carried_part, axis=3)
    grad_total = jnp.sum(later_state * state_in, axis=(2, 3))
    key_side = jnp.einsum(
        "bshe,bhde->bshd", value_heads.astype(F32), later_state, precision=HIGHEST
    )
    d_keys = d_keys + key_side * tail_decay[..., None]
    d_values = d_values + jnp.einsum(
        "bshd,bhde->bshe", key_scaled, later_state, precision=HIGHEST
    )
    grad_tail = jnp.sum(key_side * key_heads.astype(F32), axis=3) * tail_decay
    grad_cum = grad_cum - grad_tail
    last_row = (jnp.arange(count) == count - 1).astype(F32)[None, :, None]
    grad_cum = grad_cum + last_row * (
        jnp.sum(grad_tail, axis=1) + grad_total * total_decay
    )[:, None, :]
    grad_log = jnp.flip(jnp.cumsum(jnp.flip(grad_cum, 1), axis=1), 1)
    grad_gate_pre_f = -grad_log * jax.nn.sigmoid(gate_in) / GATE_TEMP
    d_bias = jnp.sum(grad_gate_pre_f, axis=(0, 1))
    grad_gate_pre = grad_gate_pre_f.astype(BF16)
    grad_query_pre = (rotate(d_queries, cosine, -sine_part) * float(HEAD) ** (-0.5)).astype(BF16)
    grad_key_pre = rotate(narrow(d_keys), cosine, -sine_part).astype(BF16)
    grad_value_pre = narrow(d_values).astype(BF16)
    grad_front = jnp.concatenate(
        [
            grad_query_pre.reshape(2 * count, n_q),
            grad_key_pre.reshape(2 * count, n_k),
            grad_value_pre.reshape(2 * count, n_k),
            grad_gate_pre.reshape(2 * count, local),
            jnp.zeros((2 * count, 128 - local), BF16),
        ],
        axis=1,
    )
    d_front = contract_rows(normed_one, grad_front)
    part = against(grad_front, w_front)
    d_gain_one = jnp.sum(part * unit_one.reshape(2 * count, width), axis=0)
    d_front = jnp.concatenate(
        [
            d_front[:, : n_front - 128 + local],
            d_gain_one[:, None],
            d_gain_two[:, None],
            jnp.broadcast_to(d_bias[None, :], (width, local)),
            jnp.zeros((width, 128 - 2 * local - 2), F32),
        ],
        axis=1,
    )
    d_front = scatter(d_front, RS["front"])
    grad_normed_one = part[:count] + swap(part[count:].astype(BF16), "core").astype(F32)
    grad_input = grad_middle + norm_back(grad_normed_one * gain_one, unit_one[0], scale_one[0])

    summed = jnp.concatenate(
        [v.astype(BF16) for v in (d_front, d_out, d_gate_ff, d_up, d_down)], axis=1
    )
    mine, theirs = to_owner(summed, core)
    ends = [0, n_q, n_q + n_k, n_q + 2 * n_k]
    g_query = beside(core, mine[:, ends[0] : ends[1]], theirs[:, ends[0] : ends[1]])
    g_key = beside(core, mine[:, ends[1] : ends[2]], theirs[:, ends[1] : ends[2]])
    g_value = beside(core, mine[:, ends[2] : ends[3]], theirs[:, ends[2] : ends[3]])
    at = ends[3]
    g_gate = beside(core, mine[:, at : at + local], theirs[:, at : at + local])
    at = at + local
    g_gains = mine[:, at : at + 2].astype(F32) + theirs[:, at : at + 2].astype(F32)
    at = at + 2
    g_bias = beside(core, mine[:1, at : at + local], theirs[:1, at : at + local])[0]
    ends = [n_front, n_front + n_out, n_front + n_out + n_ff, n_front + n_out + 2 * n_ff]
    ends.append(ends[-1] + n_ff)
    big = [
        beside(core, mine[:, a:b], theirs[:, a:b]) for a, b in zip(ends[:-1], ends[1:])
    ]
    return (
        output.astype(BF16),
        grad_input.astype(BF16),
        g_gains[:, 0],
        g_query,
        g_key,
        g_value,
        g_gate,
        g_bias,
        big[0],
        g_gains[:, 1],
        big[1],
        big[2],
        big[3].T,
    )


def solution(mesh):
    devices = mesh.devices
    fine = Mesh(
        devices.reshape(devices.shape[0], devices.shape[1] // SPAN, SPAN // 2, 2), ALL
    )
    rows, columns, split = P(ALL, None), P(None, ALL), P(ALL)
    in_specs = (rows, rows, P(), P(), split) + (rows,) * 4 + (P(), rows, split, rows, rows, columns)
    out_specs = (rows, rows, split) + (rows,) * 4 + (P(), rows, split, rows, rows, columns)
    return jax.shard_map(shards, mesh=fine, in_specs=in_specs, out_specs=out_specs, check_vma=False)
```

time: 1880 us -> 567 us (0.30)
  waiting for transfers between devices: 1320 us -> 147 us
  blocking collectives: 201 us -> 36.5 us
  starting transfers between devices: 0.85 us -> 67.8 us
  other arithmetic: 129 us -> 79 us
  local copies, waits for them, and re-layouts: 13 us -> 62.1 us
  matrix products: 190 us -> 151 us
    reduce_scatter x7 -> x4, waiting for transfers between devices: 1010 us -> 0.06 us  [scatter(): lax.psum_scatter(stacked.astype(BF16), 'hi', scatter_dimension=0, tiled=F...]
    all_gather x9 -> x1, waiting for transfers between devices: 299 us -> 0.01 us  [hi_gather(): return lax.all_gather(part, 'hi')]
    ppermute x0 -> x56, waiting for transfers between devices: none -> 147 us  [the longest x48 119 us: swap(): return lax.ppermute(v, axis, [(0, 1), (1, 0)])]
    select_n x64 -> x23, other arithmetic: 100 us -> 11.9 us  [the longest x15 9.72 us: place(): jnp.where(bit == 0, jnp.concatenate([mine, theirs], 0), jnp.concatenate([...]
    all_gather x3 -> x1, blocking collectives: 119 us -> 36.5 us  [hi_gather(): return lax.all_gather(part, 'hi')]
    unnamed x2 -> x0, blocking collectives: 81.5 us -> none
    ppermute x0 -> x56, starting transfers between devices: none -> 67.6 us  [the longest x48 55.2 us: swap(): return lax.ppermute(v, axis, [(0, 1), (1, 0)])]
    dot_general x35 -> x27, matrix products: 188 us -> 151 us  [the longest x5 33.1 us: matmul(): return jnp.dot(left, right, preferred_element_type=F32)]
  transfers between devices with their start and end apart: 17 -> 61, of which waited for: 15 -> 26; matrix products, arithmetic and copies ran while one was open for 12% -> 42% of each run, Pallas kernels for 0% -> 0%
where the time goes in v1:
time: 567 us; the launch traced here: 560 us
  matrix products  151 us (27%)
  waiting for transfers between devices  147 us (26%)
  other arithmetic  79 us (14%)
  starting transfers between devices  67.8 us (12%)
  local copies, waits for them, and re-layouts  62.1 us (11%)
  blocking collectives  36.5 us (6%)
  between operations  16.6 us (3%)
    ppermute x48, waiting for transfers between devices, swap(): return lax.ppermute(v, axis, [(0, 1), (1, 0)])  119 us
    ppermute x48, starting transfers between devices, swap(): return lax.ppermute(v, axis, [(0, 1), (1, 0)])  55.2 us
    all_gather x1, blocking collectives, hi_gather(): return lax.all_gather(part, 'hi')  36.5 us
    dot_general x5, matrix products, matmul(): return jnp.dot(left, right, preferred_element_type=F32)  33.1 us
    dot_general x5, matrix products, against(): return jnp.einsum('tb,ab->ta', left, right, preferred_element_type=F32)  26.7 us
    unnamed x190, local copies, waits for them, and re-layouts  20.8 us
    dot_general x5, matrix products, contract_rows(): return jnp.einsum('ta,tb->ab', left, right, preferred_element_type=F32)  17.3 us
    dot_general x1, matrix products, shards(): jnp.einsum('bthe,bshe->bhts', grad_mixed, value_heads, preferred_element_...  15.9 us
  transfers between devices with their start and end apart: 61, of which 26 were waited for; matrix products, arithmetic and copies ran while one was open for 42% of the time, Pallas kernels for 0%

profile of v1, /device:TPU:0, one launch (start us, length us, event | category | flops | bytes accessed | tf_op | source)
XLA Modules:
  0.0 560.0 jit_solution(10784435414536805691)
XLA Ops:
  20.8 3.0 fusion.27
  26.5 3.6 collective-permute-start.10
  31.8 2.8 collective-permute-done.10
  35.5 4.0 collective-permute-start.11
  43.1 4.0 collective-permute-done.11
  49.0 3.2 collective-permute-start.13
  52.2 36.5 %all-gather.1 = bf16[256,1408]{1,0:T(8,128)(2,1)S(1)} all-gather(bf16[64,1408]{1,0:T(8,128)(2,1)S(1)} %slice.679), channel_id=3, replica_groups=mesh['dp'=2,'hi'=4,'mid'=2,'core'=2] {'hi'}, dimensions={0}, use_global_device_ids=true | all-gather | bytes 901120 | tf_op jit(solution)/shard_map/all_gather | solution.py:48
  92.7 13.7 %collective-permute-done.14 = bf16[2,64,512]{2,1,0:T(8,128)(2,1)S(1)} collective-permute-done((bf16[2,64,512]{2,1,0:T(8,128)(2,1)S(1)}, bf16[2,64,512]{2,1,0:T(8,128)(2,1)S(1)}, u32[]{:S(2)}, u32[]{:S(2)}) %collective-permute-start.14) | collective-permute-done | bytes 131104 | tf_op jit(solution)/shard_map/ppermute | solution.py:25
  106.3 2.7 collective-permute-start.23
  113.2 2.4 fusion.102
  115.6 3.1 multiply_convert_fusion.9
  118.7 7.4 %collective-permute-done.23 = bf16[4,64,1408]{2,1,0:T(8,128)(2,1)S(1)} collective-permute-done((bf16[4,64,1408]{2,1,0:T(8,128)(2,1)S(1)}, bf16[4,64,1408]{2,1,0:T(8,128)(2,1)S(1)}, u32[]{:S(2)}, u32[]{:S(2)}) %collective-permute-start.23) | collective-permute-done | bytes 720928 | tf_op jit(solution)/shard_map/ppermute | solution.py:25
  130.5 8.1 %collective-permute-done.5 = bf16[4,64,1152]{2,1,0:T(8,128)(2,1)S(1)} collective-permute-done((bf16[4,64,1152]{2,1,0:T(8,128)(2,1)S(1)}, bf16[4,64,1152]{2,1,0:T(8,128)(2,1)S(1)}, u32[]{:S(2)}, u32[]{:S(2)}) %collective-permute-start.5) | collective-permute-done | bytes 589856 | tf_op jit(solution)/shard_map/ppermute | solution.py:25
  142.9 2.3 maximum_select_fusion.2
  150.5 2.9 fusion.15
  156.8 2.3 reduce-window.14
  168.3 8.2 %fusion.101 = f32[2,8,512,512]{3,2,1,0:T(8,128)} fusion(bf16[2,512,8,64]{1,3,2,0:T(8,128)(2,1)S(1)} %fusion.20, bf16[2,512,4,32]{1,3,2,0:T(8,128)(2,1)S(1)} %copy-done.42, bf16[2,512,4,32]{1,3,2,0:T(8,128)(2,1)S(1)} %copy-done.40), kind=kOutput, calls=%fused_computation.347 | convolution fusion | flops 541065216 | bytes 18350080 | tf_op jit(solution)/shard_map/bthd,bshd->bhts/dot_general | solution.py:276
  180.2 2.4 collective-permute-done.8
  184.0 10.2 %multiply_reduce_fusion.8 = (f32[2,512,8]{1,2,0:T(8,128)S(1)}, f32[2,512,8,64]{1,3,2,0:T(8,128)S(1)}) fusion(f32[2,8,64,512]{3,2,1,0:T(8,128)S(1)} %fusion.121, f32[2,512,8]{1,2,0:T(8,128)S(1)} %get-tuple-element.96, f32[2,8,512,512]{3,2,1,0:T(8,128)} %fusion.101, f32[2,8,512]{2,1,0:T(8,128)S(1)} %add_bitcast_fusion.3, pred[512,512]{1,0:T(8,128)(4,1)S(1)} %copy-done.55, ...), kind=kOutput, calls=%fused_computation.89 | convolution fusion | flops 560455680 | bytes 21856256 | tf_op jit(solution)/shard_map/bhts,bshe->bthe/dot_general | solution.py:278
  195.6 2.4 collective-permute-start.18
  199.7 8.5 %fusion.38 = f32[1024,1408]{1,0:T(8,128)} fusion(bf16[1024,1408]{1,0:T(8,128)(2,1)} %bitcast.402, bf16[512,1024]{1,0:T(8,128)(2,1)} %multiply_convert_fusion.9, bf16[512,1024]{1,0:T(8,128)(2,1)} %fusion.27), kind=kOutput, calls=%fused_computation.107 | convolution fusion | flops 2956984320 | bytes 10747904 | tf_op jit(solution)/shard_map/dot_general | solution.py:149
  208.2 4.1 multiply_reduce_fusion.7
  212.6 19.4 %collective-permute-done.19 = bf16[4,64,2816]{2,1,0:T(8,128)(2,1)S(1)} collective-permute-done((bf16[4,64,2816]{2,1,0:T(8,128)(2,1)}, bf16[4,64,2816]{2,1,0:T(8,128)(2,1)S(1)}, u32[]{:S(2)}, u32[]{:S(2)}) %collective-permute-start.19) | collective-permute-done | bytes 1441824 | tf_op jit(solution)/shard_map/ppermute | solution.py:25
  235.0 14.6 %collective-permute-done.20 = bf16[2,64,2816]{2,1,0:T(8,128)(2,1)S(1)} collective-permute-done((bf16[2,64,2816]{2,1,0:T(8,128)(2,1)S(1)}, bf16[2,64,2816]{2,1,0:T(8,128)(2,1)S(1)}, u32[]{:S(2)}, u32[]{:S(2)}) %collective-permute-start.20) | collective-permute-done | bytes 720928 | tf_op jit(solution)/shard_map/ppermute | solution.py:25
  252.0 6.1 %fusion.3 = f32[1024,1408]{1,0:T(8,128)} fusion(bf16[1024,2816]{1,0:T(8,128)(2,1)S(1)} %bitcast.386, bf16[512,1024]{1,0:T(8,128)(2,1)S(1)} %collective-permute-done.17, bf16[512,1024]{1,0:T(8,128)(2,1)S(1)} %multiply_convert_fusion.10), kind=kOutput, calls=%fused_computation.29 | convolution fusion | flops 2956984320 | bytes 10747904 | tf_op jit(solution)/shard_map/dot_general | solution.py:149
  258.1 11.5 %multiply_convert_fusion.3 = (bf16[1024,1408]{1,0:T(8,128)(2,1)}, bf16[1024,1408]{1,0:T(8,128)(2,1)}, bf16[1024,1408]{1,0:T(8,128)(2,1)S(1)}) fusion(f32[1024,1408]{1,0:T(8,128)} %fusion.38, f32[1024,1408]{1,0:T(8,128)} %fusion.3, bf16[1024,2816]{1,0:T(8,128)(2,1)S(1)} %bitcast.387, bf16[512,1024]{1,0:T(8,128)(2,1)S(1)} %collective-permute-done.17, ...), kind=kOutput, calls=%fused_computation.6 | convolution fusion | flops 2978611200 | bytes 25165824 | tf_op jit(solution)/shard_map/dot_general | solution.py:149
  271.1 3.8 convolution_convert_fusion
  274.9 6.3 %fusion.122 = f32[1024,1024]{1,0:T(8,128)S(1)} fusion(bf16[1024,1408]{1,0:T(8,128)(2,1)} %copy-done.86, bf16[1024,1408]{1,0:T(8,128)(2,1)S(1)} %bitcast.403), kind=kOutput, calls=%fused_computation.368 | convolution fusion | flops 2952790016 | bytes 9961472 | tf_op jit(solution)/shard_map/tb,ab->ta/dot_general | solution.py:157
  284.8 5.1 fusion.1
  289.9 3.8 convolution_convert_fusion.1
  297.8 3.8 convolution_convert_fusion.2
  304.5 6.3 %fusion.29 = f32[1024,1024]{1,0:T(8,128)S(1)} fusion(f32[1024,1024]{1,0:T(8,128)} %fusion.1, bf16[1024,1408]{1,0:T(8,128)(2,1)} %get-tuple-element.98, bf16[1024,2816]{1,0:T(8,128)(2,1)S(1)} %bitcast.389), kind=kOutput, calls=%fused_computation.91 | convolution fusion | flops 2953838592 | bytes 14155776 | tf_op jit(solution)/shard_map/tb,ab->ta/dot_general | solution.py:157
  312.9 5.7 %collective-permute-done.45 = bf16[2,64,1408]{2,1,0:T(8,128)(2,1)S(1)} collective-permute-done((bf16[2,64,1408]{2,1,0:T(8,128)(2,1)S(1)}, bf16[2,64,1408]{2,1,0:T(8,128)(2,1)S(1)}, u32[]{:S(2)}, u32[]{:S(2)}) %collective-permute-start.45) | collective-permute-done | bytes 360480 | tf_op jit(solution)/shard_map/ppermute | solution.py:25
  325.8 3.9 multiply_add_fusion
  329.7 3.2 fusion.49
  339.0 6.5 %collective-permute-done.39 = bf16[2,64,512]{2,1,0:T(8,128)(2,1)S(1)} collective-permute-done((bf16[2,64,512]{2,1,0:T(8,128)(2,1)S(1)}, bf16[2,64,512]{2,1,0:T(8,128)(2,1)S(1)}, u32[]{:S(2)}, u32[]{:S(2)}) %collective-permute-start.39) | collective-permute-done | bytes 131104 | tf_op jit(solution)/shard_map/ppermute | solution.py:25
  347.2 11.7 %collective-permute-done.41 = bf16[2,64,512]{2,1,0:T(8,128)(2,1)S(1)} collective-permute-done((bf16[2,64,512]{2,1,0:T(8,128)(2,1)S(1)}, bf16[2,64,512]{2,1,0:T(8,128)(2,1)S(1)}, u32[]{:S(2)}, u32[]{:S(2)}) %collective-permute-start.41) | collective-permute-done | bytes 131104 | tf_op jit(solution)/shard_map/ppermute | solution.py:25
  369.6 2.6 fusion.37
  372.3 4.2 fusion.51
  378.6 2.6 copy.175
  383.3 14.3 %collective-permute-done.50 = bf16[4,64,1408]{2,1,0:T(8,128)(2,1)} collective-permute-done((bf16[4,64,1408]{2,1,0:T(8,128)(2,1)}, bf16[4,64,1408]{2,1,0:T(8,128)(2,1)}, u32[]{:S(2)}, u32[]{:S(2)}) %collective-permute-start.50) | collective-permute-done | bytes 720928 | tf_op jit(solution)/shard_map/ppermute | solution.py:25
  397.7 2.7 fusion.35
  400.4 2.2 copy.176
  402.7 2.3 multiply_reduce_fusion.5
  408.2 15.9 %fusion.12 = (f32[2,8,512]{2,1,0:T(8,128)S(1)}, f32[2,8,512]{2,1,0:T(8,128)}, f32[2,8,512,512]{3,2,1,0:T(8,128)}) fusion(f32[2,8,512]{2,1,0:T(8,128)S(1)} %copy-done.67, pred[512,512]{1,0:T(8,128)(4,1)S(1)} %copy-done.56, f32[2,8,512,512]{3,2,1,0:T(8,128)} %fusion.101, bf16[2,512,8,64]{1,3,2,0:T(8,128)(2,1)S(1)} %get-tuple-element.93, ...), kind=kOutput, calls=%fused_computation.39 | convolution fusion | flops 566738944 | bytes 35487744 | tf_op jit(solution)/shard_map/bthe,bshe->bhts/dot_general | solution.py:363
  426.0 9.6 %fusion.100 = f32[2,8,64,512]{3,2,1,0:T(8,128)S(1)} fusion(f32[2,8,512,512]{3,2,1,0:T(8,128)} %get-tuple-element.195, f32[2,8,512]{2,1,0:T(8,128)S(1)} %copy-done.67, pred[512,512]{1,0:T(8,128)(4,1)S(1)} %copy-done.56, bf16[2,512,4,32]{1,3,2,0:T(8,128)(2,1)S(1)} %copy-done.43, bf16[2,512,4,32]{1,3,2,0:T(8,128)(2,1)S(1)} %copy-done.40), kind=kOutput, calls=%fused_computation.346 | convolution fusion | flops 562036736 | bytes 19693568 | tf_op jit(solution)/shard_map/bhts,bshd->bthd/dot_general | solution.py:368
  440.8 2.4 fusion.14
  443.3 3.2 fusion.9
  447.4 2.3 reduce-window.16
  450.5 10.2 %add_bitcast_fusion = f32[2,512,8,64]{1,3,2,0:T(8,128)S(1)} fusion(f32[2,8,64,512]{3,2,1,0:T(8,128)} %fusion.9, bf16[2,512,8,64]{1,3,2,0:T(8,128)(2,1)S(1)} %copy-done.6, f32[2,8,512,512]{3,2,1,0:T(8,128)} %fusion.101, f32[2,8,512]{2,1,0:T(8,128)S(1)} %copy-done.68, pred[512,512]{1,0:T(8,128)(4,1)} %iota_compare_fusion), kind=kOutput, calls=%fused_computation.76 | convolution fusion | flops 558366720 | bytes 22315008 | tf_op jit(solution)/shard_map/bhts,bthe->bshe/dot_general | solution.py:366
  462.4 9.2 %fusion.22 = f32[2,512,8,64]{1,3,2,0:T(8,128)S(1)} fusion(f32[2,8,64,512]{3,2,1,0:T(8,128)S(1)} %copy-done.83, bf16[2,512,8,64]{1,3,2,0:T(8,128)(2,1)S(1)} %fusion.20, f32[2,512,8]{1,2,0:T(8,128)S(1)} %copy-done.65, f32[2,8,512,512]{3,2,1,0:T(8,128)} %get-tuple-element.195, f32[2,8,512]{2,1,0:T(8,128)S(1)} %copy-done.69, pred[512,512]{1,0:T(8,128)(4,1)S(1)} %copy-done.57), kind=kOutput, calls=%fused_computation.65 | convolution fusion | flops 558891008 | bytes 22347776 | tf_op jit(solution)/shard_map/bhts,bthd->bshd/dot_general | solution.py:369
  475.0 4.8 multiply_reduce_fusion
  479.8 2.8 fusion.123
  482.8 2.6 copy.183
  485.9 4.1 concatenate.537
  490.3 2.7 collective-permute-start.32
  494.7 4.0 collective-permute-done.32
  503.1 2.4 convert_multiply_fusion
  505.5 2.7 slice.921
  508.2 2.7 fusion.33
  516.1 3.1 multiply_reduce_fusion.3
  519.2 13.4 %collective-permute-done.36 = bf16[2,64,1152]{2,1,0:T(8,128)(2,1)S(1)} collective-permute-done((bf16[2,64,1152]{2,1,0:T(8,128)(2,1)S(1)}, bf16[2,64,1152]{2,1,0:T(8,128)(2,1)S(1)}, u32[]{:S(2)}, u32[]{:S(2)}) %collective-permute-start.36) | collective-permute-done | bytes 294944 | tf_op jit(solution)/shard_map/ppermute | solution.py:97
  533.5 2.8 add_convert_fusion.1
  536.3 4.1 collective-permute-done.37
  (514 shorter events, 158.0 us)
Async XLA Ops:
  7.2 188.4 %all-gather.4.cloned.1.call-start = ((), (), s32[]{:S(2)}) async-start(), calls=%async_computation.8 | async-start | bytes 1802240 | tf_op jit(solution)/shard_map/all_gather | solution.py:48
  14.3 9.5 %collective-permute-start.1 = (bf16[32,5888]{1,0:T(8,128)(2,1)S(1)}, bf16[32,5888]{1,0:T(8,128)(2,1)S(1)}, u32[]{:S(2)}, u32[]{:S(2)}) collective-permute-start(bf16[32,5888]{1,0:T(8,128)(2,1)S(1)} %get-tuple-element.143), channel_id=1, source_target_pairs={{0,1},{1,0},{2,3},{3,2},{4,5},{5,4},{6,7},{7,6},{8,9},{9,8},{10,11... | collective-permute-start | bytes 1130504 | tf_op jit(solution)/shard_map/ppermute | solution.py:25
  14.8 97.3 %collective-permute-start = (bf16[512,1024]{1,0:T(8,128)(2,1)S(1)}, bf16[512,1024]{1,0:T(8,128)(2,1)S(1)}, u32[]{:S(2)}, u32[]{:S(2)}) collective-permute-start(bf16[512,1024]{1,0:T(8,128)(2,1)S(1)} %copy-done.7), channel_id=1, source_target_pairs={{0,1},{1,0},{2,3},{3,2},{4,5},{5,4},{6,7},{7,6},{8,9},{9,8},{10,11... | collective-permute-start | bytes 3145736 | tf_op jit(solution)/shard_map/ppermute | solution.py:25
  14.9 100.7 %collective-permute-start.27 = (bf16[512,1024]{1,0:T(8,128)(2,1)}, bf16[512,1024]{1,0:T(8,128)(2,1)}, u32[]{:S(2)}, u32[]{:S(2)}) collective-permute-start(bf16[512,1024]{1,0:T(8,128)(2,1)} %param.16), channel_id=1, source_target_pairs={{0,1},{1,0},{2,3},{3,2},{4,5},{5,4},{6,7},{7,6},{8,9},{9,8},{10,11... | collective-permute-start | bytes 3145736 | tf_op jit(solution)/shard_map/ppermute | solution.py:25
  17.5 147.8 %copy-start.27 = (f32[2,512,32]{1,2,0:T(8,128)}, f32[2,512,32]{1,2,0:T(8,128)S(1)}, u32[]{:S(2)}) copy-start(f32[2,512,32]{1,2,0:T(8,128)S(1)} %get-tuple-element.184) | copy-start | bytes 393220
  26.5 8.1 %collective-permute-start.10 = (bf16[64,512]{1,0:T(8,128)(2,1)}, bf16[64,512]{1,0:T(8,128)(2,1)}, u32[]{:S(2)}, u32[]{:S(2)}) collective-permute-start(bf16[64,512]{1,0:T(8,128)(2,1)} %get-tuple-element.141), channel_id=1, source_target_pairs={{0,8},{4,12},{8,0},{12,4},{1,9},{5,13},{9,1},{13,5},{2,10},{6,14},... | collective-permute-start | bytes 196616 | tf_op jit(solution)/shard_map/ppermute | solution.py:50
  31.6 10.4 %collective-permute-start.2 = (bf16[64,1152]{1,0:T(8,128)(2,1)}, bf16[64,1152]{1,0:T(8,128)(2,1)S(1)}, u32[]{:S(2)}, u32[]{:S(2)}) collective-permute-start(bf16[64,1152]{1,0:T(8,128)(2,1)} %get-tuple-element.138), channel_id=1, source_target_pairs={{0,8},{4,12},{8,0},{12,4},{1,9},{5,13},{9,1},{13,5},{2,10},{6,14},... | collective-permute-start | bytes 442376 | tf_op jit(solution)/shard_map/ppermute | solution.py:50
  31.7 508.8 %reduce-scatter.5.cloned.1.call-start = ((), (), s32[]{:S(2)}) async-start(), calls=%async_computation.4 | async-start | bytes 327680 | tf_op jit(solution)/shard_map/reduce_scatter | solution.py:105
  35.5 11.6 %collective-permute-start.11 = (bf16[2,64,512]{2,1,0:T(8,128)(2,1)S(1)}, bf16[2,64,512]{2,1,0:T(8,128)(2,1)S(1)}, u32[]{:S(2)}, u32[]{:S(2)}) collective-permute-start(bf16[2,64,512]{2,1,0:T(8,128)(2,1)S(1)} %maximum_select_fusion.25), channel_id=1, source_target_pairs={{0,4},{4,0},{8,12},{12,8},{1,5},{5,1},{9,13},{13,9},{2,6},{6,2},{1... | collective-permute-start | bytes 393224 | tf_op jit(solution)/shard_map/ppermute | solution.py:52
  43.1 47.8 %collective-permute-start.3 = (bf16[2,64,1152]{2,1,0:T(8,128)(2,1)S(1)}, bf16[2,64,1152]{2,1,0:T(8,128)(2,1)S(1)}, u32[]{:S(2)}, u32[]{:S(2)}) collective-permute-start(bf16[2,64,1152]{2,1,0:T(8,128)(2,1)S(1)} %maximum_select_fusion.17), channel_id=1, source_target_pairs={{0,4},{4,0},{8,12},{12,8},{1,5},{5,1},{9,13},{13,9},{2,6},{6,2},{1... | collective-permute-start | bytes 884744 | tf_op jit(solution)/shard_map/ppermute | solution.py:52
  47.2 43.1 %collective-permute-start.12 = (bf16[4,64,512]{2,1,0:T(8,128)(2,1)S(1)}, bf16[4,64,512]{2,1,0:T(8,128)(2,1)S(1)}, u32[]{:S(2)}, u32[]{:S(2)}) collective-permute-start(bf16[4,64,512]{2,1,0:T(8,128)(2,1)S(1)} %bitcast.429), channel_id=1, source_target_pairs={{0,2},{2,0},{1,3},{3,1},{4,6},{6,4},{5,7},{7,5},{8,10},{10,8},{9,1... | collective-permute-start | bytes 786440 | tf_op jit(solution)/shard_map/ppermute | solution.py:25
  49.0 39.7 %collective-permute-start.13 = (bf16[4,64,512]{2,1,0:T(8,128)(2,1)S(1)}, bf16[4,64,512]{2,1,0:T(8,128)(2,1)S(1)}, u32[]{:S(2)}, u32[]{:S(2)}) collective-permute-start(bf16[4,64,512]{2,1,0:T(8,128)(2,1)S(1)} %bitcast.430), channel_id=1, source_target_pairs={{0,16},{16,0},{1,17},{17,1},{2,18},{18,2},{3,19},{19,3},{4,20},{20... | collective-permute-start | bytes 786440 | tf_op jit(solution)/shard_map/ppermute | solution.py:25
  88.7 39.2 %collective-permute-start.22 = (bf16[4,64,1408]{2,1,0:T(8,128)(2,1)S(1)}, bf16[4,64,1408]{2,1,0:T(8,128)(2,1)S(1)}, u32[]{:S(2)}, u32[]{:S(2)}) collective-permute-start(bf16[4,64,1408]{2,1,0:T(8,128)(2,1)S(1)} %bitcast.404), channel_id=1, source_target_pairs={{0,2},{2,0},{1,3},{3,1},{4,6},{6,4},{5,7},{7,5},{8,10},{10,8},{9,1... | collective-permute-start | bytes 2162696 | tf_op jit(solution)/shard_map/ppermute | solution.py:25
  90.3 16.0 %collective-permute-start.14 = (bf16[2,64,512]{2,1,0:T(8,128)(2,1)S(1)}, bf16[2,64,512]{2,1,0:T(8,128)(2,1)S(1)}, u32[]{:S(2)}, u32[]{:S(2)}) collective-permute-start(bf16[2,64,512]{2,1,0:T(8,128)(2,1)S(1)} %slice.671), channel_id=1, source_target_pairs={{0,2},{2,0},{1,3},{3,1},{4,6},{6,4},{5,7},{7,5},{8,10},{10,8},{9,1... | collective-permute-start | bytes 393224 | tf_op jit(solution)/shard_map/ppermute | solution.py:25
  90.9 18.1 %collective-permute-start.15 = (bf16[2,64,512]{2,1,0:T(8,128)(2,1)S(1)}, bf16[2,64,512]{2,1,0:T(8,128)(2,1)S(1)}, u32[]{:S(2)}, u32[]{:S(2)}) collective-permute-start(bf16[2,64,512]{2,1,0:T(8,128)(2,1)S(1)} %slice.672), channel_id=1, source_target_pairs={{0,16},{16,0},{1,17},{17,1},{2,18},{18,2},{3,19},{19,3},{4,20},{20... | collective-permute-start | bytes 393224 | tf_op jit(solution)/shard_map/ppermute | solution.py:25
  106.3 19.7 %collective-permute-start.23 = (bf16[4,64,1408]{2,1,0:T(8,128)(2,1)S(1)}, bf16[4,64,1408]{2,1,0:T(8,128)(2,1)S(1)}, u32[]{:S(2)}, u32[]{:S(2)}) collective-permute-start(bf16[4,64,1408]{2,1,0:T(8,128)(2,1)S(1)} %bitcast.405), channel_id=1, source_target_pairs={{0,16},{16,0},{1,17},{17,1},{2,18},{18,2},{3,19},{19,3},{4,20},{20... | collective-permute-start | bytes 2162696 | tf_op jit(solution)/shard_map/ppermute | solution.py:25
  109.0 31.5 %collective-permute-start.4 = (bf16[4,64,1152]{2,1,0:T(8,128)(2,1)S(1)}, bf16[4,64,1152]{2,1,0:T(8,128)(2,1)S(1)}, u32[]{:S(2)}, u32[]{:S(2)}) collective-permute-start(bf16[4,64,1152]{2,1,0:T(8,128)(2,1)S(1)} %bitcast.413), channel_id=1, source_target_pairs={{0,2},{2,0},{1,3},{3,1},{4,6},{6,4},{5,7},{7,5},{8,10},{10,8},{9,1... | collective-permute-start | bytes 1769480 | tf_op jit(solution)/shard_map/ppermute | solution.py:25
  112.1 26.5 %collective-permute-start.5 = (bf16[4,64,1152]{2,1,0:T(8,128)(2,1)S(1)}, bf16[4,64,1152]{2,1,0:T(8,128)(2,1)S(1)}, u32[]{:S(2)}, u32[]{:S(2)}) collective-permute-start(bf16[4,64,1152]{2,1,0:T(8,128)(2,1)S(1)} %bitcast.414), channel_id=1, source_target_pairs={{0,16},{16,0},{1,17},{17,1},{2,18},{18,2},{3,19},{19,3},{4,20},{20... | collective-permute-start | bytes 1769480 | tf_op jit(solution)/shard_map/ppermute | solution.py:25
  112.6 36.3 %copy-start.70 = (f32[2,512]{1,0:T(2,128)}, f32[2,512]{1,0:T(2,128)S(1)}, u32[]{:S(2)}) copy-start(f32[2,512]{1,0:T(2,128)S(1)} %get-tuple-element.186) | copy-start | bytes 12292
  115.6 92.5 %collective-permute-start.16 = (bf16[1024,512]{1,0:T(8,128)(2,1)}, bf16[1024,512]{1,0:T(8,128)(2,1)}, u32[]{:S(2)}, u32[]{:S(2)}) collective-permute-start(bf16[1024,512]{1,0:T(8,128)(2,1)} %bitcast.49), channel_id=1, source_target_pairs={{0,1},{1,0},{2,3},{3,2},{4,5},{5,4},{6,7},{7,6},{8,9},{9,8},{10,11... | collective-permute-start | bytes 3145736 | tf_op jit(solution)/shard_map/ppermute | solution.py:25
  126.1 16.5 %collective-permute-start.24 = (bf16[2,64,1408]{2,1,0:T(8,128)(2,1)S(1)}, bf16[2,64,1408]{2,1,0:T(8,128)(2,1)S(1)}, u32[]{:S(2)}, u32[]{:S(2)}) collective-permute-start(bf16[2,64,1408]{2,1,0:T(8,128)(2,1)S(1)} %slice.680), channel_id=1, source_target_pairs={{0,2},{2,0},{1,3},{3,1},{4,6},{6,4},{5,7},{7,5},{8,10},{10,8},{9,1... | collective-permute-start | bytes 1081352 | tf_op jit(solution)/shard_map/ppermute | solution.py:25
  128.0 14.7 %collective-permute-start.25 = (bf16[2,64,1408]{2,1,0:T(8,128)(2,1)S(1)}, bf16[2,64,1408]{2,1,0:T(8,128)(2,1)S(1)}, u32[]{:S(2)}, u32[]{:S(2)}) collective-permute-start(bf16[2,64,1408]{2,1,0:T(8,128)(2,1)S(1)} %slice.681), channel_id=1, source_target_pairs={{0,16},{16,0},{1,17},{17,1},{2,18},{18,2},{3,19},{19,3},{4,20},{20... | collective-permute-start | bytes 1081352 | tf_op jit(solution)/shard_map/ppermute | solution.py:25
  138.6 6.8 %collective-permute-start.6 = (bf16[2,64,1152]{2,1,0:T(8,128)(2,1)S(1)}, bf16[2,64,1152]{2,1,0:T(8,128)(2,1)S(1)}, u32[]{:S(2)}, u32[]{:S(2)}) collective-permute-start(bf16[2,64,1152]{2,1,0:T(8,128)(2,1)S(1)} %slice.651), channel_id=1, source_target_pairs={{0,2},{2,0},{1,3},{3,1},{4,6},{6,4},{5,7},{7,5},{8,10},{10,8},{9,1... | collective-permute-start | bytes 884744 | tf_op jit(solution)/shard_map/ppermute | solution.py:25
  140.6 6.8 %collective-permute-start.7 = (bf16[2,64,1152]{2,1,0:T(8,128)(2,1)S(1)}, bf16[2,64,1152]{2,1,0:T(8,128)(2,1)S(1)}, u32[]{:S(2)}, u32[]{:S(2)}) collective-permute-start(bf16[2,64,1152]{2,1,0:T(8,128)(2,1)S(1)} %slice.652), channel_id=1, source_target_pairs={{0,16},{16,0},{1,17},{17,1},{2,18},{18,2},{3,19},{19,3},{4,20},{20... | collective-permute-start | bytes 884744 | tf_op jit(solution)/shard_map/ppermute | solution.py:25
  178.0 4.6 collective-permute-start.8
  195.6 12.6 %collective-permute-start.9 = (bf16[512,512]{0,1:T(8,128)(2,1)}, bf16[512,512]{0,1:T(8,128)(2,1)}, u32[]{:S(2)}, u32[]{:S(2)}) collective-permute-start(bf16[512,512]{0,1:T(8,128)(2,1)} %bitcast.37), channel_id=1, source_target_pairs={{0,1},{1,0},{2,3},{3,2},{4,5},{5,4},{6,7},{7,6},{8,9},{9,8},{10,11... | collective-permute-start | bytes 1572872 | tf_op jit(solution)/shard_map/ppermute | solution.py:25
  195.6 36.8 %collective-permute-start.18 = (bf16[4,64,2816]{2,1,0:T(8,128)(2,1)}, bf16[4,64,2816]{2,1,0:T(8,128)(2,1)S(1)}, u32[]{:S(2)}, u32[]{:S(2)}) collective-permute-start(bf16[4,64,2816]{2,1,0:T(8,128)(2,1)} %bitcast.424), channel_id=1, source_target_pairs={{0,2},{2,0},{1,3},{3,1},{4,6},{6,4},{5,7},{7,5},{8,10},{10,8},{9,1... | collective-permute-start | bytes 4325384 | tf_op jit(solution)/shard_map/ppermute | solution.py:25
  198.1 33.9 %collective-permute-start.19 = (bf16[4,64,2816]{2,1,0:T(8,128)(2,1)}, bf16[4,64,2816]{2,1,0:T(8,128)(2,1)S(1)}, u32[]{:S(2)}, u32[]{:S(2)}) collective-permute-start(bf16[4,64,2816]{2,1,0:T(8,128)(2,1)} %bitcast.425), channel_id=1, source_target_pairs={{0,16},{16,0},{1,17},{17,1},{2,18},{18,2},{3,19},{19,3},{4,20},{20... | collective-permute-start | bytes 4325384 | tf_op jit(solution)/shard_map/ppermute | solution.py:25
  212.5 39.4 %collective-permute-start.17 = (bf16[512,1024]{1,0:T(8,128)(2,1)S(1)}, bf16[512,1024]{1,0:T(8,128)(2,1)S(1)}, u32[]{:S(2)}, u32[]{:S(2)}) collective-permute-start(bf16[512,1024]{1,0:T(8,128)(2,1)S(1)} %multiply_convert_fusion.10), channel_id=1, source_target_pairs={{0,1},{1,0},{2,3},{3,2},{4,5},{5,4},{6,7},{7,6},{8,9},{9,8},{10,11... | collective-permute-start | bytes 3145736 | tf_op jit(solution)/shard_map/ppermute | solution.py:25
  232.0 17.5 %collective-permute-start.20 = (bf16[2,64,2816]{2,1,0:T(8,128)(2,1)S(1)}, bf16[2,64,2816]{2,1,0:T(8,128)(2,1)S(1)}, u32[]{:S(2)}, u32[]{:S(2)}) collective-permute-start(bf16[2,64,2816]{2,1,0:T(8,128)(2,1)S(1)} %slice.675), channel_id=1, source_target_pairs={{0,2},{2,0},{1,3},{3,1},{4,6},{6,4},{5,7},{7,5},{8,10},{10,8},{9,1... | collective-permute-start | bytes 2162696 | tf_op jit(solution)/shard_map/ppermute | solution.py:25
  232.4 17.5 %collective-permute-start.21 = (bf16[2,64,2816]{2,1,0:T(8,128)(2,1)S(1)}, bf16[2,64,2816]{2,1,0:T(8,128)(2,1)S(1)}, u32[]{:S(2)}, u32[]{:S(2)}) collective-permute-start(bf16[2,64,2816]{2,1,0:T(8,128)(2,1)S(1)} %slice.676), channel_id=1, source_target_pairs={{0,16},{16,0},{1,17},{17,1},{2,18},{18,2},{3,19},{19,3},{4,20},{20... | collective-permute-start | bytes 2162696 | tf_op jit(solution)/shard_map/ppermute | solution.py:25
  252.0 37.9 %copy-start.79 = (bf16[512,1024]{1,0:T(8,128)(2,1)}, bf16[512,1024]{1,0:T(8,128)(2,1)S(1)}, u32[]{:S(2)}) copy-start(bf16[512,1024]{1,0:T(8,128)(2,1)S(1)} %collective-permute-done.17) | copy-start | bytes 3145732
  281.5 29.5 %collective-permute-start.51 = (bf16[2,64,1408]{2,1,0:T(8,128)(2,1)S(1)}, bf16[2,64,1408]{2,1,0:T(8,128)(2,1)S(1)}, u32[]{:S(2)}, u32[]{:S(2)}) collective-permute-start(bf16[2,64,1408]{2,1,0:T(8,128)(2,1)S(1)} %get-tuple-element.144), channel_id=1, source_target_pairs={{0,2},{2,0},{1,3},{3,1},{4,6},{6,4},{5,7},{7,5},{8,10},{10,8},{9,1... | collective-permute-start | bytes 1081352 | tf_op jit(solution)/shard_map/ppermute | solution.py:25
  283.1 38.4 %collective-permute-start.53 = (bf16[2,64,1408]{2,1,0:T(8,128)(2,1)S(1)}, bf16[2,64,1408]{2,1,0:T(8,128)(2,1)S(1)}, u32[]{:S(2)}, u32[]{:S(2)}) collective-permute-start(bf16[2,64,1408]{2,1,0:T(8,128)(2,1)S(1)} %get-tuple-element.145), channel_id=1, source_target_pairs={{0,16},{16,0},{1,17},{17,1},{2,18},{18,2},{3,19},{19,3},{4,20},{20... | collective-permute-start | bytes 1081352 | tf_op jit(solution)/shard_map/ppermute | solution.py:25
  296.2 36.9 %collective-permute-start.47 = (bf16[2,64,1408]{2,1,0:T(8,128)(2,1)}, bf16[2,64,1408]{2,1,0:T(8,128)(2,1)S(1)}, u32[]{:S(2)}, u32[]{:S(2)}) collective-permute-start(bf16[2,64,1408]{2,1,0:T(8,128)(2,1)} %get-tuple-element.146), channel_id=1, source_target_pairs={{0,2},{2,0},{1,3},{3,1},{4,6},{6,4},{5,7},{7,5},{8,10},{10,8},{9,1... | collective-permute-start | bytes 1081352 | tf_op jit(solution)/shard_map/ppermute | solution.py:25
  296.7 37.4 %collective-permute-start.49 = (bf16[2,64,1408]{2,1,0:T(8,128)(2,1)}, bf16[2,64,1408]{2,1,0:T(8,128)(2,1)S(1)}, u32[]{:S(2)}, u32[]{:S(2)}) collective-permute-start(bf16[2,64,1408]{2,1,0:T(8,128)(2,1)} %get-tuple-element.147), channel_id=1, source_target_pairs={{0,16},{16,0},{1,17},{17,1},{2,18},{18,2},{3,19},{19,3},{4,20},{20... | collective-permute-start | bytes 1081352 | tf_op jit(solution)/shard_map/ppermute | solution.py:25
  303.3 9.5 %collective-permute-start.43 = (bf16[2,64,1408]{2,1,0:T(8,128)(2,1)S(1)}, bf16[2,64,1408]{2,1,0:T(8,128)(2,1)S(1)}, u32[]{:S(2)}, u32[]{:S(2)}) collective-permute-start(bf16[2,64,1408]{2,1,0:T(8,128)(2,1)S(1)} %get-tuple-element.148), channel_id=1, source_target_pairs={{0,2},{2,0},{1,3},{3,1},{4,6},{6,4},{5,7},{7,5},{8,10},{10,8},{9,1... | collective-permute-start | bytes 1081352 | tf_op jit(solution)/shard_map/ppermute | solution.py:25
  311.0 7.6 %collective-permute-start.45 = (bf16[2,64,1408]{2,1,0:T(8,128)(2,1)S(1)}, bf16[2,64,1408]{2,1,0:T(8,128)(2,1)S(1)}, u32[]{:S(2)}, u32[]{:S(2)}) collective-permute-start(bf16[2,64,1408]{2,1,0:T(8,128)(2,1)S(1)} %get-tuple-element.149), channel_id=1, source_target_pairs={{0,16},{16,0},{1,17},{17,1},{2,18},{18,2},{3,19},{19,3},{4,20},{20... | collective-permute-start | bytes 1081352 | tf_op jit(solution)/shard_map/ppermute | solution.py:25
  312.8 11.7 %collective-permute-start.26 = (bf16[512,1024]{1,0:T(8,128)(2,1)S(1)}, bf16[512,1024]{1,0:T(8,128)(2,1)S(1)}, u32[]{:S(2)}, u32[]{:S(2)}) collective-permute-start(bf16[512,1024]{1,0:T(8,128)(2,1)S(1)} %slice.923), channel_id=1, source_target_pairs={{0,1},{1,0},{2,3},{3,2},{4,5},{5,4},{6,7},{7,6},{8,9},{9,8},{10,11... | collective-permute-start | bytes 3145736 | tf_op jit(solution)/shard_map/ppermute | solution.py:25
  318.6 4.4 collective-permute-start.28
  321.5 186.7 %collective-permute-start.52 = (bf16[4,64,1408]{2,1,0:T(8,128)(2,1)}, bf16[4,64,1408]{2,1,0:T(8,128)(2,1)}, u32[]{:S(2)}, u32[]{:S(2)}) collective-permute-start(bf16[4,64,1408]{2,1,0:T(8,128)(2,1)} %pad_maximum_fusion.15), channel_id=1, source_target_pairs={{0,16},{16,0},{1,17},{17,1},{2,18},{18,2},{3,19},{19,3},{4,20},{20... | collective-permute-start | bytes 2162696 | tf_op jit(solution)/shard_map/ppermute | solution.py:25
  323.1 45.9 %collective-permute-start.44 = (bf16[4,64,1408]{2,1,0:T(8,128)(2,1)}, bf16[4,64,1408]{2,1,0:T(8,128)(2,1)}, u32[]{:S(2)}, u32[]{:S(2)}) collective-permute-start(bf16[4,64,1408]{2,1,0:T(8,128)(2,1)} %pad_maximum_fusion.11), channel_id=1, source_target_pairs={{0,16},{16,0},{1,17},{17,1},{2,18},{18,2},{3,19},{19,3},{4,20},{20... | collective-permute-start | bytes 2162696 | tf_op jit(solution)/shard_map/ppermute | solution.py:25
  324.4 45.1 %collective-permute-start.46 = (bf16[4,64,1408]{2,1,0:T(8,128)(2,1)}, bf16[4,64,1408]{2,1,0:T(8,128)(2,1)}, u32[]{:S(2)}, u32[]{:S(2)}) collective-permute-start(bf16[4,64,1408]{2,1,0:T(8,128)(2,1)} %pad_maximum_fusion.12), channel_id=1, source_target_pairs={{0,2},{2,0},{1,3},{3,1},{4,6},{6,4},{5,7},{7,5},{8,10},{10,8},{9,1... | collective-permute-start | bytes 2162696 | tf_op jit(solution)/shard_map/ppermute | solution.py:25
  333.1 2.7 collective-permute-start.38
  336.6 8.9 %collective-permute-start.39 = (bf16[2,64,512]{2,1,0:T(8,128)(2,1)S(1)}, bf16[2,64,512]{2,1,0:T(8,128)(2,1)S(1)}, u32[]{:S(2)}, u32[]{:S(2)}) collective-permute-start(bf16[2,64,512]{2,1,0:T(8,128)(2,1)S(1)} %get-tuple-element.166), channel_id=1, source_target_pairs={{0,2},{2,0},{1,3},{3,1},{4,6},{6,4},{5,7},{7,5},{8,10},{10,8},{9,1... | collective-permute-start | bytes 393224 | tf_op jit(solution)/shard_map/ppermute | solution.py:25
  337.4 21.5 %collective-permute-start.41 = (bf16[2,64,512]{2,1,0:T(8,128)(2,1)S(1)}, bf16[2,64,512]{2,1,0:T(8,128)(2,1)S(1)}, u32[]{:S(2)}, u32[]{:S(2)}) collective-permute-start(bf16[2,64,512]{2,1,0:T(8,128)(2,1)S(1)} %get-tuple-element.167), channel_id=1, source_target_pairs={{0,16},{16,0},{1,17},{17,1},{2,18},{18,2},{3,19},{19,3},{4,20},{20... | collective-permute-start | bytes 393224 | tf_op jit(solution)/shard_map/ppermute | solution.py:25
  345.6 18.6 %collective-permute-start.40 = (bf16[4,64,512]{2,1,0:T(8,128)(2,1)S(1)}, bf16[4,64,512]{2,1,0:T(8,128)(2,1)S(1)}, u32[]{:S(2)}, u32[]{:S(2)}) collective-permute-start(bf16[4,64,512]{2,1,0:T(8,128)(2,1)S(1)} %pad_maximum_fusion.26), channel_id=1, source_target_pairs={{0,16},{16,0},{1,17},{17,1},{2,18},{18,2},{3,19},{19,3},{4,20},{20... | collective-permute-start | bytes 786440 | tf_op jit(solution)/shard_map/ppermute | solution.py:25
  358.9 7.6 %collective-permute-start.42 = (bf16[4,64,512]{2,1,0:T(8,128)(2,1)S(1)}, bf16[4,64,512]{2,1,0:T(8,128)(2,1)S(1)}, u32[]{:S(2)}, u32[]{:S(2)}) collective-permute-start(bf16[4,64,512]{2,1,0:T(8,128)(2,1)S(1)} %pad_maximum_fusion.27), channel_id=1, source_target_pairs={{0,2},{2,0},{1,3},{3,1},{4,6},{6,4},{5,7},{7,5},{8,10},{10,8},{9,1... | collective-permute-start | bytes 786440 | tf_op jit(solution)/shard_map/ppermute | solution.py:25
  364.1 144.1 %collective-permute-start.54 = (bf16[4,64,1408]{2,1,0:T(8,128)(2,1)}, bf16[4,64,1408]{2,1,0:T(8,128)(2,1)}, u32[]{:S(2)}, u32[]{:S(2)}) collective-permute-start(bf16[4,64,1408]{2,1,0:T(8,128)(2,1)} %pad_maximum_fusion.16), channel_id=1, source_target_pairs={{0,2},{2,0},{1,3},{3,1},{4,6},{6,4},{5,7},{7,5},{8,10},{10,8},{9,1... | collective-permute-start | bytes 2162696 | tf_op jit(solution)/shard_map/ppermute | solution.py:25
  366.6 16.8 %collective-permute-start.48 = (bf16[4,64,1408]{2,1,0:T(8,128)(2,1)}, bf16[4,64,1408]{2,1,0:T(8,128)(2,1)}, u32[]{:S(2)}, u32[]{:S(2)}) collective-permute-start(bf16[4,64,1408]{2,1,0:T(8,128)(2,1)} %pad_maximum_fusion.13), channel_id=1, source_target_pairs={{0,16},{16,0},{1,17},{17,1},{2,18},{18,2},{3,19},{19,3},{4,20},{20... | collective-permute-start | bytes 2162696 | tf_op jit(solution)/shard_map/ppermute | solution.py:25
  368.9 172.4 %reduce-scatter.7.cloned.1.call-start = ((), (), s32[]{:S(2)}) async-start(), calls=%async_computation.5 | async-start | bytes 901120 | tf_op jit(solution)/shard_map/reduce_scatter | solution.py:105
  369.0 28.7 %collective-permute-start.50 = (bf16[4,64,1408]{2,1,0:T(8,128)(2,1)}, bf16[4,64,1408]{2,1,0:T(8,128)(2,1)}, u32[]{:S(2)}, u32[]{:S(2)}) collective-permute-start(bf16[4,64,1408]{2,1,0:T(8,128)(2,1)} %pad_maximum_fusion.14), channel_id=1, source_target_pairs={{0,2},{2,0},{1,3},{3,1},{4,6},{6,4},{5,7},{7,5},{8,10},{10,8},{9,1... | collective-permute-start | bytes 2162696 | tf_op jit(solution)/shard_map/ppermute | solution.py:25
  372.2 170.1 %reduce-scatter.9.cloned.1.call-start = ((), (), s32[]{:S(2)}) async-start(), calls=%async_computation.6 | async-start | bytes 901120 | tf_op jit(solution)/shard_map/reduce_scatter | solution.py:105
  377.4 23.1 %collective-permute-start.29 = (bf16[512,512]{1,0:T(8,128)(2,1)}, bf16[512,512]{1,0:T(8,128)(2,1)}, u32[]{:S(2)}, u32[]{:S(2)}) collective-permute-start(bf16[512,512]{1,0:T(8,128)(2,1)} %select_convert_fusion.1), channel_id=1, source_target_pairs={{0,1},{1,0},{2,3},{3,2},{4,5},{5,4},{6,7},{7,6},{8,9},{9,8},{10,11... | collective-permute-start | bytes 1572872 | tf_op jit(solution)/shard_map/ppermute | solution.py:25
  400.4 142.9 %reduce-scatter.11.cloned.1.call-start = ((), (), s32[]{:S(2)}) async-start(), calls=%async_computation.7 | async-start | bytes 901120 | tf_op jit(solution)/shard_map/reduce_scatter | solution.py:105
  424.3 15.5 %collective-permute-start.30 = (bf16[8,64,64]{2,1,0:T(8,128)(2,1)S(1)}, bf16[8,64,64]{2,1,0:T(8,128)(2,1)S(1)}, u32[]{:S(2)}, u32[]{:S(2)}) collective-permute-start(bf16[8,64,64]{2,1,0:T(8,128)(2,1)S(1)} %fusion.68), channel_id=1, source_target_pairs={{2,0},{3,1},{6,4},{7,5},{10,8},{11,9},{14,12},{15,13},{18,16},{19,... | collective-permute-start | bytes 196616 | tf_op jit(solution)/shard_map/ppermute | solution.py:360
  490.3 8.4 %collective-permute-start.32 = (bf16[2,64,1152]{2,1,0:T(8,128)(2,1)S(1)}, bf16[2,64,1152]{2,1,0:T(8,128)(2,1)S(1)}, u32[]{:S(2)}, u32[]{:S(2)}) collective-permute-start(bf16[2,64,1152]{2,1,0:T(8,128)(2,1)S(1)} %get-tuple-element.150), channel_id=1, source_target_pairs={{0,2},{2,0},{1,3},{3,1},{4,6},{6,4},{5,7},{7,5},{8,10},{10,8},{9,1... | collective-permute-start | bytes 884744 | tf_op jit(solution)/shard_map/ppermute | solution.py:25
  493.0 8.2 %collective-permute-start.34 = (bf16[2,64,1152]{2,1,0:T(8,128)(2,1)S(1)}, bf16[2,64,1152]{2,1,0:T(8,128)(2,1)S(1)}, u32[]{:S(2)}, u32[]{:S(2)}) collective-permute-start(bf16[2,64,1152]{2,1,0:T(8,128)(2,1)S(1)} %get-tuple-element.151), channel_id=1, source_target_pairs={{0,16},{16,0},{1,17},{17,1},{2,18},{18,2},{3,19},{19,3},{4,20},{20... | collective-permute-start | bytes 884744 | tf_op jit(solution)/shard_map/ppermute | solution.py:25
  499.7 13.5 %collective-permute-start.33 = (bf16[4,64,1152]{2,1,0:T(8,128)(2,1)}, bf16[4,64,1152]{2,1,0:T(8,128)(2,1)}, u32[]{:S(2)}, u32[]{:S(2)}) collective-permute-start(bf16[4,64,1152]{2,1,0:T(8,128)(2,1)} %pad_maximum_fusion.21), channel_id=1, source_target_pairs={{0,16},{16,0},{1,17},{17,1},{2,18},{18,2},{3,19},{19,3},{4,20},{20... | collective-permute-start | bytes 1769480 | tf_op jit(solution)/shard_map/ppermute | solution.py:25
  501.3 13.0 %collective-permute-start.35 = (bf16[4,64,1152]{2,1,0:T(8,128)(2,1)S(1)}, bf16[4,64,1152]{2,1,0:T(8,128)(2,1)}, u32[]{:S(2)}, u32[]{:S(2)}) collective-permute-start(bf16[4,64,1152]{2,1,0:T(8,128)(2,1)S(1)} %pad_maximum_fusion.22), channel_id=1, source_target_pairs={{0,2},{2,0},{1,3},{3,1},{4,6},{6,4},{5,7},{7,5},{8,10},{10,8},{9,1... | collective-permute-start | bytes 1769480 | tf_op jit(solution)/shard_map/ppermute | solution.py:25
  508.2 7.9 %collective-permute-start.31 = (bf16[512,1024]{1,0:T(8,128)(2,1)}, bf16[512,1024]{1,0:T(8,128)(2,1)}, u32[]{:S(2)}, u32[]{:S(2)}) collective-permute-start(bf16[512,1024]{1,0:T(8,128)(2,1)} %slice.921), channel_id=1, source_target_pairs={{0,1},{1,0},{2,3},{3,2},{4,5},{5,4},{6,7},{7,6},{8,9},{9,8},{10,11... | collective-permute-start | bytes 3145736 | tf_op jit(solution)/shard_map/ppermute | solution.py:25
  516.0 16.7 %collective-permute-start.36 = (bf16[2,64,1152]{2,1,0:T(8,128)(2,1)S(1)}, bf16[2,64,1152]{2,1,0:T(8,128)(2,1)S(1)}, u32[]{:S(2)}, u32[]{:S(2)}) collective-permute-start(bf16[2,64,1152]{2,1,0:T(8,128)(2,1)S(1)} %fusion.59), channel_id=1, source_target_pairs={{0,4},{4,0},{8,12},{12,8},{1,5},{5,1},{9,13},{13,9},{2,6},{6,2},{1... | collective-permute-start | bytes 884744 | tf_op jit(solution)/shard_map/ppermute | solution.py:97
  532.7 7.7 %collective-permute-start.37 = (bf16[64,1152]{1,0:T(8,128)(2,1)S(1)}, bf16[64,1152]{1,0:T(8,128)(2,1)S(1)}, u32[]{:S(2)}, u32[]{:S(2)}) collective-permute-start(bf16[64,1152]{1,0:T(8,128)(2,1)S(1)} %fusion.73), channel_id=1, source_target_pairs={{0,8},{4,12},{8,0},{12,4},{1,9},{5,13},{9,1},{13,5},{2,10},{6,14},... | collective-permute-start | bytes 442376 | tf_op jit(solution)/shard_map/ppermute | solution.py:102
  544.4 1.7 collective-permute-start.55
  (85 other events, 433.7 us)
Sparse Core Ops, SparseCore 0:
  31.8 50.4 all-gather.3
  369.0 18.0 reduce-scatter.4
  389.5 20.9 reduce-scatter.6
  412.7 21.9 reduce-scatter.8
  511.0 25.3 reduce-scatter.10

commit v2 on v1

v2 whole, which is shorter than its diff:
```python
import functools

import jax
import jax.numpy as jnp
from jax import lax
from jax.experimental import pallas as pl
from jax.experimental.pallas import tpu as pltpu
from jax.sharding import Mesh, PartitionSpec as P

HEADS = 16
HEAD = 64
KVH = 2
LATENT = 256
SPAN = 4

epsilon = 1e-05
head_floor = 0.25
ROPE_BASE = 10000.0
GATE_TEMP = 16.0

CHIPS = ("dp", "hi", "mid")
ALL = ("dp", "hi", "mid", "core")
F32 = jnp.float32
BF16 = jnp.bfloat16


def swap(v, axis):
    return lax.ppermute(v, axis, [(0, 1), (1, 0)])


def place(bit, mine, theirs):
    return jnp.where(
        bit == 0, jnp.concatenate([mine, theirs], 0), jnp.concatenate([theirs, mine], 0)
    )


def small_slice():
    return lax.axis_size("dp") == 2 and lax.axis_size("hi") == 4


def gather(part):
    return lax.all_gather(part, CHIPS, axis=0, tiled=True)


def add3(a, b, c):
    return a.astype(F32) + b.astype(F32) + c.astype(F32)


def scatter(whole):
    return lax.psum_scatter(whole, CHIPS, scatter_dimension=0, tiled=True)


def beside(core, mine, theirs):
    return jnp.where(
        core == 0, jnp.concatenate([mine, theirs], 1), jnp.concatenate([theirs, mine], 1)
    ).astype(F32)


HALF = HEADS // 2
PAIRS = HALF // 2
WIDE = 2 * HEAD
N_Q = HALF * HEAD
N_K = N_Q // 2
N_FRONT = N_Q + 2 * N_K + WIDE
FLOPS = 0.55e9


def dot(left, right):
    return jnp.dot(left, right, preferred_element_type=F32)


def dot_t(left, right):
    return lax.dot_general(left, right, (((1,), (1,)), ((), ())), preferred_element_type=F32)


def t_dot(left, right):
    return lax.dot_general(left, right, (((0,), (0,)), ((), ())), preferred_element_type=F32)


def thirds(v):
    high = v.astype(BF16)
    rest = v - high.astype(F32)
    middle = rest.astype(BF16)
    return high, middle, (rest - middle.astype(F32)).astype(BF16)


def iota(shape, axis):
    return lax.broadcasted_iota(jnp.int32, shape, axis)


def spread_pair(per_head, p):
    lane = iota((1, WIDE), 1)
    return jnp.where(
        lane < HEAD, per_head[:, 2 * p : 2 * p + 1], per_head[:, 2 * p + 1 : 2 * p + 2]
    )


def head_sums(v):
    lane = iota((1, WIDE), 1)
    low = jnp.sum(jnp.where(lane < HEAD, v, 0.0), axis=1, keepdims=True)
    high = jnp.sum(jnp.where(lane < HEAD, 0.0, v), axis=1, keepdims=True)
    return jnp.where(lane < HEAD, low, high)


def turn(v, cosine, sine_part):
    lane = iota((1, WIDE), 1)
    other = jnp.where(
        lane % HEAD < HEAD // 2,
        pltpu.roll(v, WIDE - HEAD // 2, 1),
        pltpu.roll(v, HEAD // 2, 1),
    )
    return v * cosine + other * sine_part


def own_blocks():
    return (iota((WIDE, WIDE), 0) < HEAD) == (iota((WIDE, WIDE), 1) < HEAD)


def q_cols(p):
    return slice(WIDE * p, WIDE * (p + 1))


def k_cols(p):
    return slice(N_Q + WIDE * (p % 2), N_Q + WIDE * (p % 2 + 1))


def v_cols(p):
    return slice(N_Q + N_K + WIDE * (p % 2), N_Q + N_K + WIDE * (p % 2 + 1))


def without(kernel, start, count):
    return lambda *refs: kernel(*refs[:start], *refs[start + count :])


ANYWHERE = pl.BlockSpec(memory_space=pl.ANY)
SCALARS = pl.BlockSpec(memory_space=pltpu.SMEM)


def inverse_rms(values, added=epsilon):
    return lax.rsqrt(jnp.mean(values * values, axis=-1, keepdims=True) + added)


def norm_back(grad_unit, unit_rows, scale_rows):
    return scale_rows * (
        grad_unit - unit_rows * jnp.mean(grad_unit * unit_rows, axis=-1, keepdims=True)
    )


def row_of(where, i, b, rows):
    hi = where[2] ^ (0, 2, 1, 3)[i]
    index = ((where[1] ^ b[0]) * 4 + hi) * 2 + (where[3] ^ b[1])
    return pl.multiple_of(index * rows, rows)


def pack_kernel(core_ref, q_ref, k_ref, v_ref, a_ref, g1_ref, g2_ref, o_ref, f_ref, u_ref, d_ref, *outs):
    def put(out, at, v):
        out[:, at : at + v.shape[1]] = v
        return at + v.shape[1]

    rows = q_ref.shape[0]
    lane = iota((1, WIDE), 1)
    gates = a_ref[...].astype(F32)
    gains = [g1_ref[...].astype(F32), g2_ref[...].astype(F32)]
    for i in range(2):
        front, rest = outs[2 * i : 2 * i + 2]
        mine = core_ref[0] if i == 0 else 1 - core_ref[0]

        def half(ref):
            n = ref.shape[1] // 2
            return jnp.where(mine == 0, ref[:, :n], ref[:, n:])

        at = put(front, 0, half(q_ref))
        at = put(front, at, half(k_ref))
        at = put(front, at, half(v_ref))
        some = jnp.where(mine == 0, gates[:HALF], gates[HALF:])
        small = jnp.concatenate([some, *gains, jnp.zeros((WIDE - HALF - 2, rows), F32)], 0)
        at = put(front, at, small.T.astype(BF16))
        put(front, at, half(o_ref))
        at = put(rest, 0, half(f_ref))
        at = put(rest, at, half(u_ref))
        put(rest, at, half(d_ref))


def pack(core, *weights):
    rows = weights[0].shape[0]
    n_out, n_ff = weights[6].shape[1] // 2, weights[7].shape[1] // 2
    return pl.pallas_call(
        pack_kernel,
        in_specs=[pl.BlockSpec(memory_space=pltpu.SMEM)]
        + [pl.BlockSpec(memory_space=pltpu.VMEM)] * len(weights),
        out_specs=[pl.BlockSpec(memory_space=pltpu.VMEM)] * 4,
        out_shape=[
            jax.ShapeDtypeStruct((rows, n), BF16) for n in (N_FRONT + n_out, 3 * n_ff)
        ]
        * 2,
        name="pack",
    )(core.reshape(1).astype(jnp.int32), *weights)


def front_kernel(
    core_ref, own_ref, other_ref, bias_ref, cos_ref, sin_ref, *refs
):
    *pieces, w_ref, out_ref = refs[:-9]
    normed_ref, qkv_ref, c_ref, ct_ref, z_ref, gains_ref, u_ref, leave_ref, first_u = refs[-9:]
    step = pl.program_id(0)
    slot = step ^ core_ref[0]

    @pl.when(step == 0)
    def _():
        if len(pieces) == 1:
            w_ref[...] = pieces[0][:, :N_FRONT]
            out_ref[...] = pieces[0][:, N_FRONT:]
        else:
            own, over_dp, over_mid, first, second = pieces
            rows = own.shape[1]
            for i in range(4):
                far = first[i] if i < 2 else second[i - 2]
                for v, b in ((own[i], (0, 0)), (over_dp[i], (1, 0)), (over_mid[i], (0, 1)), (far, (1, 1))):
                    to = pl.ds(row_of(core_ref, i, b, rows), rows)
                    w_ref[to, :] = v[:, :N_FRONT]
                    out_ref[to, :] = v[:, N_FRONT:]

    x = jnp.where(slot == 0, own_ref[...], other_ref[...]).astype(F32)
    gains = w_ref[:, N_FRONT - WIDE :].astype(F32).T[HALF : HALF + 8]
    gains_ref[...] = gains
    scale = lax.rsqrt(jnp.mean(x * x, axis=-1, keepdims=True) + epsilon)
    normed = (x * scale * gains[:1]).astype(BF16)
    normed_ref[...] = normed
    pre = dot(normed, w_ref[...])
    cosine, sine_part = cos_ref[...], sin_ref[...]
    for p in range(PAIRS):
        turned = turn(pre[:, q_cols(p)], cosine, sine_part)
        qkv_ref[:, q_cols(p)] = (turned * float(HEAD) ** (-0.5)).astype(BF16)
    for p in range(PAIRS // 2):
        qkv_ref[:, k_cols(p)] = turn(pre[:, k_cols(p)], cosine, sine_part).astype(BF16)
        qkv_ref[:, v_cols(p)] = pre[:, v_cols(p)].astype(BF16)
    z = pre[:, N_FRONT - WIDE :] + bias_ref[...]
    z_ref[...] = z
    small = jnp.exp(-jnp.abs(z))
    log_part = jnp.where(
        small < 0.01, small * (1.0 - small * (0.5 - small * (1.0 / 3.0))), jnp.log(1.0 + small)
    )
    softplus = jnp.maximum(z, 0.0) + log_part
    log_decay = jnp.where(iota((1, WIDE), 1) < HALF, -softplus / GATE_TEMP, 0.0)
    count = x.shape[0]
    lower = (iota((count, count), 0) >= iota((count, count), 1)).astype(BF16)
    c = sum(dot(lower, third) for third in thirds(log_decay))
    c_ref[...] = c
    ct_ref[...] = c.T[:HALF]
    last = c[count - 1 :]
    tail = jnp.exp(last - c)
    mask = own_blocks()
    for p in range(PAIRS):
        scaled = (qkv_ref[:, k_cols(p)].astype(F32) * spread_pair(tail, p)).astype(BF16)
        update = jnp.where(mask, t_dot(scaled, qkv_ref[:, v_cols(p)]), 0.0)

        @pl.when(step == 0)
        def _():
            u_ref[p] = update
            first_u[p] = update

        @pl.when(step == 1)
        def _():
            grown = spread_pair(jnp.exp(last), p) * first_u[p] + update
            leave_ref[p] = grown.astype(BF16)


def tile_of(qkv_ref, c, ct, r, rows, p, h):
    lane = iota((1, WIDE), 1)
    mine = (lane < HEAD) if h == 0 else (lane >= HEAD)
    span = slice(rows * r, rows * (r + 1))
    upto = rows * (r + 1)
    query = jnp.where(mine, qkv_ref[span, q_cols(p)], 0)
    scores = dot_t(query, qkv_ref[:upto, k_cols(p)])
    head = 2 * p + h
    differences = c[span, head : head + 1] - ct[head : head + 1, :upto]
    causal = iota((rows, upto), 0) + rows * r >= iota((rows, upto), 1)
    decays = jnp.exp(jnp.where(causal, differences, -1e30))
    return mine, span, upto, scores, decays


def mix_kernel(
    core_ref, qkv_ref, c_ref, ct_ref, s0_ref, u_ref,
    mixed_ref, own_ref, sent_ref, s1_ref, state,
):
    step = pl.program_id(0)
    slot = step ^ core_ref[0]
    count = c_ref.shape[0]
    rows = count // 2
    lane = iota((1, WIDE), 1)
    c, ct = c_ref[...], ct_ref[...]

    @pl.when(step == 0)
    def _():
        state[...] = s0_ref[...].astype(F32)

    growth = jnp.exp(c)
    for p in range(PAIRS):
        held = state[p]
        carried = spread_pair(growth, p) * dot(qkv_ref[:, q_cols(p)], held.astype(BF16))
        for r in range(2):
            parts = []
            for h in range(2):
                mine, span, upto, scores, decays = tile_of(qkv_ref, c, ct, r, rows, p, h)
                weighted = (scores * decays).astype(BF16)
                parts.append(dot(weighted, qkv_ref[:upto, v_cols(p)]))
            mixed = jnp.where(lane < HEAD, parts[0], parts[1]) + carried[span]
            mixed_ref[span, q_cols(p)] = mixed
            scale = lax.rsqrt(head_sums(mixed * mixed) * (1.0 / HEAD) + head_floor)
            normed = (mixed * scale).astype(BF16)

            @pl.when(slot == 0)
            def _():
                own_ref[span, q_cols(p)] = normed

            @pl.when(slot == 1)
            def _():
                sent_ref[span, q_cols(p)] = normed

        @pl.when(step == 0)
        def _():
            grown = spread_pair(growth[count - 1 :], p) * held + u_ref[p]
            s1_ref[p] = grown
            state[p] = grown


def out_kernel(
    core_ref, own_ref, got_ref, half_ref, other_ref, x_ref, gains_ref, middle_ref, normed_ref
):
    core = core_ref[0]
    n = own_ref.shape[1]
    mine = pl.ds(pl.multiple_of(core * n, n), n)
    theirs = pl.ds(pl.multiple_of((1 - core) * n, n), n)
    own, got = own_ref[...], got_ref[...]
    a = dot(own, half_ref[mine, :]) + dot(got, half_ref[theirs, :])
    b = dot(own, other_ref[mine, :]) + dot(got, other_ref[theirs, :])
    attention = jnp.where(core == 0, jnp.concatenate([a, b], 1), jnp.concatenate([b, a], 1))
    middle = x_ref[...].astype(F32) + attention
    middle_ref[...] = middle
    normed_ref[...] = (middle * inverse_rms(middle) * gains_ref[1:2]).astype(BF16)


def permuted(v, back=False):
    n = v.shape[1] // 8
    order = [4 * (j % 2) + j // 2 for j in range(8)]
    if back:
        order = [2 * (j % 4) + j // 4 for j in range(8)]
    return jnp.concatenate([v[:, n * j : n * (j + 1)] for j in order], 1)


def ff_kernel(
    small, where_ref, weight_ref, own_ref, other_ref, cot_ref, cot_other_ref, gate_ref, up_ref,
    hidden_ref, slopes_ref, x_ref, branch_ref,
):
    first = pl.program_id(0) == 0
    x = jnp.where(first, own_ref[...], other_ref[...])
    x_ref[...] = x
    cot = jnp.where(first, cot_ref[...], cot_other_ref[...]).astype(F32)
    branch = (cot * weight_ref[0]).astype(BF16)
    branch_ref[...] = permuted(branch) if small else branch
    gate = dot(x, gate_ref[...])
    up = dot(x, up_ref[...])
    n = gate.shape[1]
    sigmoid = 1.0 / (1.0 + jnp.exp(-gate))
    silu = gate * sigmoid
    hidden_ref[...] = (silu * up).astype(BF16)
    slopes_ref[:, :n] = (up * (sigmoid * (1.0 + gate * (1.0 - sigmoid)))).astype(BF16)
    slopes_ref[:, n:] = silu.astype(BF16)


def ff_back_kernel(small, where_ref, g_ref, w_ref, slopes_ref, grad_ref):
    branch = permuted(g_ref[...], True) if small else g_ref[...]
    grad = dot(branch, w_ref[...])
    n = grad.shape[1]
    grad_ref[:, :n] = (grad * slopes_ref[:, :n].astype(F32)).astype(BF16)
    grad_ref[:, n:] = (grad * slopes_ref[:, n:].astype(F32)).astype(BF16)


def part_kernel(grad_ref, gate_ref, up_ref, part_ref):
    n = gate_ref.shape[1]
    part = dot_t(grad_ref[:, :n], gate_ref[...]) + dot_t(grad_ref[:, n:], up_ref[...])
    part_ref[...] = part.astype(part_ref.dtype)


def middle_kernel(
    core_ref, weight_ref, grad_ref, gate_ref, up_ref, got_ref, cot_ref, middle_ref, gains_ref,
    half_ref, other_ref, grad_middle_ref, attention_ref, gain_ref, own_ref, sent_ref,
):
    core = core_ref[0]
    n = gate_ref.shape[1]
    part = dot_t(grad_ref[:, :n], gate_ref[...]) + dot_t(grad_ref[:, n:], up_ref[...])
    part = part + got_ref[...].astype(F32)
    middle = middle_ref[...]
    scale = inverse_rms(middle)
    unit = middle * scale
    gain_ref[...] = jnp.broadcast_to(jnp.sum(part * unit, axis=0, keepdims=True), gain_ref.shape)
    grad_middle = cot_ref[...].astype(F32) * weight_ref[0]
    grad_middle = grad_middle + norm_back(part * gains_ref[1:2], unit, scale)
    grad_middle_ref[...] = grad_middle
    attention = grad_middle.astype(BF16)
    attention_ref[...] = attention
    n = half_ref.shape[1]
    low, high = attention[:, :n], attention[:, n:]
    kept, rest = jnp.where(core == 0, low, high), jnp.where(core == 0, high, low)
    for ref, at in ((own_ref, core), (sent_ref, 1 - core)):
        rows = pl.ds(pl.multiple_of(at * n, n), n)
        ref[...] = (dot_t(kept, half_ref[rows, :]) + dot_t(rest, other_ref[rows, :])).astype(BF16)


def out_back_kernel(core_ref, own_ref, got_ref, attention_ref, kept_ref, sent_ref):
    core = core_ref[0]
    n = own_ref.shape[1]
    low, high = attention_ref[:, :n], attention_ref[:, n:]
    kept, rest = jnp.where(core == 0, low, high), jnp.where(core == 0, high, low)
    for ref, at in ((own_ref, core), (got_ref, 1 - core)):
        rows = pl.ds(pl.multiple_of(at * n, n), n)
        heads = ref[...]
        kept_ref[rows, :] = t_dot(heads, kept).astype(BF16)
        sent_ref[rows, :] = t_dot(heads, rest).astype(BF16)


def head_back_kernel(
    core_ref, own_ref, got_ref, mixed_ref, q_ref, c_ref,
    gm_ref, p1_ref, enter_ref, first_p, decay,
):
    step = pl.program_id(0)
    slot = step ^ core_ref[0]
    count = c_ref.shape[0]
    growth = jnp.exp(c_ref[...])
    mask = own_blocks()
    for p in range(PAIRS):
        mixed = mixed_ref[:, q_cols(p)]
        grad = jnp.where(slot == 0, own_ref[:, q_cols(p)], got_ref[:, q_cols(p)]).astype(F32)
        scale = lax.rsqrt(head_sums(mixed * mixed) * (1.0 / HEAD) + head_floor)
        unit = mixed * scale
        back = scale * (grad - unit * (head_sums(grad * unit) * (1.0 / HEAD)))
        gm = back.astype(BF16)
        gm_ref[:, q_cols(p)] = gm
        grown = (q_ref[:, q_cols(p)].astype(F32) * spread_pair(growth, p)).astype(BF16)
        through = jnp.where(mask, t_dot(grown, gm), 0.0)

        @pl.when(step == 0)
        def _():
            first_p[p] = through
            decay[p] = jnp.broadcast_to(spread_pair(growth[count - 1 :], p), (8, WIDE))

        @pl.when(step == 1)
        def _():
            p1_ref[p] = through
            enter_ref[p] = (first_p[p] + decay[p][:1] * through).astype(BF16)


def back_kernel(
    core_ref, qkv_ref, c_ref, ct_ref, z_ref, gm_ref, s0_ref, s1_ref, e1_ref, p1_ref, cos_ref,
    sin_ref, front_ref, bias_ref, later, early,
):
    step = pl.program_id(0)
    count = c_ref.shape[0]
    rows = count // 2
    lane = iota((1, WIDE), 1)
    c, ct = c_ref[...], ct_ref[...]
    growth = jnp.exp(c)
    last = c[count - 1 :]
    tail = jnp.exp(last - c)
    last_row = iota((count, 1), 0) == count - 1
    per_head = jnp.zeros((count, WIDE), F32)
    key_sums, value_sums = [None, None], [None, None]
    cosine, sine_part = cos_ref[...], -sin_ref[...]

    @pl.when(step == 0)
    def _():
        later[...] = e1_ref[...].astype(F32)
        early[...] = s1_ref[...]

    @pl.when(step == 1)
    def _():
        early[...] = s0_ref[...].astype(F32)

    for p in range(PAIRS):
        held, ahead = early[p], later[p]
        query, key, value = qkv_ref[:, q_cols(p)], qkv_ref[:, k_cols(p)], qkv_ref[:, v_cols(p)]
        gm = gm_ref[:, q_cols(p)]
        query_t, gm_t = query.astype(F32).T.astype(BF16), gm.astype(F32).T.astype(BF16)
        d_query, d_key_t, d_value_t = [], [], []
        for h in range(2):
            by_rows, key_t, value_t = [], None, None
            for r in range(2):
                mine, span, upto, scores, decays = tile_of(qkv_ref, c, ct, r, rows, p, h)
                weighted = (scores * decays).astype(BF16)
                grad_weighted = dot_t(jnp.where(mine, gm[span], 0), value[:upto])
                grad_scores = (grad_weighted * decays).astype(BF16)
                by_rows.append(dot(grad_scores, key[:upto]))
                part = slice(HEAD * h, HEAD * (h + 1))
                one_key = dot(query_t[part, span], grad_scores)
                one_value = dot(gm_t[part, span], weighted)
                if r == 0:
                    key_t, value_t = one_key, one_value
                else:
                    key_t = jnp.concatenate([one_key[:, :rows] + key_t, one_key[:, rows:]], 1)
                    value_t = jnp.concatenate(
                        [one_value[:, :rows] + value_t, one_value[:, rows:]], 1
                    )
            d_query.append(jnp.concatenate(by_rows, 0))
            d_key_t.append(key_t)
            d_value_t.append(value_t)
        d_query = jnp.where(lane < HEAD, d_query[0], d_query[1])
        d_query = d_query + spread_pair(growth, p) * dot_t(gm, held.astype(BF16))
        ahead_low = ahead.astype(BF16)
        tails = spread_pair(tail, p)
        d_key_tail = tails * dot_t(value, ahead_low)
        d_key = jnp.concatenate(d_key_t, 0).T + d_key_tail
        d_value = jnp.concatenate(d_value_t, 0).T
        key_f = key.astype(F32)
        d_value = d_value + dot((key_f * tails).astype(BF16), ahead_low)
        total = spread_pair(jnp.exp(last), p)
        at_last = jnp.sum(key_f * d_key_tail, axis=0, keepdims=True)
        at_last = at_last + jnp.sum(ahead * held, axis=0, keepdims=True) * total
        grad_c = query.astype(F32) * d_query - key_f * d_key
        grad_c = grad_c + jnp.where(last_row, at_last, 0.0)
        to_head = iota((WIDE, WIDE), 1) == 2 * p + (iota((WIDE, WIDE), 0) >= HEAD)
        for third in thirds(grad_c):
            per_head = per_head + dot(third, to_head.astype(BF16))
        turned = turn(d_query, cosine, sine_part) * float(HEAD) ** (-0.5)
        front_ref[:, q_cols(p)] = turned.astype(BF16)
        if p < 2:
            key_sums[p], value_sums[p] = d_key, d_value
        else:
            key_sums[p - 2] = key_sums[p - 2] + d_key
            value_sums[p - 2] = value_sums[p - 2] + d_value

        @pl.when(step == 0)
        def _():
            later[p] = p1_ref[p] + total * ahead

    for p in range(2):
        front_ref[:, k_cols(p)] = turn(key_sums[p], cosine, sine_part).astype(BF16)
        front_ref[:, v_cols(p)] = value_sums[p].astype(BF16)
    upper = (iota((count, count), 0) <= iota((count, count), 1)).astype(BF16)
    grad_log = sum(dot(upper, third) for third in thirds(per_head))
    z = z_ref[...]
    grad_gate = jnp.where(lane < HALF, -grad_log / (GATE_TEMP * (1.0 + jnp.exp(-z))), 0.0)
    front_ref[:, N_FRONT - WIDE :] = grad_gate.astype(BF16)
    summed = jnp.broadcast_to(jnp.sum(grad_gate, axis=0, keepdims=True), (8, WIDE))

    @pl.when(step == 0)
    def _():
        bias_ref[...] = summed

    @pl.when(step == 1)
    def _():
        bias_ref[...] += summed


def front_back_kernel(
    core_ref, normed_ref, grad_ref, w_ref, own_ref, other_ref, gain_ref, bias_ref, kept_ref,
    got_ref, part_ref, sent_ref, *refs,
):
    *outs, d_ref = refs
    grad = grad_ref[...]
    d = t_dot(normed_ref[...], grad)
    part = dot_t(grad, w_ref[...])
    count = own_ref.shape[0]
    part_ref[...] = part[:count]
    sent_ref[...] = part[count:].astype(BF16)
    d_gain = jnp.zeros((1, part.shape[1]), F32)
    for ref, rows in ((own_ref, part[:count]), (other_ref, part[count:])):
        x = ref[...].astype(F32)
        unit = x * lax.rsqrt(jnp.mean(x * x, axis=-1, keepdims=True) + epsilon)
        d_gain = d_gain + jnp.sum(rows * unit, axis=0, keepdims=True)
    main = N_FRONT - WIDE
    d_ref[:, :main] = d[:, :main].astype(BF16)
    rest = jnp.concatenate(
        [jnp.zeros((HALF, d_gain.shape[1]), F32), d_gain, gain_ref[:1]]
        + [jnp.zeros((WIDE - HALF - 2, d_gain.shape[1]), F32)],
        0,
    ).T
    d_ref[:, main:N_FRONT] = (d[:, main:] + rest + pltpu.roll(bias_ref[...], HALF + 2, 1)[:1]).astype(BF16)
    d_ref[:, N_FRONT:] = (kept_ref[...].astype(F32) + got_ref[...].astype(F32)).astype(BF16)
    if len(outs) == 1:
        outs[0][...] = d_ref[...]
    else:
        own, over_dp, over_mid, first, second = outs
        rows = own.shape[1]
        for i in range(4):
            for ref, b in ((own, (0, 0)), (over_dp, (1, 0)), (over_mid, (0, 1))):
                ref[i] = d_ref[pl.ds(row_of(core_ref, i, b, rows), rows), :]
            far = first if i < 2 else second
            far[i % 2] = d_ref[pl.ds(row_of(core_ref, i, (1, 1), rows), rows), :]


def far_kernel(core_ref, far_ref, to_dp_ref, to_mid_ref):
    far = far_ref[...].reshape((-1,) + far_ref.shape[-1:])
    n = to_dp_ref.shape[0]
    to_dp_ref[...] = far[:n]
    to_mid_ref[...] = far[n:]


def sends_kernel(core_ref, dp_ref, mid_ref, to_mid_ref, to_dp_ref, over_dp_ref, over_mid_ref):
    width = dp_ref.shape[-1]
    over_dp, over_mid = dp_ref[...].reshape(-1, width), mid_ref[...].reshape(-1, width)
    to_mid, to_dp = to_mid_ref[...].reshape(-1, width), to_dp_ref[...].reshape(-1, width)
    n = to_dp.shape[0]
    over_dp_ref[:n] = over_dp[:n]
    over_dp_ref[n:] = (over_dp[n:].astype(F32) + to_dp.astype(F32)).astype(BF16)
    over_mid_ref[:n] = (over_mid[:n].astype(F32) + to_mid.astype(F32)).astype(BF16)
    over_mid_ref[n:] = over_mid[n:]


def own_kernel(core_ref, own_ref, dp_ref, mid_ref, sum_ref):
    own = own_ref[...].reshape(dp_ref.shape).astype(F32)
    sum_ref[...] = (own + dp_ref[...].astype(F32) + mid_ref[...].astype(F32)).astype(BF16)


def sum_kernel(core_ref, own_ref, dp_ref, mid_ref, kept_ref, sent_ref):
    n = kept_ref.shape[0]
    whole = own_ref[...].astype(F32) + dp_ref[...].astype(F32) + mid_ref[...].astype(F32)
    kept_ref[...] = whole[:n]
    sent_ref[...] = whole[n:].astype(BF16)


def down_kernel(core_ref, hidden_ref, w_ref, out_ref):
    out_ref[...] = dot_t(hidden_ref[...], w_ref[...]).astype(BF16)


def output_kernel(core_ref, hidden_ref, w_ref, middle_ref, got_ref, out_ref):
    out = middle_ref[...] + dot_t(hidden_ref[...], w_ref[...])
    out_ref[...] = (out + got_ref[...].astype(F32)).astype(BF16)


def input_kernel(core_ref, part_ref, got_ref, middle_ref, x_ref, gains_ref, out_ref):
    x = x_ref[...].astype(F32)
    scale = inverse_rms(x)
    grad = (part_ref[...] + got_ref[...].astype(F32)) * gains_ref[:1]
    out_ref[...] = (middle_ref[...] + norm_back(grad, x * scale, scale)).astype(BF16)


def last_kernel(core_ref, pair_ref, got_ref, mine_ref, sent_ref):
    whole = (pair_ref[...] + got_ref[...].astype(F32)).astype(BF16)
    n = mine_ref.shape[0]
    low, high = whole[:n], whole[n:]
    mine_ref[...] = jnp.where(core_ref[0] == 0, low, high)
    sent_ref[...] = jnp.where(core_ref[0] == 0, high, low)


def unpack_kernel(
    core_ref, mine_ref, got_ref, q_ref, k_ref, v_ref, a_ref, o_ref, gains_ref, bias_ref
):
    def both(ref, at):
        n = ref.shape[1] // 2
        a, b = mine_ref[:, at : at + n].astype(F32), got_ref[:, at : at + n].astype(F32)
        ref[:, :n] = jnp.where(core_ref[0] == 0, a, b)
        ref[:, n:] = jnp.where(core_ref[0] == 0, b, a)
        return at + n

    at = both(q_ref, 0)
    at = both(k_ref, at)
    at = both(v_ref, at)
    both(o_ref, N_FRONT)
    a = mine_ref[:, at:N_FRONT].astype(F32).T
    b = got_ref[:, at:N_FRONT].astype(F32).T
    low, high = jnp.where(core_ref[0] == 0, a, b), jnp.where(core_ref[0] == 0, b, a)
    a_ref[:HALF] = low[:HALF]
    a_ref[HALF:] = high[:HALF]
    gains_ref[...] = (a + b)[HALF : HALF + 8]
    bias_ref[:HALF] = low[HALF + 2 : 2 * HALF + 2]
    bias_ref[HALF:] = high[HALF + 2 : 2 * HALF + 2]


def call(kernel, ins, outs, name, microseconds, megabytes, steps=1, scratch=(), deps=(), reverse=False):
    order = (lambda i, s: (1 - i) ^ s[0]) if reverse else (lambda i, s: i ^ s[0])

    def spec(kind, shape):
        zeros = (0,) * (len(shape) - 1)
        if kind == "all":
            return pl.BlockSpec(shape, lambda i, s: (0,) + zeros)
        if kind == "scalar":
            return SCALARS
        if kind == "block":
            return pl.BlockSpec((shape[0] // 2,) + shape[1:], lambda i, s: (order(i, s),) + zeros)
        if kind == "rows":
            return pl.BlockSpec((shape[0] // steps,) + shape[1:], lambda i, s: (i,) + zeros)
        if kind == "entry":
            return pl.BlockSpec((None,) + shape[1:], lambda i, s: (order(i, s),) + zeros)
        if kind == "queries":
            return pl.BlockSpec((shape[0] // 2, N_Q), lambda i, s: (order(i, s), 0))
        if kind in ("own", "over_dp", "over_mid", "far"):
            a, b = int(kind in ("over_dp", "far")), int(kind in ("over_mid", "far"))
            block = (1, shape[1], 1) + shape[3:]
            return pl.BlockSpec(block, lambda i, s: (s[1] ^ a, 0, s[3] ^ b, 0, 0))
        block, index = kind
        return pl.BlockSpec(block, lambda i, s: index)

    where, *ins = ins
    moved = sum(v.size * v.dtype.itemsize for _, v in ins)
    return pl.pallas_call(
        without(kernel, 1 + len(ins), len(deps)),
        grid_spec=pltpu.PrefetchScalarGridSpec(
            num_scalar_prefetch=1,
            grid=(steps,),
            in_specs=[spec(kind, v.shape) for kind, v in ins] + [ANYWHERE] * len(deps),
            out_specs=[spec(kind, shape) for kind, shape, _ in outs],
            scratch_shapes=scratch,
        ),
        out_shape=[jax.ShapeDtypeStruct(shape, kind) for _, shape, kind in outs],
        compiler_params=pltpu.CompilerParams(
            dimension_semantics=("arbitrary",), vmem_limit_bytes=megabytes * 1024 * 1024
        ),
        cost_estimate=pl.CostEstimate(
            flops=int(microseconds * FLOPS), bytes_accessed=moved, transcendentals=0
        ),
        name=name,
    )(where, *[v for _, v in ins], *deps)


def piece(whole, a, b, low, count):
    sizes = (1, count, 1) + whole.shape[3:]
    return lax.dynamic_slice(whole, (a, low, b, 0, 0), sizes).reshape((count,) + whole.shape[3:])


def square_sends(over_dp, over_mid, to_mid, to_dp):
    half = to_mid.shape[0]
    send_mid = jnp.concatenate([over_mid[:half] + to_mid, over_mid[half:]], 0)
    send_dp = jnp.concatenate([over_dp[:half], over_dp[half:] + to_dp], 0)
    return send_dp, send_mid


def hi_swap(v, difference):
    return lax.ppermute(v, "hi", [(i, i ^ difference) for i in range(4)])


def sequence_weights(group_ids, loss_weights):
    group_count = loss_weights.shape[0]
    member = (group_ids[:, None] == jnp.arange(group_count, dtype=jnp.int32)[None, :]).astype(F32)
    counts = jnp.sum(member, axis=0)
    raw_weight = jnp.sum(member * loss_weights.astype(F32)[None, :], axis=1) / jnp.sum(
        member * counts[None, :], axis=1
    )
    return raw_weight * (group_ids.shape[0] / jnp.sum(raw_weight))


def shards(
    tokens,
    cotangent,
    group_ids,
    loss_weights,
    gain_one,
    w_query,
    w_key,
    w_value,
    w_gate,
    gate_bias,
    w_out,
    gain_two,
    w_gate_ff,
    w_up,
    w_down,
):
    count, width = tokens.shape
    both = 2 * count
    n_out, n_ff = w_out.shape[1] // 2, w_up.shape[1] // 2
    n_first = N_FRONT + n_out
    core, mid = lax.axis_index("core"), lax.axis_index("mid")
    dp, hi = lax.axis_index("dp"), lax.axis_index("hi")
    where = jnp.stack([core, dp, hi, mid]).astype(jnp.int32)
    small = small_slice()
    sequence = lax.axis_index(ALL) // SPAN
    square = (PAIRS, WIDE, WIDE)

    packed = pack(
        core, w_query, w_key, w_value, w_gate.T, gain_one[None], gain_two[None], w_out, w_gate_ff,
        w_up, w_down.T,
    )
    first = place(core, packed[0], swap(packed[2], "core"))
    rest = place(core, packed[1], swap(packed[3], "core"))
    w_rest = gather(rest)
    if small:
        pair = jnp.stack([first, hi_swap(first, 2)])
        own = jnp.concatenate([pair, hi_swap(pair, 1)], 0)
        over_dp, over_mid = swap(own, "dp"), swap(own, "mid")
        pieces = (own, over_dp, over_mid, swap(over_dp[:2], "mid"), swap(over_mid[2:], "dp"))
    else:
        pieces = (gather(first),)
    other_tokens, other_cotangent = swap(tokens, "core"), swap(cotangent, "core")
    gate_block, up_block, down_block = [((width, n_ff), (0, i)) for i in range(3)]

    block = 2 * mid + (core ^ jnp.arange(2))
    positions = (block[:, None] * count + jnp.arange(count)[None, :]).reshape(-1)
    frequency = ROPE_BASE ** (-jnp.arange(HEAD // 2, dtype=F32) / (HEAD // 2))
    angles = positions.astype(F32)[:, None] * frequency[None, :]
    cosine, sine_part = jnp.cos(angles), jnp.sin(angles)
    cosine = jnp.concatenate([cosine] * 4, 1)
    sine_part = jnp.concatenate([-sine_part, sine_part] * 2, 1)
    own_bias = lax.dynamic_slice_in_dim(gate_bias, core * HALF, HALF)
    own_bias = jnp.concatenate([own_bias, jnp.zeros((WIDE - HALF,), F32)])[None, :]
    w_front, w_half, normed_one, qkv, c, ct, z, gains, update, leaving = call(
        front_kernel,
        [where, ("all", tokens), ("all", other_tokens), ("all", own_bias)]
        + [("block", cosine), ("block", sine_part)]
        + [("all", v) for v in pieces],
        [("all", (width, N_FRONT), BF16), ("all", (width, n_out), BF16)]
        + [("block", (both, width), BF16), ("block", (both, 2 * N_Q), BF16)]
        + [("block", (both, WIDE), F32), ("entry", (2, HALF, count), F32)]
        + [("block", (both, WIDE), F32), ("all", (8, width), F32)]
        + [("all", square, F32), ("all", square, BF16)],
        "front",
        14,
        24,
        2,
        [pltpu.VMEM(square, F32)],
    )
    state_0 = lax.ppermute(leaving, "mid", [(0, 1)])
    w_other = swap(w_half, "core")
    mixed_out, normed_own, normed_sent, state_1 = call(
        mix_kernel,
        [where, ("block", qkv), ("block", c), ("entry", ct), ("all", state_0), ("all", update)],
        [("block", (both, N_Q), F32)]
        + [("all", (count, N_Q), BF16)] * 2
        + [("all", square, F32)],
        "mix",
        11,
        16,
        2,
        [pltpu.VMEM(square, F32)],
    )
    normed_got = swap(normed_sent, "core")
    middle, normed_two_own = call(
        out_kernel,
        [where]
        + [("all", v) for v in (normed_own, normed_got, w_half, w_other, tokens, gains)],
        [("all", (count, width), F32), ("all", (count, width), BF16)],
        "out",
        4,
        16,
    )
    normed_two_other = swap(normed_two_own, "core")
    seq_weights = sequence_weights(group_ids, loss_weights)
    own_weight = jnp.sum(jnp.where(jnp.arange(group_ids.shape[0]) == sequence, seq_weights, 0.0))
    own_weight = own_weight.reshape(1)
    hidden, slopes, normed_two, grad_branch = call(
        functools.partial(ff_kernel, small),
        [where, ("scalar", own_weight), ("all", normed_two_own), ("all", normed_two_other)]
        + [("all", cotangent), ("all", other_cotangent)]
        + [(gate_block, w_rest), (up_block, w_rest)],
        [("rows", (both, n_ff), BF16), ("rows", (both, 2 * n_ff), BF16)]
        + [("rows", (both, width), BF16)] * 2,
        "ff",
        15,
        44,
        2,
    )
    d_down = jnp.einsum(
        "ta,tb->ab", grad_branch, hidden, preferred_element_type=F32
    ).astype(BF16)
    if small:
        by_hi = d_down
        down_hi = d_down.reshape(4, -1, n_ff)
        down_hi = lax.psum_scatter(down_hi, "hi", scatter_dimension=0, tiled=False)
        down_hi = down_hi.reshape(2, 1, 2, -1, n_ff)
    else:
        by_hi = d_down
        down_sum = scatter(d_down)
    (grad_ff,) = call(
        functools.partial(ff_back_kernel, small),
        [where, ("rows", grad_branch), (down_block, w_rest), ("rows", slopes)],
        [("rows", (both, 2 * n_ff), BF16)],
        "ff_back",
        9,
        32,
        2,
        deps=(by_hi,),
    )
    d_ff = jnp.einsum(
        "ta,tb->ab", normed_two, grad_ff, preferred_element_type=F32
    ).astype(BF16)
    if small:
        d_ff = d_ff.reshape(2, 4, 2, -1, 2 * n_ff)
        ff_sends = [piece(d_ff, 1 - dp, 1 - mid, i, 2) for i in (0, 2)]
        ff_one = swap(ff_sends[0], "dp"), swap(ff_sends[1], "mid")
    else:
        ff_sends = [d_ff]
        ff_sum = scatter(d_ff)
    (part_sent,) = call(
        lambda _, *refs: part_kernel(*refs),
        [where, (((count, 2 * n_ff), (1, 0)), grad_ff), (gate_block, w_rest), (up_block, w_rest)],
        [("all", (count, width), BF16)],
        "part",
        8,
        24,
        deps=ff_sends,
    )
    part_got = swap(part_sent, "core")
    grad_middle, grad_attention, d_gain_two, grad_own, grad_sent = call(
        middle_kernel,
        [where, ("scalar", own_weight), (((count, 2 * n_ff), (0, 0)), grad_ff)]
        + [(gate_block, w_rest), (up_block, w_rest)]
        + [("all", v) for v in (part_got, cotangent, middle, gains, w_half, w_other)],
        [("all", (count, width), F32), ("all", (count, width), BF16), ("all", (8, width), F32)]
        + [("all", (count, N_Q), BF16)] * 2,
        "middle",
        12,
        36,
        deps=(part_sent,),
    )
    grad_got = swap(grad_sent, "core")
    d_out_kept, d_out_sent = call(
        out_back_kernel,
        [where] + [("all", v) for v in (normed_own, normed_got, grad_attention)],
        [("all", (width, n_out), BF16)] * 2,
        "out_back",
        2,
        16,
    )
    d_out_got = swap(d_out_sent, "core")
    grad_mixed, through, entering = call(
        head_back_kernel,
        [where, ("all", grad_own), ("all", grad_got), ("block", mixed_out), ("queries", qkv)]
        + [("block", c)],
        [("block", (both, N_Q), BF16), ("all", square, F32), ("all", square, BF16)],
        "head_back",
        8,
        16,
        2,
        [pltpu.VMEM(square, F32), pltpu.VMEM((PAIRS, 8, WIDE), F32)],
        deps=(d_out_sent,),
    )
    state_last = lax.ppermute(entering, "mid", [(1, 0)])
    down_rows = ((count, n_ff), (1, 0)), ((count, n_ff), (0, 0))
    (out_sent,) = call(
        down_kernel,
        [where, (down_rows[0], hidden), (down_block, w_rest)],
        [("all", (count, width), BF16)],
        "out_sent",
        5,
        16,
        deps=(entering,),
    )
    if small:
        ff_sends = call(
            sends_kernel,
            [where, ("over_dp", d_ff), ("over_mid", d_ff)] + [("all", v) for v in ff_one],
            [("all", (width // 4, 2 * n_ff), BF16)] * 2,
            "ff_sends",
            3,
            16,
            deps=(state_last, out_sent),
        )
        ff_got = swap(ff_sends[0], "dp"), swap(ff_sends[1], "mid")
    grad_front, d_bias = call(
        back_kernel,
        [where, ("block", qkv), ("block", c), ("entry", ct), ("block", z), ("block", grad_mixed)]
        + [("all", v) for v in (state_0, state_1, state_last, through)]
        + [("block", cosine), ("block", sine_part)],
        [("block", (both, N_FRONT), BF16), ("all", (8, WIDE), F32)],
        "back",
        20,
        24,
        2,
        [pltpu.VMEM(square, F32), pltpu.VMEM(square, F32)],
        deps=ff_sends,
        reverse=True,
    )
    (output,) = call(
        output_kernel,
        [where, (down_rows[1], hidden), (down_block, w_rest)]
        + [("all", v) for v in (middle, swap(out_sent, "core"))],
        [("all", (count, width), BF16)],
        "output",
        5.5,
        16,
        deps=(grad_front,),
    )
    if small:
        (ff_hi,) = call(
            own_kernel,
            [where, ("own", d_ff)] + [("all", v.reshape(4, -1, 2 * n_ff)) for v in ff_got],
            [("all", (4, width // 16, 2 * n_ff), BF16)],
            "ff_own",
            3,
            16,
            deps=(output,),
        )
        ff_sum = lax.psum_scatter(ff_hi, "hi", scatter_dimension=0, tiled=False)
        shapes = [(4, width // 16, n_first)] * 3 + [(2, width // 16, n_first)] * 2
        deps = (ff_hi,)
    else:
        shapes = [(width, n_first)]
        deps = (output,)
    part_kept, part_sent, *d_first = call(
        front_back_kernel,
        [where]
        + [("all", v) for v in (normed_one, grad_front, w_front, tokens, other_tokens)]
        + [("all", v) for v in (d_gain_two, d_bias, d_out_kept, d_out_got)],
        [("all", (count, width), F32), ("all", (count, width), BF16)]
        + [("all", shape, BF16) for shape in shapes],
        "front_back",
        12,
        32,
        scratch=[pltpu.VMEM((width, n_first), BF16)],
        deps=deps,
    )
    part_got = swap(part_sent, "core")

    def add_input(deps):
        return call(
            input_kernel,
            [where]
            + [("all", v) for v in (part_kept, part_got, grad_middle, tokens, gains)],
            [("all", (count, width), BF16)],
            "grad_input",
            4.5,
            16,
            deps=deps,
        )

    if small:
        own, over_dp, over_mid, far_0, far_1 = d_first
        one = swap(far_0, "dp"), swap(far_1, "mid")
        down_sends = call(
            far_kernel,
            [where, ("far", down_hi)],
            [("all", (width // 32, n_ff), BF16)] * 2,
            "down_far",
            1.5,
            16,
            deps=(far_0,),
        )
        down_one = swap(down_sends[0], "dp"), swap(down_sends[1], "mid")
        sends = square_sends(over_dp, over_mid, *one)
        down_sends = call(
            sends_kernel,
            [where, ("over_dp", down_hi), ("over_mid", down_hi)] + [("all", v) for v in down_one],
            [("all", (width // 16, n_ff), BF16)] * 2,
            "down_sends",
            2,
            16,
            deps=(sends[0],),
        )
        down_got = swap(down_sends[0], "dp"), swap(down_sends[1], "mid")
        (grad_input,) = add_input(sends[:1])
        kept, sent = call(
            sum_kernel,
            [where]
            + [("all", v) for v in (own, swap(sends[0], "dp"), swap(sends[1], "mid"))],
            [("all", (2,) + own.shape[1:], F32), ("all", (2,) + own.shape[1:], BF16)],
            "first_sum",
            2,
            16,
            deps=(grad_input, *down_sends),
        )
        pair = kept + hi_swap(sent, 1).astype(F32)
        last, last_got = pair[0], hi_swap(pair[1].astype(BF16), 2)
        (down_sum,) = call(
            own_kernel,
            [where, ("own", down_hi)] + [("all", v) for v in down_got],
            [("all", (width // 16, n_ff), BF16)],
            "down_own",
            1.5,
            16,
            deps=(kept,),
        )
    else:
        last = scatter(d_first[0]).astype(F32)
        last_got = jnp.zeros_like(last, BF16)
        (grad_input,) = add_input(())

    def owned(rows):
        n = rows.shape[0] // 2
        mine = lax.dynamic_slice_in_dim(rows, core * n, n)
        return mine, swap(lax.dynamic_slice_in_dim(rows, (1 - core) * n, n), "core")

    outs = []
    for v in (ff_sum[:, :n_ff], ff_sum[:, n_ff:], down_sum):
        mine, theirs = owned(v)
        outs.append((mine, theirs))
    n = last.shape[0] // 2
    mine, sent = call(
        last_kernel,
        [where, ("all", last), ("all", last_got)],
        [("all", (n, n_first), BF16)] * 2,
        "last",
        1.5,
        16,
        deps=tuple(theirs for _, theirs in outs),
    )
    theirs = swap(sent, "core")
    g_gate_ff, g_up, g_down = [beside(core, *v) for v in outs]
    g_query, g_key, g_value, g_gate, g_out, g_gains, g_bias = call(
        unpack_kernel,
        [where, ("all", mine), ("all", theirs)],
        [("all", (n, 2 * N_Q), F32)]
        + [("all", (n, 2 * N_K), F32)] * 2
        + [("all", (HEADS, n), F32), ("all", (n, 2 * n_out), F32)]
        + [("all", (8, n), F32), ("all", (HEADS, n), F32)],
        "unpack",
        1.5,
        16,
    )
    return (
        output,
        grad_input,
        g_gains[0],
        g_query,
        g_key,
        g_value,
        g_gate.T,
        g_bias[:, 0],
        g_out,
        g_gains[1],
        g_gate_ff,
        g_up,
        g_down.T,
    )


def solution(mesh):
    devices = mesh.devices
    fine = Mesh(
        devices.reshape(devices.shape[0], devices.shape[1] // SPAN, SPAN // 2, 2), ALL
    )
    rows, columns, split = P(ALL, None), P(None, ALL), P(ALL)
    in_specs = (rows, rows, P(), P(), split) + (rows,) * 4 + (P(), rows, split, rows, rows, columns)
    out_specs = (rows, rows, split) + (rows,) * 4 + (P(), rows, split, rows, rows, columns)
    return jax.shard_map(shards, mesh=fine, in_specs=in_specs, out_specs=out_specs, check_vma=False)
```

time: 567 us -> 373 us (0.66)
  matrix products: 151 us -> 14.7 us
  Pallas kernels: 0 us -> 117 us
  other arithmetic: 79 us -> 12.5 us
  blocking collectives: 36.5 us -> 0 us
  local copies, waits for them, and re-layouts: 62.1 us -> 33.3 us
  starting transfers between devices: 67.8 us -> 39 us
  waiting for transfers between devices: 147 us -> 133 us
    dot_general x27 -> x2, matrix products: 151 us -> 14.7 us  [the longest x1 8.15 us: shards(): jnp.einsum('ta,tb->ab', grad_branch, hidden, preferred_element_type=F32)]
    pallas_call x0 -> x23, Pallas kernels: none -> 117 us  [the longest x22 115 us: call(): pl.pallas_call(without(kernel, 1 + len(ins), len(deps)), grid_spec=pltpu....]
    ppermute x48 -> x32, waiting for transfers between devices: 119 us -> 78.6 us  [swap(): return lax.ppermute(v, axis, [(0, 1), (1, 0)])]
    all_gather x1 -> x0, blocking collectives: 36.5 us -> none  [hi_gather(): return lax.all_gather(part, 'hi')]
    ppermute x48 -> x32, starting transfers between devices: 55.2 us -> 22.4 us  [swap(): return lax.ppermute(v, axis, [(0, 1), (1, 0)])]
    convert_element_type x22 -> x0, other arithmetic: 24.1 us -> none  [the longest x4 8.83 us: scatter(): stacked.astype(BF16)]
    slice x57 -> x4, local copies, waits for them, and re-layouts: 20.5 us -> 1.72 us  [the longest x1 1.04 us: shards(): ff_sum[:, n_ff:]]
    ppermute x8 -> x6, waiting for transfers between devices: 28.3 us -> 44.1 us  [the longest x4 37.5 us: hi_swap(): return lax.ppermute(v, 'hi', [(i, i ^ difference) for i in range(4)])]
  transfers between devices with their start and end apart: 61 -> 41, of which waited for: 26 -> 24; matrix products, arithmetic and copies ran while one was open for 42% -> 5% of each run, Pallas kernels for 0% -> 27%
where the time goes in v2:
time: 373 us; the launch traced here: 366 us
  waiting for transfers between devices  133 us (36%)
  Pallas kernels  117 us (31%)
  starting transfers between devices  39 us (10%)
  local copies, waits for them, and re-layouts  33.3 us (9%)
  between operations  15.7 us (4%)
  matrix products  14.7 us (4%)
  other arithmetic  12.5 us (3%)
    pallas_call x22, Pallas kernels, call(): pl.pallas_call(without(kernel, 1 + len(ins), len(deps)), grid_spec=pltpu....  115 us
    ppermute x32, waiting for transfers between devices, swap(): return lax.ppermute(v, axis, [(0, 1), (1, 0)])  78.6 us
    ppermute x4, waiting for transfers between devices, hi_swap(): return lax.ppermute(v, 'hi', [(i, i ^ difference) for i in range(4)])  37.5 us
    unnamed x147, local copies, waits for them, and re-layouts  29.6 us
    ppermute x32, starting transfers between devices, swap(): return lax.ppermute(v, axis, [(0, 1), (1, 0)])  22.4 us
    ppermute x4, starting transfers between devices, hi_swap(): return lax.ppermute(v, 'hi', [(i, i ^ difference) for i in range(4)])  10.6 us
    all_gather x1, waiting for transfers between devices, gather(): return lax.all_gather(part, CHIPS, axis=0, tiled=True)  10.6 us
    dot_general x1, matrix products, shards(): jnp.einsum('ta,tb->ab', grad_branch, hidden, preferred_element_type=F32)  8.15 us
  transfers between devices with their start and end apart: 41, of which 24 were waited for; matrix products, arithmetic and copies ran while one was open for 5% of the time, Pallas kernels for 27%

profile of v2, /device:TPU:0, one launch (start us, length us, event | category | flops | bytes accessed | tf_op | source)
XLA Modules:
  0.0 365.6 jit_solution(2588527474499844590)
XLA Ops:
  7.2 2.1 pack.1
  9.9 1.4 collective-permute-done.13
  11.3 2.0 maximum_select_fusion
  16.0 4.0 %collective-permute-start.2 = (bf16[64,1664]{1,0:T(8,128)(2,1)S(1)}, bf16[64,1664]{1,0:T(8,128)(2,1)S(1)}, u32[]{:S(2)}, u32[]{:S(2)}) collective-permute-start(bf16[64,1664]{1,0:T(8,128)(2,1)S(1)} %maximum_select_fusion.2), channel_id=1, source_target_pairs={{0,8},{4,12},{8,0},{12,4},{1,9},{5,13},{9,1},{13,5},{2,10},{6,14},... | collective-permute-start | bytes 638984 | tf_op jit(solution)/shard_map/ppermute | solution.py:728
  20.1 14.1 %collective-permute-done.2 = bf16[64,1664]{1,0:T(8,128)(2,1)S(1)} collective-permute-done((bf16[64,1664]{1,0:T(8,128)(2,1)S(1)}, bf16[64,1664]{1,0:T(8,128)(2,1)S(1)}, u32[]{:S(2)}, u32[]{:S(2)}) %collective-permute-start.2) | collective-permute-done | bytes 213024 | tf_op jit(solution)/shard_map/ppermute | solution.py:728
  34.2 4.7 %collective-permute-start.3 = (bf16[2,64,1664]{2,1,0:T(8,128)(2,1)S(1)}, bf16[2,64,1664]{2,1,0:T(8,128)(2,1)S(1)}, u32[]{:S(2)}, u32[]{:S(2)}) collective-permute-start(bf16[2,64,1664]{2,1,0:T(8,128)(2,1)S(1)} %pad_maximum_fusion.5), channel_id=1, source_target_pairs={{0,4},{4,0},{8,12},{12,8},{1,5},{5,1},{9,13},{13,9},{2,6},{6,2},{1... | collective-permute-start | bytes 1277960 | tf_op jit(solution)/shard_map/ppermute | solution.py:728
  38.9 11.9 %collective-permute-done.3 = bf16[2,64,1664]{2,1,0:T(8,128)(2,1)S(1)} collective-permute-done((bf16[2,64,1664]{2,1,0:T(8,128)(2,1)S(1)}, bf16[2,64,1664]{2,1,0:T(8,128)(2,1)S(1)}, u32[]{:S(2)}, u32[]{:S(2)}) %collective-permute-start.3) | collective-permute-done | bytes 426016 | tf_op jit(solution)/shard_map/ppermute | solution.py:728
  51.0 1.6 collective-permute-start.5
  52.6 1.5 collective-permute-start.4
  54.3 23.8 %collective-permute-done.5.refs_8_ = bf16[4,64,1664]{2,1,0:T(8,128)(2,1)S(1)} collective-permute-done((bf16[4,64,1664]{2,1,0:T(8,128)(2,1)S(1)}, bf16[4,64,1664]{2,1,0:T(8,128)(2,1)S(1)}, u32[]{:S(2)}, u32[]{:S(2)}) %collective-permute-start.5) | collective-permute-done | bytes 852000 | tf_op jit(solution)/shard_map/ppermute | solution.py:28
  78.1 1.5 collective-permute-start.7
  79.6 6.6 %collective-permute-done.4.refs_7_ = bf16[4,64,1664]{2,1,0:T(8,128)(2,1)S(1)} collective-permute-done((bf16[4,64,1664]{2,1,0:T(8,128)(2,1)S(1)}, bf16[4,64,1664]{2,1,0:T(8,128)(2,1)S(1)}, u32[]{:S(2)}, u32[]{:S(2)}) %collective-permute-start.4) | collective-permute-done | bytes 852000 | tf_op jit(solution)/shard_map/ppermute | solution.py:28
  86.3 1.6 collective-permute-start.6
  88.0 1.9 fusion.3
  90.8 4.2 %collective-permute-done.7.refs_10_ = bf16[2,64,1664]{2,1,0:T(8,128)(2,1)S(1)} collective-permute-done((bf16[2,64,1664]{2,1,0:T(8,128)(2,1)S(1)}, bf16[2,64,1664]{2,1,0:T(8,128)(2,1)S(1)}, u32[]{:S(2)}, u32[]{:S(2)}) %collective-permute-start.7) | collective-permute-done | bytes 426016 | tf_op jit(solution)/shard_map/ppermute | solution.py:28
  95.0 2.5 collective-permute-done.6.refs_9_
  97.4 11.9 %front.1 = (bf16[1024,1152]{1,0:T(8,128)(2,1)S(1)}, bf16[1024,512]{1,0:T(8,128)(2,1)S(1)}, bf16[1024,1024]{1,0:T(8,128)(2,1)S(1)}, bf16[1024,1024]{1,0:T(8,128)(...) custom-call(s32[4]{0:T(128)S(1)} %pad_add_fusion.refs_0_, ...), custom_call_target="tpu_custom_call" | custom-call | flops 7699999744 | bytes 6554112 | tf_op jit(solution)/shard_map/front/pallas_call | solution.py:695
  109.4 3.9 %collective-permute-start.8 = (bf16[4,128,128]{2,1,0:T(8,128)(2,1)S(1)}, bf16[4,128,128]{2,1,0:T(8,128)(2,1)S(1)}, u32[]{:S(2)}, u32[]{:S(2)}) collective-permute-start(bf16[4,128,128]{2,1,0:T(8,128)(2,1)S(1)} %get-tuple-element.78), channel_id=1, source_target_pairs={{0,2},{1,3},{4,6},{5,7},{8,10},{9,11},{12,14},{13,15},{16,18},{17,... | collective-permute-start | bytes 393224 | tf_op jit(solution)/shard_map/ppermute | solution.py:811
  113.4 5.2 %collective-permute-done.8.refs_4_.refs_6_ = bf16[4,128,128]{2,1,0:T(8,128)(2,1)S(1)} collective-permute-done((bf16[4,128,128]{2,1,0:T(8,128)(2,1)S(1)}, bf16[4,128,128]{2,1,0:T(8,128)(2,1)S(1)}, u32[]{:S(2)}, u32[]{:S(2)}) %collective-permute-start.8) | collective-permute-done | bytes 131104 | tf_op jit(solution)/shard_map/ppermute | solution.py:811
  118.7 10.3 %mix.1 = (f32[1024,512]{1,0:T(8,128)S(1)}, bf16[512,512]{1,0:T(8,128)(2,1)S(1)}, bf16[512,512]{1,0:T(8,128)(2,1)S(1)}, f32[4,128,128]{2,1,0:T(8,128)S(1)}) custom-call(s32[4]{0:T(128)S(1)} %pad_add_fusion.refs_0_, bf16[1024,1024]{1,0:T(8,128)(2,1)S(1)} %get-tuple-element.75.refs_1_.refs_4_, f32[1024,128]{1,0:T(8,128)S(1)} %get-tuple-element.76.refs_2_.refs_5_, ...), custom_call_target="tpu_custom_call" | custom-call | flops 6049999872 | bytes 3047424 | tf_op jit(solution)/shard_map/mix/pallas_call | solution.py:695
  129.1 1.3 copy-done.49
  130.9 1.4 collective-permute-done.9.refs_2_
  132.3 2.2 out.1
  134.6 1.3 copy-done.5
  138.7 10.6 %all-gather.2.cloned.1.call-done.refs_6_.refs_7_.refs_2_.refs_3_.refs_4_ = bf16[1024,4224]{1,0:T(8,128)(2,1)} async-done(((bf16[64,4224]{1,0:T(8,128)(2,1)}), bf16[1024,4224]{1,0:T(8,128)(2,1)}) %all-gather.2.cloned.1.call-update) | async-done | bytes 8650768 | tf_op jit(solution)/shard_map/all_gather | solution.py:42
  149.3 14.7 %ff.1 = (bf16[1024,1408]{1,0:T(8,128)(2,1)}, bf16[1024,2816]{1,0:T(8,128)(2,1)}, bf16[1024,1024]{1,0:T(8,128)(2,1)S(1)}, bf16[1024,1024]{1,0:T(8,128)(2,1)S(1)}) custom-call(s32[4]{0:T(128)S(1)} %pad_add_fusion.refs_0_, f32[1]{0:T(128)} %bitcast.4.refs_1_, bf16[512,1024]{1,0:T(8,128)(2,1)S(1)} %get-tuple-element.84.refs_2_, ...), custom_call_target="tpu_custom_call" | custom-call | flops 8249999872 | bytes 21495812 | tf_op jit(solution)/shard_map/ff/pallas_call | solution.py:695
  163.9 8.2 %convolution_convert_fusion.1.refs_4_ = bf16[1024,1408]{1,0:T(8,128)(2,1)} fusion(bf16[1024,1024]{1,0:T(8,128)(2,1)S(1)} %get-tuple-element.89.refs_1_, bf16[1024,1408]{1,0:T(8,128)(2,1)} %get-tuple-element.87.refs_1_), kind=kOutput, calls=%fused_computation.1 | convolution fusion | flops 2954231808 | bytes 7864320 | tf_op jit(solution)/shard_map/ta,tb->ab/dot_general | solution.py:851
  172.4 1.6 copy-done.3
  173.9 2.6 copy-done.7
  176.6 1.6 copy-done.12
  178.2 6.8 %ff_back.1.refs_1_.refs_2_ = bf16[1024,2816]{1,0:T(8,128)(2,1)S(1)} custom-call(s32[4]{0:T(128)S(1)} %pad_add_fusion.refs_0_, bf16[1024,1024]{1,0:T(8,128)(2,1)S(1)} %copy-done.12, bf16[1024,4224]{1,0:T(8,128)(2,1)} %all-gather.2.cloned.1.call-done.refs_6_.refs_7_.refs_2_.refs_3_.refs_4_, bf16[1024,2816]{1,0:T(8,128)(2,1)S(1)} %copy-done.7, ...), custom_call_target="tpu_custom_call" | custom-call | flops 4950000128 | bytes 16515072 | tf_op jit(solution)/shard_map/ff_back/pallas_call | solution.py:695
  185.0 6.5 %convolution_convert_fusion = bf16[1024,2816]{1,0:T(8,128)(2,1)S(1)} fusion(bf16[1024,1024]{1,0:T(8,128)(2,1)S(1)} %copy-done.46, bf16[1024,2816]{1,0:T(8,128)(2,1)S(1)} %ff_back.1.refs_1_.refs_2_), kind=kOutput, calls=%fused_computation | convolution fusion | flops 5908463616 | bytes 13631488 | tf_op jit(solution)/shard_map/ta,tb->ab/dot_general | solution.py:872
  192.7 2.4 copy-done
  195.2 4.0 %part.1.refs_11_ = bf16[512,1024]{1,0:T(8,128)(2,1)S(1)} custom-call(s32[4]{0:T(128)S(1)} %pad_add_fusion.refs_0_, bf16[1024,2816]{1,0:T(8,128)(2,1)S(1)} %ff_back.1.refs_1_.refs_2_, bf16[1024,4224]{1,0:T(8,128)(2,1)S(1)} %bitcast.43, bf16[1024,4224]{1,0:T(8,128)(2,1)S(1)} %bitcast.43, bf16[2,64,2816]{2,1,0:T(8,128)(2,1)} %get-tuple-element.138.refs_4_, ...), custom_call_target="tpu_custom_call" | custom-call | flops 4400000000 | bytes 23068672 | tf_op jit(solution)/shard_map/part/pallas_call | solution.py:695
  199.3 2.6 collective-permute-done.14.refs_5_
  202.0 2.7 copy-done.2
  205.9 9.4 %middle.1 = (f32[512,1024]{1,0:T(8,128)S(1)}, bf16[512,1024]{1,0:T(8,128)(2,1)S(1)}, f32[8,1024]{1,0:T(8,128)S(1)}, bf16[512,512]{1,0:T(8,128)(2,1)S(1)}, bf16[512,512]{1,0:T(8,128)(2,1)S(1)}) custom-call(s32[4]{0:T(128)S(1)} %pad_add_fusion.refs_0_, f32[1]{0:T(128)} %bitcast.4.refs_1_, bf16[1024,2816]{1,0:T(8,128)(2,1)S(1)} %copy-done.2, ...), custom_call_target="tpu_custom_call" | custom-call | flops 6600000000 | bytes 29392900 | tf_op jit(solution)/shard_map/middle/pallas_call | solution.py:695
  215.6 3.3 collective-permute-start.19
  218.8 1.4 collective-permute-start.18
  220.2 2.8 out_back.1
  223.1 6.9 %head_back.1 = (bf16[1024,512]{1,0:T(8,128)(2,1)S(1)}, f32[4,128,128]{2,1,0:T(8,128)S(1)}, bf16[4,128,128]{2,1,0:T(8,128)(2,1)S(1)}) custom-call(s32[4]{0:T(128)S(1)} %pad_add_fusion.refs_0_, bf16[512,512]{1,0:T(8,128)(2,1)S(1)} %get-tuple-element.92.refs_1_, bf16[512,512]{1,0:T(8,128)(2,1)S(1)} %collective-permute-done.15.refs_2_, ...), custom_call_target="tpu_custom_call" | custom-call | flops 4400000000 | bytes 5767168 | tf_op jit(solution)/shard_map/head_back/pallas_call | solution.py:695
  230.1 1.8 collective-permute-start.17
  231.9 2.4 out_sent.1.refs_6_
  234.3 1.6 collective-permute-done.19.refs_4_
  237.1 1.3 collective-permute-done.17.refs_5_.refs_8_
  239.4 1.4 collective-permute-start.21
  241.4 17.7 %back.1 = (bf16[1024,1152]{1,0:T(8,128)(2,1)S(1)}, f32[8,128]{1,0:T(8,128)S(1)}) custom-call(s32[4]{0:T(128)S(1)} %pad_add_fusion.refs_0_, bf16[1024,1024]{1,0:T(8,128)(2,1)S(1)} %copy-done.48, f32[1024,128]{1,0:T(8,128)S(1)} %copy-done.56, f32[2,8,512]{2,1,0:T(8,128)S(1)} %get-tuple-element.77.refs_3_, f32[1024,128]{1,0:T(8,128)S(1)} %copy-done.58, ...), custom_call_target="tpu_custom_call" | custom-call | flops 11000000512 | bytes 6062080 | tf_op jit(solution)/shard_map/back/pallas_call | solution.py:695
  259.1 3.4 output.1.refs_4_
  262.5 10.3 %collective-permute-done.21 = bf16[256,2816]{1,0:T(8,128)(2,1)S(1)} collective-permute-done((bf16[256,2816]{1,0:T(8,128)(2,1)S(1)}, bf16[256,2816]{1,0:T(8,128)(2,1)S(1)}, u32[]{:S(2)}, u32[]{:S(2)}) %collective-permute-start.21) | collective-permute-done | bytes 1441824 | tf_op jit(solution)/shard_map/ppermute | solution.py:28
  275.2 2.2 ff_own.1.refs_10_
  279.8 1.7 copy-done.52
  281.4 1.6 copy-done.54
  283.0 9.7 %front_back.1 = (f32[512,1024]{1,0:T(8,128)S(1)}, bf16[512,1024]{1,0:T(8,128)(2,1)S(1)}, bf16[4,64,1664]{2,1,0:T(8,128)(2,1)S(1)}, bf16[4,64,1664]{2,1,0:T(8,128...) custom-call(s32[4]{0:T(128)S(1)} %pad_add_fusion.refs_0_, ...), custom_call_target="tpu_custom_call" | custom-call | flops 6600000000 | bytes 11046912 | tf_op jit(solution)/shard_map/front_back/pallas_call | solution.py:695
  296.2 1.3 copy-done.39
  298.6 9.6 %collective-permute-done.26 = bf16[2,64,1664]{2,1,0:T(8,128)(2,1)S(1)} collective-permute-done((bf16[2,64,1664]{2,1,0:T(8,128)(2,1)}, bf16[2,64,1664]{2,1,0:T(8,128)(2,1)S(1)}, u32[]{:S(2)}, u32[]{:S(2)}) %collective-permute-start.26) | collective-permute-done | bytes 426016 | tf_op jit(solution)/shard_map/ppermute | solution.py:28
  313.6 1.5 collective-permute-start.28
  315.1 1.4 collective-permute-start.29
  316.6 1.6 copy-done.40
  318.2 3.8 %grad_input.1.refs_4_ = bf16[512,1024]{1,0:T(8,128)(2,1)} custom-call(s32[4]{0:T(128)S(1)} %pad_add_fusion.refs_0_, f32[512,1024]{1,0:T(8,128)S(1)} %copy-done.40, bf16[512,1024]{1,0:T(8,128)(2,1)} %collective-permute-done.23.refs_2_, f32[512,1024]{1,0:T(8,128)S(1)} %copy-done.25, bf16[512,1024]{1,0:T(8,128)(2,1)S(1)} %copy-done.28, ...), custom_call_target="tpu_custom_call" | custom-call | flops 2475000064 | bytes 6324224 | tf_op jit(solution)/shard_map/grad_input/pallas_call | solution.py:695
  322.0 10.0 %collective-permute-done.28.refs_3_ = bf16[32,1408]{1,0:T(8,128)(2,1)S(1)} collective-permute-done((bf16[32,1408]{1,0:T(8,128)(2,1)S(1)}, bf16[32,1408]{1,0:T(8,128)(2,1)S(1)}, u32[]{:S(2)}, u32[]{:S(2)}) %collective-permute-start.28) | collective-permute-done | bytes 90144 | tf_op jit(solution)/shard_map/ppermute | solution.py:28
  334.3 2.2 first_sum.1
  341.1 3.6 collective-permute-done.30
  344.8 1.5 collective-permute-start.31
  346.4 7.9 %collective-permute-done.31.refs_2_ = bf16[64,1664]{1,0:T(8,128)(2,1)S(1)} collective-permute-done((bf16[64,1664]{1,0:T(8,128)(2,1)S(1)}, bf16[64,1664]{1,0:T(8,128)(2,1)S(1)}, u32[]{:S(2)}, u32[]{:S(2)}) %collective-permute-start.31) | collective-permute-done | bytes 213024 | tf_op jit(solution)/shard_map/ppermute | solution.py:728
  (233 shorter events, 39.3 us)
Async XLA Ops:
  7.2 142.1 %all-gather.2.cloned.1.call-start = ((), (), s32[]{:S(2)}) async-start(), calls=%async_computation.2 | async-start | bytes 9191424 | tf_op jit(solution)/shard_map/all_gather | solution.py:42
  9.4 10.6 %copy-start.61 = (bf16[32,1664]{1,0:T(8,128)(2,1)S(1)}, bf16[32,1664]{1,0:T(8,128)(2,1)}, u32[]{:S(2)}) copy-start(bf16[32,1664]{1,0:T(8,128)(2,1)} %get-tuple-element.73) | copy-start | bytes 319492
  9.4 1.9 collective-permute-start.13
  13.3 40.8 %copy-start.63 = (f32[16]{0:T(128)S(1)}, f32[16]{0:T(128)}, u32[]{:S(2)}) copy-start(f32[16]{0:T(128)} %param.24) | copy-start | bytes 196
  13.3 298.5 %reduce-scatter.3.cloned.1.call-start = ((), (), s32[]{:S(2)}) async-start(), calls=%async_computation.3 | async-start | bytes 3604480 | tf_op jit(solution)/shard_map/reduce_scatter | solution.py:857
  13.4 1.6 collective-permute-start.1
  16.0 18.2 %collective-permute-start.2 = (bf16[64,1664]{1,0:T(8,128)(2,1)S(1)}, bf16[64,1664]{1,0:T(8,128)(2,1)S(1)}, u32[]{:S(2)}, u32[]{:S(2)}) collective-permute-start(bf16[64,1664]{1,0:T(8,128)(2,1)S(1)} %maximum_select_fusion.2), channel_id=1, source_target_pairs={{0,8},{4,12},{8,0},{12,4},{1,9},{5,13},{9,1},{13,5},{2,10},{6,14},... | collective-permute-start | bytes 638984 | tf_op jit(solution)/shard_map/ppermute | solution.py:728
  34.2 16.6 %collective-permute-start.3 = (bf16[2,64,1664]{2,1,0:T(8,128)(2,1)S(1)}, bf16[2,64,1664]{2,1,0:T(8,128)(2,1)S(1)}, u32[]{:S(2)}, u32[]{:S(2)}) collective-permute-start(bf16[2,64,1664]{2,1,0:T(8,128)(2,1)S(1)} %pad_maximum_fusion.5), channel_id=1, source_target_pairs={{0,4},{4,0},{8,12},{12,8},{1,5},{5,1},{9,13},{13,9},{2,6},{6,2},{1... | collective-permute-start | bytes 1277960 | tf_op jit(solution)/shard_map/ppermute | solution.py:728
  51.0 27.1 %collective-permute-start.5 = (bf16[4,64,1664]{2,1,0:T(8,128)(2,1)S(1)}, bf16[4,64,1664]{2,1,0:T(8,128)(2,1)S(1)}, u32[]{:S(2)}, u32[]{:S(2)}) collective-permute-start(bf16[4,64,1664]{2,1,0:T(8,128)(2,1)S(1)} %pad_maximum_fusion.refs_6_), channel_id=1, source_target_pairs={{0,2},{2,0},{1,3},{3,1},{4,6},{6,4},{5,7},{7,5},{8,10},{10,8},{9,1... | collective-permute-start | bytes 2555912 | tf_op jit(solution)/shard_map/ppermute | solution.py:28
  52.6 33.6 %collective-permute-start.4 = (bf16[4,64,1664]{2,1,0:T(8,128)(2,1)S(1)}, bf16[4,64,1664]{2,1,0:T(8,128)(2,1)S(1)}, u32[]{:S(2)}, u32[]{:S(2)}) collective-permute-start(bf16[4,64,1664]{2,1,0:T(8,128)(2,1)S(1)} %pad_maximum_fusion.refs_6_), channel_id=1, source_target_pairs={{0,16},{16,0},{1,17},{17,1},{2,18},{18,2},{3,19},{19,3},{4,20},{20... | collective-permute-start | bytes 2555912 | tf_op jit(solution)/shard_map/ppermute | solution.py:28
  54.1 36.7 %collective-permute-start = (bf16[512,1024]{1,0:T(8,128)(2,1)}, bf16[512,1024]{1,0:T(8,128)(2,1)}, u32[]{:S(2)}, u32[]{:S(2)}) collective-permute-start(bf16[512,1024]{1,0:T(8,128)(2,1)} %refs_4_.5), channel_id=1, source_target_pairs={{0,1},{1,0},{2,3},{3,2},{4,5},{5,4},{6,7},{7,6},{8,9},{9,8},{10,11... | collective-permute-start | bytes 3145736 | tf_op jit(solution)/shard_map/ppermute | solution.py:28
  78.1 16.8 %collective-permute-start.7 = (bf16[2,64,1664]{2,1,0:T(8,128)(2,1)S(1)}, bf16[2,64,1664]{2,1,0:T(8,128)(2,1)S(1)}, u32[]{:S(2)}, u32[]{:S(2)}) collective-permute-start(bf16[2,64,1664]{2,1,0:T(8,128)(2,1)S(1)} %slice.54), channel_id=1, source_target_pairs={{0,16},{16,0},{1,17},{17,1},{2,18},{18,2},{3,19},{19,3},{4,20},{20... | collective-permute-start | bytes 1277960 | tf_op jit(solution)/shard_map/ppermute | solution.py:28
  86.3 11.2 %collective-permute-start.6 = (bf16[2,64,1664]{2,1,0:T(8,128)(2,1)S(1)}, bf16[2,64,1664]{2,1,0:T(8,128)(2,1)S(1)}, u32[]{:S(2)}, u32[]{:S(2)}) collective-permute-start(bf16[2,64,1664]{2,1,0:T(8,128)(2,1)S(1)} %slice.53), channel_id=1, source_target_pairs={{0,2},{2,0},{1,3},{3,1},{4,6},{6,4},{5,7},{7,5},{8,10},{10,8},{9,1... | collective-permute-start | bytes 1277960 | tf_op jit(solution)/shard_map/ppermute | solution.py:28
  88.0 9.5 %copy-start.26 = (bf16[512,1024]{1,0:T(8,128)(2,1)S(1)}, bf16[512,1024]{1,0:T(8,128)(2,1)}, u32[]{:S(2)}) copy-start(bf16[512,1024]{1,0:T(8,128)(2,1)} %refs_4_.5) | copy-start | bytes 3145732
  90.8 18.6 %copy-start.20 = (f32[1024,128]{1,0:T(8,128)}, f32[1024,128]{1,0:T(8,128)S(1)}, u32[]{:S(2)}) copy-start(f32[1024,128]{1,0:T(8,128)S(1)} %get-tuple-element.156.refs_4_.refs_10_) | copy-start | bytes 1572868
  90.8 18.6 %copy-start.22 = (f32[1024,128]{1,0:T(8,128)}, f32[1024,128]{1,0:T(8,128)S(1)}, u32[]{:S(2)}) copy-start(f32[1024,128]{1,0:T(8,128)S(1)} %get-tuple-element.157.refs_5_.refs_11_) | copy-start | bytes 1572868
  109.4 19.6 %copy-start.47 = (bf16[1024,1024]{1,0:T(8,128)(2,1)}, bf16[1024,1024]{1,0:T(8,128)(2,1)S(1)}, u32[]{:S(2)}) copy-start(bf16[1024,1024]{1,0:T(8,128)(2,1)S(1)} %get-tuple-element.75.refs_1_.refs_4_) | copy-start | bytes 6291460
  109.4 19.6 %copy-start.51 = (bf16[1024,1152]{1,0:T(8,128)(2,1)}, bf16[1024,1152]{1,0:T(8,128)(2,1)S(1)}, u32[]{:S(2)}) copy-start(bf16[1024,1152]{1,0:T(8,128)(2,1)S(1)} %get-tuple-element.106.refs_3_) | copy-start | bytes 7077892
  109.4 19.6 %copy-start.53 = (bf16[1024,1024]{1,0:T(8,128)(2,1)}, bf16[1024,1024]{1,0:T(8,128)(2,1)S(1)}, u32[]{:S(2)}) copy-start(bf16[1024,1024]{1,0:T(8,128)(2,1)S(1)} %get-tuple-element.105.refs_1_) | copy-start | bytes 6291460
  109.4 19.6 %copy-start.55 = (f32[1024,128]{1,0:T(8,128)}, f32[1024,128]{1,0:T(8,128)S(1)}, u32[]{:S(2)}) copy-start(f32[1024,128]{1,0:T(8,128)S(1)} %get-tuple-element.76.refs_2_.refs_5_) | copy-start | bytes 1572868
  109.4 19.6 %copy-start.57 = (f32[1024,128]{1,0:T(8,128)}, f32[1024,128]{1,0:T(8,128)S(1)}, u32[]{:S(2)}) copy-start(f32[1024,128]{1,0:T(8,128)S(1)} %get-tuple-element.98.refs_4_) | copy-start | bytes 1572868
  109.4 22.9 %copy-start.15 = (bf16[1024,512]{1,0:T(8,128)(2,1)}, bf16[1024,512]{1,0:T(8,128)(2,1)S(1)}, u32[]{:S(2)}) copy-start(bf16[1024,512]{1,0:T(8,128)(2,1)S(1)} %get-tuple-element.82.refs_3_.refs_9_) | copy-start | bytes 3145732
  109.4 9.2 %collective-permute-start.8 = (bf16[4,128,128]{2,1,0:T(8,128)(2,1)S(1)}, bf16[4,128,128]{2,1,0:T(8,128)(2,1)S(1)}, u32[]{:S(2)}, u32[]{:S(2)}) collective-permute-start(bf16[4,128,128]{2,1,0:T(8,128)(2,1)S(1)} %get-tuple-element.78), channel_id=1, source_target_pairs={{0,2},{1,3},{4,6},{5,7},{8,10},{9,11},{12,14},{13,15},{16,18},{17,... | collective-permute-start | bytes 393224 | tf_op jit(solution)/shard_map/ppermute | solution.py:811
  113.3 18.9 %collective-permute-start.10 = (bf16[1024,512]{1,0:T(8,128)(2,1)S(1)}, bf16[1024,512]{1,0:T(8,128)(2,1)S(1)}, u32[]{:S(2)}, u32[]{:S(2)}) collective-permute-start(bf16[1024,512]{1,0:T(8,128)(2,1)S(1)} %get-tuple-element.82.refs_3_.refs_9_), channel_id=1, source_target_pairs={{0,1},{1,0},{2,3},{3,2},{4,5},{5,4},{6,7},{7,6},{8,9},{9,8},{10,11... | collective-permute-start | bytes 3145736 | tf_op jit(solution)/shard_map/ppermute | solution.py:28
  118.7 11.7 %copy-start.13 = (bf16[512,1024]{1,0:T(8,128)(2,1)S(1)}, bf16[512,1024]{1,0:T(8,128)(2,1)}, u32[]{:S(2)}) copy-start(bf16[512,1024]{1,0:T(8,128)(2,1)} %refs_6_.1) | copy-start | bytes 3145732
  130.4 1.9 collective-permute-start.9
  130.4 7.9 %collective-permute-start.12 = (bf16[512,1024]{1,0:T(8,128)(2,1)S(1)}, bf16[512,1024]{1,0:T(8,128)(2,1)S(1)}, u32[]{:S(2)}, u32[]{:S(2)}) collective-permute-start(bf16[512,1024]{1,0:T(8,128)(2,1)S(1)} %copy-done.13), channel_id=1, source_target_pairs={{0,1},{1,0},{2,3},{3,2},{4,5},{5,4},{6,7},{7,6},{8,9},{9,8},{10,11... | collective-permute-start | bytes 3145736 | tf_op jit(solution)/shard_map/ppermute | solution.py:28
  135.9 2.8 collective-permute-start.11
  172.1 164.7 %reduce-scatter.5.cloned.1.call-start = ((), (), s32[]{:S(2)}) async-start(), calls=%async_computation.4 | async-start | bytes 1802240 | tf_op jit(solution)/shard_map/reduce_scatter | solution.py:982
  185.0 10.2 %copy-start.1 = (bf16[1024,2816]{1,0:T(8,128)(2,1)}, bf16[1024,2816]{1,0:T(8,128)(2,1)S(1)}, u32[]{:S(2)}) copy-start(bf16[1024,2816]{1,0:T(8,128)(2,1)S(1)} %ff_back.1.refs_1_.refs_2_) | copy-start | bytes 17301508
  185.0 10.2 %slice-start = ((s8[8650752]{0:T(1024)(128)(4,1)}), s8[4194304]{0:T(1024)(128)(4,1)S(1)}, s32[]{:S(2)}) async-start(s8[8650752]{0:T(1024)(128)(4,1)} %bitcast.42), calls=%async_computation.5 | async-start | bytes 8388608
  185.0 10.2 %slice-start.1 = ((s8[8650752]{0:T(1024)(128)(4,1)}), s8[4194304]{0:T(1024)(128)(4,1)S(1)}, s32[]{:S(2)}) async-start(s8[8650752]{0:T(1024)(128)(4,1)} %bitcast.42), calls=%async_computation.6 | async-start | bytes 8388608
  185.0 10.2 %slice-start.2 = ((s8[8650752]{0:T(1024)(128)(4,1)}), s8[262144]{0:T(1024)(128)(4,1)S(1)}, s32[]{:S(2)}) async-start(s8[8650752]{0:T(1024)(128)(4,1)} %bitcast.42), calls=%async_computation.7 | async-start | bytes 524288
  199.2 2.7 collective-permute-start.14
  205.9 14.3 %copy-start.34 = (bf16[512,512]{1,0:T(8,128)(2,1)S(1)}, bf16[512,512]{1,0:T(8,128)(2,1)}, u32[]{:S(2)}) copy-start(bf16[512,512]{1,0:T(8,128)(2,1)} %copy-done.33) | copy-start | bytes 1572868
  205.9 14.3 %copy-start.44 = (bf16[512,512]{1,0:T(8,128)(2,1)S(1)}, bf16[512,512]{1,0:T(8,128)(2,1)}, u32[]{:S(2)}) copy-start(bf16[512,512]{1,0:T(8,128)(2,1)} %copy-done.43) | copy-start | bytes 1572868
  205.9 17.1 %copy-start.50 = (f32[1024,512]{1,0:T(8,128)S(1)}, f32[1024,512]{1,0:T(8,128)}, u32[]{:S(2)}) copy-start(f32[1024,512]{1,0:T(8,128)} %copy-done.49) | copy-start | bytes 6291460
  215.4 7.7 %collective-permute-start.15 = (bf16[512,512]{1,0:T(8,128)(2,1)S(1)}, bf16[512,512]{1,0:T(8,128)(2,1)S(1)}, u32[]{:S(2)}, u32[]{:S(2)}) collective-permute-start(bf16[512,512]{1,0:T(8,128)(2,1)S(1)} %get-tuple-element.93), channel_id=1, source_target_pairs={{0,1},{1,0},{2,3},{3,2},{4,5},{5,4},{6,7},{7,6},{8,9},{9,8},{10,11... | collective-permute-start | bytes 1572872 | tf_op jit(solution)/shard_map/ppermute | solution.py:28
  215.6 20.4 %collective-permute-start.19 = (bf16[2,64,2816]{2,1,0:T(8,128)(2,1)}, bf16[2,64,2816]{2,1,0:T(8,128)(2,1)S(1)}, u32[]{:S(2)}, u32[]{:S(2)}) collective-permute-start(bf16[2,64,2816]{2,1,0:T(8,128)(2,1)} %get-tuple-element.137.refs_5_), channel_id=1, source_target_pairs={{0,2},{2,0},{1,3},{3,1},{4,6},{6,4},{5,7},{7,5},{8,10},{10,8},{9,1... | collective-permute-start | bytes 2162696 | tf_op jit(solution)/shard_map/ppermute | solution.py:28
  218.8 18.3 %collective-permute-start.18 = (bf16[2,64,2816]{2,1,0:T(8,128)(2,1)}, bf16[2,64,2816]{2,1,0:T(8,128)(2,1)S(1)}, u32[]{:S(2)}, u32[]{:S(2)}) collective-permute-start(bf16[2,64,2816]{2,1,0:T(8,128)(2,1)} %get-tuple-element.138.refs_4_), channel_id=1, source_target_pairs={{0,16},{16,0},{1,17},{17,1},{2,18},{18,2},{3,19},{19,3},{4,20},{20... | collective-permute-start | bytes 2162696 | tf_op jit(solution)/shard_map/ppermute | solution.py:28
  223.0 8.8 %slice-start.3 = ((s8[8650752]{0:T(1024)(128)(4,1)}), s8[4194304]{0:T(1024)(128)(4,1)S(1)}, s32[]{:S(2)}) async-start(s8[8650752]{0:T(1024)(128)(4,1)} %bitcast.44), calls=%async_computation.8 | async-start | bytes 8388608
  230.1 8.4 %collective-permute-start.17 = (bf16[4,128,128]{2,1,0:T(8,128)(2,1)S(1)}, bf16[4,128,128]{2,1,0:T(8,128)(2,1)S(1)}, u32[]{:S(2)}, u32[]{:S(2)}) collective-permute-start(bf16[4,128,128]{2,1,0:T(8,128)(2,1)S(1)} %get-tuple-element.97.refs_3_), channel_id=1, source_target_pairs={{2,0},{3,1},{6,4},{7,5},{10,8},{11,9},{14,12},{15,13},{18,16},{19,... | collective-permute-start | bytes 393224 | tf_op jit(solution)/shard_map/ppermute | solution.py:926
  239.4 33.4 %collective-permute-start.21 = (bf16[256,2816]{1,0:T(8,128)(2,1)S(1)}, bf16[256,2816]{1,0:T(8,128)(2,1)S(1)}, u32[]{:S(2)}, u32[]{:S(2)}) collective-permute-start(bf16[256,2816]{1,0:T(8,128)(2,1)S(1)} %get-tuple-element.102.refs_12_), channel_id=1, source_target_pairs={{0,16},{16,0},{1,17},{17,1},{2,18},{18,2},{3,19},{19,3},{4,20},{20... | collective-permute-start | bytes 4325384 | tf_op jit(solution)/shard_map/ppermute | solution.py:28
  240.9 33.1 %collective-permute-start.22 = (bf16[256,2816]{1,0:T(8,128)(2,1)S(1)}, bf16[256,2816]{1,0:T(8,128)(2,1)S(1)}, u32[]{:S(2)}, u32[]{:S(2)}) collective-permute-start(bf16[256,2816]{1,0:T(8,128)(2,1)S(1)} %get-tuple-element.103.refs_13_), channel_id=1, source_target_pairs={{0,2},{2,0},{1,3},{3,1},{4,6},{6,4},{5,7},{7,5},{8,10},{10,8},{9,1... | collective-permute-start | bytes 4325384 | tf_op jit(solution)/shard_map/ppermute | solution.py:28
  240.9 18.3 %collective-permute-start.16 = (bf16[512,1024]{1,0:T(8,128)(2,1)S(1)}, bf16[512,1024]{1,0:T(8,128)(2,1)S(1)}, u32[]{:S(2)}, u32[]{:S(2)}) collective-permute-start(bf16[512,1024]{1,0:T(8,128)(2,1)S(1)} %out_sent.1.refs_6_), channel_id=1, source_target_pairs={{0,1},{1,0},{2,3},{3,2},{4,5},{5,4},{6,7},{7,6},{8,9},{9,8},{10,11... | collective-permute-start | bytes 3145736 | tf_op jit(solution)/shard_map/ppermute | solution.py:28
  240.9 36.4 %collective-permute-start.20 = (bf16[1024,512]{1,0:T(8,128)(2,1)}, bf16[1024,512]{1,0:T(8,128)(2,1)}, u32[]{:S(2)}, u32[]{:S(2)}) collective-permute-start(bf16[1024,512]{1,0:T(8,128)(2,1)} %get-tuple-element.96.refs_6_), channel_id=1, source_target_pairs={{0,1},{1,0},{2,3},{3,2},{4,5},{5,4},{6,7},{7,6},{8,9},{9,8},{10,11... | collective-permute-start | bytes 3145736 | tf_op jit(solution)/shard_map/ppermute | solution.py:28
  297.5 10.6 %collective-permute-start.26 = (bf16[2,64,1664]{2,1,0:T(8,128)(2,1)}, bf16[2,64,1664]{2,1,0:T(8,128)(2,1)S(1)}, u32[]{:S(2)}, u32[]{:S(2)}) collective-permute-start(bf16[2,64,1664]{2,1,0:T(8,128)(2,1)} %get-tuple-element.117.refs_2_), channel_id=1, source_target_pairs={{0,16},{16,0},{1,17},{17,1},{2,18},{18,2},{3,19},{19,3},{4,20},{20... | collective-permute-start | bytes 1277960 | tf_op jit(solution)/shard_map/ppermute | solution.py:28
  298.2 12.8 %collective-permute-start.24 = (bf16[2,64,1664]{2,1,0:T(8,128)(2,1)}, bf16[2,64,1664]{2,1,0:T(8,128)(2,1)S(1)}, u32[]{:S(2)}, u32[]{:S(2)}) collective-permute-start(bf16[2,64,1664]{2,1,0:T(8,128)(2,1)} %copy-done.35), channel_id=1, source_target_pairs={{0,2},{2,0},{1,3},{3,1},{4,6},{6,4},{5,7},{7,5},{8,10},{10,8},{9,1... | collective-permute-start | bytes 1277960 | tf_op jit(solution)/shard_map/ppermute | solution.py:28
  298.6 18.0 %collective-permute-start.23 = (bf16[512,1024]{1,0:T(8,128)(2,1)}, bf16[512,1024]{1,0:T(8,128)(2,1)}, u32[]{:S(2)}, u32[]{:S(2)}) collective-permute-start(bf16[512,1024]{1,0:T(8,128)(2,1)} %copy-done.29), channel_id=1, source_target_pairs={{0,1},{1,0},{2,3},{3,2},{4,5},{5,4},{6,7},{7,6},{8,9},{9,8},{10,11... | collective-permute-start | bytes 3145736 | tf_op jit(solution)/shard_map/ppermute | solution.py:28
  310.4 23.8 %collective-permute-start.27 = (bf16[4,64,1664]{2,1,0:T(8,128)(2,1)}, bf16[4,64,1664]{2,1,0:T(8,128)(2,1)}, u32[]{:S(2)}, u32[]{:S(2)}) collective-permute-start(bf16[4,64,1664]{2,1,0:T(8,128)(2,1)} %pad_maximum_fusion.2), channel_id=1, source_target_pairs={{0,2},{2,0},{1,3},{3,1},{4,6},{6,4},{5,7},{7,5},{8,10},{10,8},{9,1... | collective-permute-start | bytes 2555912 | tf_op jit(solution)/shard_map/ppermute | solution.py:28
  311.2 23.0 %collective-permute-start.25 = (bf16[4,64,1664]{2,1,0:T(8,128)(2,1)S(1)}, bf16[4,64,1664]{2,1,0:T(8,128)(2,1)}, u32[]{:S(2)}, u32[]{:S(2)}) collective-permute-start(bf16[4,64,1664]{2,1,0:T(8,128)(2,1)S(1)} %pad_maximum_fusion.1.refs_6_.refs_5_), channel_id=1, source_target_pairs={{0,16},{16,0},{1,17},{17,1},{2,18},{18,2},{3,19},{19,3},{4,20},{20... | collective-permute-start | bytes 2555912 | tf_op jit(solution)/shard_map/ppermute | solution.py:28
  313.6 18.3 %collective-permute-start.28 = (bf16[32,1408]{1,0:T(8,128)(2,1)S(1)}, bf16[32,1408]{1,0:T(8,128)(2,1)S(1)}, u32[]{:S(2)}, u32[]{:S(2)}) collective-permute-start(bf16[32,1408]{1,0:T(8,128)(2,1)S(1)} %get-tuple-element.118), channel_id=1, source_target_pairs={{0,16},{16,0},{1,17},{17,1},{2,18},{18,2},{3,19},{19,3},{4,20},{20... | collective-permute-start | bytes 270344 | tf_op jit(solution)/shard_map/ppermute | solution.py:28
  315.1 16.8 %collective-permute-start.29 = (bf16[32,1408]{1,0:T(8,128)(2,1)S(1)}, bf16[32,1408]{1,0:T(8,128)(2,1)S(1)}, u32[]{:S(2)}, u32[]{:S(2)}) collective-permute-start(bf16[32,1408]{1,0:T(8,128)(2,1)S(1)} %get-tuple-element.119), channel_id=1, source_target_pairs={{0,2},{2,0},{1,3},{3,1},{4,6},{6,4},{5,7},{7,5},{8,10},{10,8},{9,1... | collective-permute-start | bytes 270344 | tf_op jit(solution)/shard_map/ppermute | solution.py:28
  318.2 13.8 %copy-start.31 = (bf16[1,256,1408]{2,1,0:T(8,128)(2,1)S(1)}, bf16[1,256,1408]{2,1,0:T(8,128)(2,1)}, u32[]{:S(2)}) copy-start(bf16[1,256,1408]{2,1,0:T(8,128)(2,1)} %reduce-scatter.3.cloned.1.call-done) | copy-start | bytes 2162692
  321.9 12.3 %copy-start.36 = (bf16[512,1024]{1,0:T(8,128)(2,1)S(1)}, bf16[512,1024]{1,0:T(8,128)(2,1)}, u32[]{:S(2)}) copy-start(bf16[512,1024]{1,0:T(8,128)(2,1)} %grad_input.1.refs_4_) | copy-start | bytes 3145732
  321.9 12.3 %copy-start.38 = (bf16[4,64,1664]{2,1,0:T(8,128)(2,1)S(1)}, bf16[4,64,1664]{2,1,0:T(8,128)(2,1)}, u32[]{:S(2)}) copy-start(bf16[4,64,1664]{2,1,0:T(8,128)(2,1)} %copy-done.37) | copy-start | bytes 2555908
  332.5 6.1 %collective-permute-start.34 = (bf16[64,1408]{1,0:T(8,128)(2,1)S(1)}, bf16[64,1408]{1,0:T(8,128)(2,1)S(1)}, u32[]{:S(2)}, u32[]{:S(2)}) collective-permute-start(bf16[64,1408]{1,0:T(8,128)(2,1)S(1)} %get-tuple-element.120.refs_5_), channel_id=1, source_target_pairs={{0,16},{16,0},{1,17},{17,1},{2,18},{18,2},{3,19},{19,3},{4,20},{20... | collective-permute-start | bytes 540680 | tf_op jit(solution)/shard_map/ppermute | solution.py:28
  333.1 5.5 %collective-permute-start.35 = (bf16[64,1408]{1,0:T(8,128)(2,1)S(1)}, bf16[64,1408]{1,0:T(8,128)(2,1)S(1)}, u32[]{:S(2)}, u32[]{:S(2)}) collective-permute-start(bf16[64,1408]{1,0:T(8,128)(2,1)S(1)} %get-tuple-element.121.refs_6_), channel_id=1, source_target_pairs={{0,2},{2,0},{1,3},{3,1},{4,6},{6,4},{5,7},{7,5},{8,10},{10,8},{9,1... | collective-permute-start | bytes 540680 | tf_op jit(solution)/shard_map/ppermute | solution.py:28
  336.5 8.2 %collective-permute-start.30 = (bf16[2,64,1664]{2,1,0:T(8,128)(2,1)S(1)}, bf16[2,64,1664]{2,1,0:T(8,128)(2,1)S(1)}, u32[]{:S(2)}, u32[]{:S(2)}) collective-permute-start(bf16[2,64,1664]{2,1,0:T(8,128)(2,1)S(1)} %get-tuple-element.123), channel_id=1, source_target_pairs={{0,4},{4,0},{8,12},{12,8},{1,5},{5,1},{9,13},{13,9},{2,6},{6,2},{1... | collective-permute-start | bytes 1277960 | tf_op jit(solution)/shard_map/ppermute | solution.py:728
  337.9 2.4 collective-permute-start.33
  338.0 1.5 collective-permute-start.32
  339.2 7.1 %collective-permute-start.36 = (bf16[32,1408]{1,0:T(8,128)(2,1)S(1)}, bf16[32,1408]{1,0:T(8,128)(2,1)S(1)}, u32[]{:S(2)}, u32[]{:S(2)}) collective-permute-start(bf16[32,1408]{1,0:T(8,128)(2,1)S(1)} %get-tuple-element.146), channel_id=1, source_target_pairs={{0,1},{1,0},{2,3},{3,2},{4,5},{5,4},{6,7},{7,6},{8,9},{9,8},{10,11... | collective-permute-start | bytes 270344 | tf_op jit(solution)/shard_map/ppermute | solution.py:28
  344.8 9.4 %collective-permute-start.31 = (bf16[64,1664]{1,0:T(8,128)(2,1)S(1)}, bf16[64,1664]{1,0:T(8,128)(2,1)S(1)}, u32[]{:S(2)}, u32[]{:S(2)}) collective-permute-start(bf16[64,1664]{1,0:T(8,128)(2,1)S(1)} %fusion), channel_id=1, source_target_pairs={{0,8},{4,12},{8,0},{12,4},{1,9},{5,13},{9,1},{13,5},{2,10},{6,14},... | collective-permute-start | bytes 638984 | tf_op jit(solution)/shard_map/ppermute | solution.py:728
  354.8 1.4 collective-permute-start.37
  (50 other events, 215.3 us)
Sparse Core Ops, SparseCore 0:
  13.4 135.7 all-gather.1
  172.3 57.1 reduce-scatter.2
  298.3 31.5 reduce-scatter.4
